TPU v7x, 32 devices: a whole 2x2x4 slice. The times are simulated.
32 devices in a mesh: fsdp: 8 (over y, x, core), dp: 4 (over z).
Axes of the slice: x: 2, y: 2, z: 4, core: 2. Of those that a mesh axis runs over, the one named last changes fastest.
Arguments:
- tokens: bfloat16 [8192, 2048], P(('fsdp', 'dp')), may hold values from -6 to 6
- cotangent: bfloat16 [8192, 2048], P(('fsdp', 'dp')), may hold values from -6 to 6
- order: int32 [32, 256], P(('fsdp', 'dp')), may hold values from 0 to 255, each once within a row
- lengths: int32 [64, 3], P(('fsdp', 'dp')), may hold values from 1 to 96, 128 in all within a row
- w_qkv: float32 [2048, 3072], P(('fsdp', 'dp')), may hold values from -0.125 to 0.125
- w_out: float32 [2048, 2048], P(('fsdp', 'dp')), may hold values from -0.375 to 0.375
- w_gate_up: float32 [2048, 16384], P(('fsdp', 'dp')), may hold values from -0.125 to 0.125
- w_down: float32 [8192, 2048], P(('fsdp', 'dp')), may hold values from -0.0625 to 0.0625
- gains: float32 [4224], replicated, may hold values from 0.5 to 7
- first_qkv: float32 [2048, 3072], P(('fsdp', 'dp')), may hold values from -9.1552734e-05 to 9.1552734e-05
- first_out: float32 [2048, 2048], P(('fsdp', 'dp')), may hold values from -9.1552734e-05 to 9.1552734e-05
- first_gate_up: float32 [2048, 16384], P(('fsdp', 'dp')), may hold values from -9.1552734e-05 to 9.1552734e-05
- first_down: float32 [8192, 2048], P(('fsdp', 'dp')), may hold values from -9.1552734e-05 to 9.1552734e-05
- first_gains: float32 [4224], replicated, may hold values from -0.00036621094 to 0.00036621094
- second_qkv: float32 [2048, 3072], P(('fsdp', 'dp')), may hold values from 8.714005e-10 to 3.452719e-09
- second_out: float32 [2048, 2048], P(('fsdp', 'dp')), may hold values from 8.714005e-10 to 3.452719e-09
- second_gate_up: float32 [2048, 16384], P(('fsdp', 'dp')), may hold values from 8.714005e-10 to 3.452719e-09
- second_down: float32 [8192, 2048], P(('fsdp', 'dp')), may hold values from 8.714005e-10 to 3.452719e-09
- second_gains: float32 [4224], replicated, may hold values from 1.3810876e-08 to 5.5901165e-08
Outputs:
- mixed: bfloat16 [8192, 2048], P(('fsdp', 'dp'))
- input_grad: float32 [8192, 2048], P(('fsdp', 'dp'))
- grad_norm: float32 [], replicated
- new_qkv: float32 [2048, 3072], P(('fsdp', 'dp'))
- new_out: float32 [2048, 2048], P(('fsdp', 'dp'))
- new_gate_up: float32 [2048, 16384], P(('fsdp', 'dp'))
- new_down: float32 [8192, 2048], P(('fsdp', 'dp'))
- new_gains: float32 [4224], replicated
- next_first_qkv: float32 [2048, 3072], P(('fsdp', 'dp'))
- next_first_out: float32 [2048, 2048], P(('fsdp', 'dp'))
- next_first_gate_up: float32 [2048, 16384], P(('fsdp', 'dp'))
- next_first_down: float32 [8192, 2048], P(('fsdp', 'dp'))
- next_first_gains: float32 [4224], replicated
- next_second_qkv: float32 [2048, 3072], P(('fsdp', 'dp'))
- next_second_out: float32 [2048, 2048], P(('fsdp', 'dp'))
- next_second_gate_up: float32 [2048, 16384], P(('fsdp', 'dp'))
- next_second_down: float32 [8192, 2048], P(('fsdp', 'dp'))
- next_second_gains: float32 [4224], replicated
Inputs may be any that keep to these rules, and one draw needn't show every extreme that they name: `order`: each row is a permutation. Each row holds 3 lengths summing to 128; the last length of a row is padding.
All inputs are finite; a program needn't handle non-finite values.
Results may differ from a plain program's by a relative error of at most 0.025.
Values may be sent and summed in bfloat16 or wider, within the bound.
A program may use at most 512 MiB of HBM per device.

v0:
```python
import jax
import jax.numpy as jnp
from jax import lax
from jax.sharding import PartitionSpec as P

D = 2048
HEADS = 32
HD = 64
KVH = 8
FF = 8192
TOK_DEV = 256
MB = 2
SEQS = 3
STEP = 10
MB_TOK = 128


EPSILON = 1e-05
ROPE_BASE = 1000000.0
FIRST_DECAY = 0.9
SECOND_DECAY = 0.95
LEARN_RATE = 0.05
GAIN_RATE = 2.0
WEIGHT_DECAY = 0.1
ADAM_EPSILON = 1e-08
CLIP_NORM = 1.0
MASKED = -1e30


def rms_norm(values, gain_vec):
    return (
        values * lax.rsqrt(jnp.mean(values * values, axis=-1, keepdims=True) + EPSILON) * gain_vec
    )


def rope_tables(position):
    half_width = HD // 2
    frequency = ROPE_BASE ** (jnp.arange(half_width, dtype=jnp.float32) * (-2.0 / HD))
    angles = position[:, None] * frequency[None, :]
    return (jnp.cos(angles)[:, None, :], jnp.sin(angles)[:, None, :])


def rotate(values, cosine_table, sine_table):
    half_width = HD // 2
    first_part = values[..., :half_width]
    second_part = values[..., half_width:]
    return jnp.concatenate(
        [
            first_part * cosine_table - second_part * sine_table,
            second_part * cosine_table + first_part * sine_table,
        ],
        axis=-1,
    )


def layout(lengths_row):
    seq_ends = jnp.cumsum(lengths_row)
    places = jnp.arange(MB_TOK, dtype=jnp.int32)
    passed = (places[:, None] >= seq_ends[None, :]).astype(jnp.int32)
    segment = jnp.sum(passed, axis=1)
    starts = jnp.sum(passed * lengths_row[None, :], axis=1)
    position = (places - starts).astype(jnp.float32)
    valid_rows = (segment < SEQS - 1).astype(jnp.float32)
    allowed = (segment[:, None] == segment[None, :]) & (places[None, :] <= places[:, None])
    return (position, valid_rows, allowed)


def swiglu(gate_up):
    return jax.nn.silu(gate_up[:, :FF]) * gate_up[:, FF:]


def column_product(left_side, right_side):
    return lax.dot_general(
        left_side, right_side, (((0,), (0,)), ((), ())), preferred_element_type=jnp.float32
    )


def contract_last(left_side, right_side):
    return lax.dot_general(
        left_side, right_side, (((1,), (1,)), ((), ())), preferred_element_type=jnp.float32
    )


def adam_step(weight, first_state, second, gradient, factor, step_rate, decay_rate):
    clipped = gradient * factor
    first_new = FIRST_DECAY * first_state + (1.0 - FIRST_DECAY) * clipped
    second_new = SECOND_DECAY * second + (1.0 - SECOND_DECAY) * clipped * clipped
    first_hat = first_new / (1.0 - FIRST_DECAY**STEP)
    second_hat = second_new / (1.0 - SECOND_DECAY**STEP)
    weight_new = weight - step_rate * (
        first_hat / (jnp.sqrt(second_hat) + ADAM_EPSILON) + decay_rate * weight
    )
    return (weight_new, first_new, second_new)


def per_device(
    tokens,
    cotangent,
    order,
    lengths,
    w_qkv,
    w_out,
    w_gate_up,
    w_down,
    gains,
    first_qkv,
    first_out,
    first_gate_up,
    first_down,
    first_gains,
    second_qkv,
    second_out,
    second_gate_up,
    second_down,
    second_gains,
):
    owned_rows = (
        lax.all_gather(w_qkv.astype(jnp.bfloat16), "dp", axis=0, tiled=True),
        lax.all_gather(w_out.astype(jnp.bfloat16), "dp", axis=0, tiled=True),
        lax.all_gather(w_gate_up.astype(jnp.bfloat16), "dp", axis=0, tiled=True),
        lax.all_gather(w_down.astype(jnp.bfloat16), "dp", axis=0, tiled=True),
    )
    order_row = order[0]
    places = jnp.arange(TOK_DEV, dtype=jnp.int32)
    inverse = jnp.zeros((TOK_DEV,), jnp.int32).at[order_row].set(places)
    packed_in = tokens[order_row]
    packed_back = cotangent[order_row]
    attn_gain = gains[:D]
    ffn_gain = gains[D : 2 * D]
    query_gain = gains[2 * D : 2 * D + HD]
    key_gain = gains[2 * D + HD :]
    group_size = HEADS // KVH
    kv_width = KVH * HD
    score_scale = HD ** (-0.5)
    gain_sum = jnp.zeros(gains.shape, jnp.float32)
    out_parts = []
    back_parts = []
    kept_act = []
    kept_down = []
    kept_norm_two = []
    kept_gate_up = []
    kept_attended = []
    kept_branch = []
    kept_norm_one = []
    kept_proj = []
    for micro_index in range(MB):
        first_row = micro_index * MB_TOK
        rows_in = packed_in[first_row : first_row + MB_TOK].astype(jnp.float32)
        back_rows = packed_back[first_row : first_row + MB_TOK].astype(jnp.float32)
        position, valid_rows, allowed = layout(lengths[micro_index])
        valid_col = valid_rows[:, None]
        cosine_table, sine_table = rope_tables(position)
        attn_pair = (
            lax.all_gather(owned_rows[0], "fsdp", axis=0, tiled=True),
            lax.all_gather(owned_rows[1], "fsdp", axis=0, tiled=True),
        )
        normed_one, norm_one_pull = jax.vjp(rms_norm, rows_in, attn_gain)
        normed_one_low = normed_one.astype(jnp.bfloat16)
        projected = jnp.dot(normed_one_low, attn_pair[0], preferred_element_type=jnp.float32)
        query_raw = projected[:, :D].reshape(MB_TOK, HEADS, HD)
        key_raw = projected[:, D : D + kv_width].reshape(MB_TOK, KVH, HD)
        values_low = projected[:, D + kv_width :].reshape(MB_TOK, KVH, HD).astype(jnp.bfloat16)

        def turn_heads(query_in, key_in, query_scale, key_scale):
            return (
                rotate(rms_norm(query_in, query_scale), cosine_table, sine_table),
                rotate(rms_norm(key_in, key_scale), cosine_table, sine_table),
            )

        turned, turn_pull = jax.vjp(turn_heads, query_raw, key_raw, query_gain, key_gain)
        queries_low = turned[0].astype(jnp.bfloat16).reshape(MB_TOK, KVH, group_size, HD)
        keys_low = turned[1].astype(jnp.bfloat16)
        scores = (
            jnp.einsum("tkgd,ukd->kgtu", queries_low, keys_low, preferred_element_type=jnp.float32)
            * score_scale
        )
        scores = jnp.where(allowed, scores, MASKED)
        row_peak = jnp.max(scores, axis=-1, keepdims=True)
        powers = jnp.exp(scores - row_peak)
        totals = jnp.sum(powers, axis=-1, keepdims=True)
        log_total = row_peak + jnp.log(totals)
        probs_low = (powers / totals).astype(jnp.bfloat16)
        attended = jnp.einsum(
            "kgtu,ukd->tkgd", probs_low, values_low, preferred_element_type=jnp.float32
        )
        attended_low = attended.reshape(MB_TOK, D).astype(jnp.bfloat16)
        hidden = rows_in + valid_col * jnp.dot(
            attended_low, attn_pair[1], preferred_element_type=jnp.float32
        )
        ffn_pair = (
            lax.all_gather(owned_rows[2], "fsdp", axis=0, tiled=True),
            lax.all_gather(owned_rows[3], "fsdp", axis=0, tiled=True),
        )
        normed_two, norm_two_pull = jax.vjp(rms_norm, hidden, ffn_gain)
        normed_two_low = normed_two.astype(jnp.bfloat16)
        gate_up = jnp.dot(normed_two_low, ffn_pair[0], preferred_element_type=jnp.float32)
        activation, glu_pull = jax.vjp(swiglu, gate_up)
        activation_low = activation.astype(jnp.bfloat16)
        output = hidden + valid_col * jnp.dot(
            activation_low, ffn_pair[1], preferred_element_type=jnp.float32
        )
        out_parts.append(output.astype(jnp.bfloat16))
        ffn_back = (
            lax.all_gather(owned_rows[2], "fsdp", axis=0, tiled=True),
            lax.all_gather(owned_rows[3], "fsdp", axis=0, tiled=True),
        )
        down_back = (valid_col * back_rows).astype(jnp.bfloat16)
        (gate_up_grad,) = glu_pull(contract_last(down_back, ffn_back[1]))
        gate_up_back = gate_up_grad.astype(jnp.bfloat16)
        normed_two_grad = contract_last(gate_up_back, ffn_back[0])
        kept_act.append(activation_low)
        kept_down.append(down_back)
        kept_norm_two.append(normed_two_low)
        kept_gate_up.append(gate_up_back)
        hidden_norm_grad, ffn_gain_grad = norm_two_pull(normed_two_grad)
        hidden_grad = back_rows + hidden_norm_grad
        attn_back = (
            lax.all_gather(owned_rows[0], "fsdp", axis=0, tiled=True),
            lax.all_gather(owned_rows[1], "fsdp", axis=0, tiled=True),
        )
        branch_back = (valid_col * hidden_grad).astype(jnp.bfloat16)
        attended_back = contract_last(branch_back, attn_back[1]).astype(jnp.bfloat16)
        kept_attended.append(attended_low)
        kept_branch.append(branch_back)
        attended_four = attended_back.reshape(MB_TOK, KVH, group_size, HD)
        scores_again = (
            jnp.einsum("tkgd,ukd->kgtu", queries_low, keys_low, preferred_element_type=jnp.float32)
            * score_scale
        )
        scores_again = jnp.where(allowed, scores_again, MASKED)
        probs_again = jnp.exp(scores_again - log_total)
        probs_grad = jnp.einsum(
            "tkgd,ukd->kgtu", attended_four, values_low, preferred_element_type=jnp.float32
        )
        spread = jnp.sum(probs_again * probs_grad, axis=-1, keepdims=True)
        score_back = (probs_again * (probs_grad - spread)).astype(jnp.bfloat16)
        query_grad = (
            jnp.einsum("kgtu,ukd->tkgd", score_back, keys_low, preferred_element_type=jnp.float32)
            * score_scale
        )
        key_grad = (
            jnp.einsum(
                "kgtu,tkgd->ukd", score_back, queries_low, preferred_element_type=jnp.float32
            )
            * score_scale
        )
        value_grad = jnp.einsum(
            "kgtu,tkgd->ukd",
            probs_again.astype(jnp.bfloat16),
            attended_four,
            preferred_element_type=jnp.float32,
        )
        query_in_grad, key_in_grad, query_gain_grad, key_gain_grad = turn_pull(
            (query_grad.reshape(MB_TOK, HEADS, HD), key_grad)
        )
        projected_back = jnp.concatenate(
            [
                query_in_grad.reshape(MB_TOK, D),
                key_in_grad.reshape(MB_TOK, kv_width),
                value_grad.reshape(MB_TOK, kv_width),
            ],
            axis=1,
        ).astype(jnp.bfloat16)
        normed_one_grad = contract_last(projected_back, attn_back[0])
        kept_norm_one.append(normed_one_low)
        kept_proj.append(projected_back)
        rows_grad, attn_gain_grad = norm_one_pull(normed_one_grad)
        back_parts.append(hidden_grad + rows_grad)
        gain_sum = gain_sum + jnp.concatenate(
            [attn_gain_grad, ffn_gain_grad, query_gain_grad, key_gain_grad]
        )
    grad_down = lax.psum_scatter(
        column_product(
            jnp.concatenate(kept_act, axis=0), jnp.concatenate(kept_down, axis=0)
        ).astype(jnp.bfloat16),
        "fsdp",
        scatter_dimension=0,
        tiled=True,
    )
    grad_gate_up = lax.psum_scatter(
        column_product(
            jnp.concatenate(kept_norm_two, axis=0), jnp.concatenate(kept_gate_up, axis=0)
        ).astype(jnp.bfloat16),
        "fsdp",
        scatter_dimension=0,
        tiled=True,
    )
    grad_out = lax.psum_scatter(
        column_product(
            jnp.concatenate(kept_attended, axis=0), jnp.concatenate(kept_branch, axis=0)
        ).astype(jnp.bfloat16),
        "fsdp",
        scatter_dimension=0,
        tiled=True,
    )
    grad_qkv = lax.psum_scatter(
        column_product(
            jnp.concatenate(kept_norm_one, axis=0), jnp.concatenate(kept_proj, axis=0)
        ).astype(jnp.bfloat16),
        "fsdp",
        scatter_dimension=0,
        tiled=True,
    )
    output_all = jnp.concatenate(out_parts, axis=0)[inverse]
    input_grad = jnp.concatenate(back_parts, axis=0)[inverse]
    owned = (
        lax.psum_scatter(grad_qkv, "dp", scatter_dimension=0, tiled=True).astype(jnp.float32),
        lax.psum_scatter(grad_out, "dp", scatter_dimension=0, tiled=True).astype(jnp.float32),
        lax.psum_scatter(grad_gate_up, "dp", scatter_dimension=0, tiled=True).astype(jnp.float32),
        lax.psum_scatter(grad_down, "dp", scatter_dimension=0, tiled=True).astype(jnp.float32),
    )
    local_squares = (
        jnp.sum(owned[0] * owned[0])
        + jnp.sum(owned[1] * owned[1])
        + jnp.sum(owned[2] * owned[2])
        + jnp.sum(owned[3] * owned[3])
    )
    gain_total, square_total = lax.psum((gain_sum, local_squares), ("fsdp", "dp"))
    global_norm = jnp.sqrt(square_total + jnp.sum(gain_total * gain_total))
    factor = CLIP_NORM / jnp.maximum(global_norm, CLIP_NORM)
    new_qkv, next_first_qkv, next_second_qkv = adam_step(
        w_qkv, first_qkv, second_qkv, owned[0], factor, LEARN_RATE, WEIGHT_DECAY
    )
    new_out, next_first_out, next_second_out = adam_step(
        w_out, first_out, second_out, owned[1], factor, LEARN_RATE, WEIGHT_DECAY
    )
    new_gate_up, next_first_gate_up, next_second_gate_up = adam_step(
        w_gate_up, first_gate_up, second_gate_up, owned[2], factor, LEARN_RATE, WEIGHT_DECAY
    )
    new_down, next_first_down, next_second_down = adam_step(
        w_down, first_down, second_down, owned[3], factor, LEARN_RATE, WEIGHT_DECAY
    )
    new_gains, next_first_gains, next_second_gains = adam_step(
        gains, first_gains, second_gains, gain_total, factor, GAIN_RATE, 0.0
    )
    return (
        output_all,
        input_grad,
        global_norm,
        new_qkv,
        new_out,
        new_gate_up,
        new_down,
        new_gains,
        next_first_qkv,
        next_first_out,
        next_first_gate_up,
        next_first_down,
        next_first_gains,
        next_second_qkv,
        next_second_out,
        next_second_gate_up,
        next_second_down,
        next_second_gains,
    )


def solution(mesh):
    in_specs = (
        P(("fsdp", "dp"), None),
        P(("fsdp", "dp"), None),
        P(("fsdp", "dp"), None),
        P(("fsdp", "dp"), None),
        P(("fsdp", "dp"), None),
        P(("fsdp", "dp"), None),
        P(("fsdp", "dp"), None),
        P(("fsdp", "dp"), None),
        P(),
        P(("fsdp", "dp"), None),
        P(("fsdp", "dp"), None),
        P(("fsdp", "dp"), None),
        P(("fsdp", "dp"), None),
        P(),
        P(("fsdp", "dp"), None),
        P(("fsdp", "dp"), None),
        P(("fsdp", "dp"), None),
        P(("fsdp", "dp"), None),
        P(),
    )
    out_specs = (
        P(("fsdp", "dp"), None),
        P(("fsdp", "dp"), None),
        P(),
        P(("fsdp", "dp"), None),
        P(("fsdp", "dp"), None),
        P(("fsdp", "dp"), None),
        P(("fsdp", "dp"), None),
        P(),
        P(("fsdp", "dp"), None),
        P(("fsdp", "dp"), None),
        P(("fsdp", "dp"), None),
        P(("fsdp", "dp"), None),
        P(),
        P(("fsdp", "dp"), None),
        P(("fsdp", "dp"), None),
        P(("fsdp", "dp"), None),
        P(("fsdp", "dp"), None),
        P(),
    )
    return jax.shard_map(
        per_device, mesh=mesh, in_specs=in_specs, out_specs=out_specs, check_vma=False
    )
```

profile of v0, /device:TPU:0, one launch (start us, length us, event | category | flops | bytes accessed | tf_op | source)
XLA Modules:
  0.0 2193.9 jit_solution(7116295364406105708)
XLA Ops:
  16.3 33.7 %all-gather.9.cloned.1.call-done = bf16[256,3072]{1,0:T(8,128)(2,1)} async-done(((bf16[64,3072]{1,0:T(8,128)(2,1)}), bf16[256,3072]{1,0:T(8,128)(2,1)}) %all-gather.9.cloned.1.call-update) | async-done | bytes 1572880 | tf_op jit(solution)/shard_map/all_gather | solution.py:118
  50.1 28.9 %all-gather.13.cloned.1.call-done = bf16[256,2048]{1,0:T(8,128)(2,1)} async-done(((bf16[64,2048]{1,0:T(8,128)(2,1)}), bf16[256,2048]{1,0:T(8,128)(2,1)}) %all-gather.13.cloned.1.call-update) | async-done | bytes 1048592 | tf_op jit(solution)/shard_map/all_gather | solution.py:119
  79.0 151.2 %all-gather.17.cloned.1.call-done = bf16[256,16384]{1,0:T(8,128)(2,1)} async-done(((bf16[64,16384]{1,0:T(8,128)(2,1)}), bf16[256,16384]{1,0:T(8,128)(2,1)}) %all-gather.17.cloned.1.call-update) | async-done | bytes 8388624 | tf_op jit(solution)/shard_map/all_gather | solution.py:120
  230.4 80.9 %all-gather.21.cloned.1.call-done = bf16[1024,2048]{1,0:T(8,128)(2,1)} async-done(((bf16[256,2048]{1,0:T(8,128)(2,1)}), bf16[1024,2048]{1,0:T(8,128)(2,1)}) %all-gather.21.cloned.1.call-update) | async-done | bytes 4194320 | tf_op jit(solution)/shard_map/all_gather | solution.py:121
  321.3 62.4 %all-gather.11.cloned.1.call-done = bf16[2048,3072]{1,0:T(8,128)(2,1)} async-done(((bf16[256,3072]{1,0:T(8,128)(2,1)}), bf16[2048,3072]{1,0:T(8,128)(2,1)}) %all-gather.11.cloned.1.call-update) | async-done | bytes 12582928 | tf_op jit(solution)/shard_map/all_gather | solution.py:154
  410.1 29.9 %all-gather.15.cloned.1.call-done = bf16[2048,2048]{1,0:T(8,128)(2,1)} async-done(((bf16[256,2048]{1,0:T(8,128)(2,1)}), bf16[2048,2048]{1,0:T(8,128)(2,1)}) %all-gather.15.cloned.1.call-update) | async-done | bytes 8388624 | tf_op jit(solution)/shard_map/all_gather | solution.py:155
  448.3 296.3 %all-gather.19.cloned.1.call-done = bf16[2048,16384]{1,0:T(8,128)(2,1)} async-done(((bf16[256,16384]{1,0:T(8,128)(2,1)}), bf16[2048,16384]{1,0:T(8,128)(2,1)}) %all-gather.19.cloned.1.call-update) | async-done | bytes 67108880 | tf_op jit(solution)/shard_map/all_gather | solution.py:191
  744.7 30.3 %fusion.153 = f32[128,16384]{1,0:T(8,128)} fusion(bf16[128,2048]{1,0:T(8,128)(2,1)S(1)} %multiply_convert_fusion.5, bf16[2048,16384]{1,0:T(8,128)(2,1)} %all-gather.19.cloned.1.call-done), kind=kOutput, calls=%fused_computation.321 | convolution fusion | flops 8589934592 | bytes 76021760 | tf_op jit(solution)/shard_map/dot_general | solution.py:196
  775.0 132.4 %all-gather.23.cloned.1.call-done = bf16[8192,2048]{1,0:T(8,128)(2,1)} async-done(((bf16[1024,2048]{1,0:T(8,128)(2,1)}), bf16[8192,2048]{1,0:T(8,128)(2,1)}) %all-gather.23.cloned.1.call-update) | async-done | bytes 33554448 | tf_op jit(solution)/shard_map/all_gather | solution.py:192
  907.4 22.5 %fusion.110 = (f32[128,8192]{1,0:T(8,128)}, f32[128,8192]{1,0:T(8,128)}, bf16[128,8192]{1,0:T(8,128)(2,1)}) fusion(f32[128,16384]{1,0:T(8,128)} %fusion.153, bf16[128,2048]{1,0:T(8,128)(2,1)S(1)} %copy-done.49, bf16[8192,2048]{1,0:T(8,128)(2,1)} %all-gather.23.cloned.1.call-done), kind=kOutput, calls=%fused_computation.217 | convolution fusion | flops 4309647360 | bytes 52953088 | tf_op jit(solution)/shard_map/dot_general | solution.py:79
  935.8 30.4 %multiply_reduce_fusion.3 = (f32[2048]{0:T(1024)}, f32[128]{0:T(128)S(1)}, bf16[128,2048]{1,0:T(8,128)(2,1)S(1)}, f32[128,2048]{1,0:T(8,128)}) fusion(f32[128,2048]{1,0:T(8,128)S(1)} %get-tuple-element.119, f32[128]{0:T(128)S(1)} %fusion.124, f32[2048]{0:T(1024)S(1)} %copy-done.85, f32[128,2048]{1,0:T(8,128)S(1)} %get-tuple-element.121, ...), kind=kOutput, calls=%fused_computation.161 | convolution fusion | flops 8592291840 | bytes 74991104 | tf_op jit(solution)/shard_map/dot_general | solution.py:79
  966.2 26.3 %fusion.155 = f32[128,16384]{1,0:T(8,128)} fusion(bf16[128,2048]{1,0:T(8,128)(2,1)S(1)} %get-tuple-element.91, bf16[2048,16384]{1,0:T(8,128)(2,1)} %all-gather.19.cloned.1.call-done), kind=kOutput, calls=%fused_computation.323 | convolution fusion | flops 8589934592 | bytes 76021760 | tf_op jit(solution)/shard_map/dot_general | solution.py:196
  992.5 22.9 %fusion.111 = (f32[128,8192]{1,0:T(8,128)}, f32[128,8192]{1,0:T(8,128)}, bf16[128,8192]{1,0:T(8,128)(2,1)}) fusion(f32[128,16384]{1,0:T(8,128)} %fusion.155, bf16[128,2048]{1,0:T(8,128)(2,1)S(1)} %copy-done.51, bf16[8192,2048]{1,0:T(8,128)(2,1)} %all-gather.23.cloned.1.call-done), kind=kOutput, calls=%fused_computation.218 | convolution fusion | flops 4309647360 | bytes 52953088 | tf_op jit(solution)/shard_map/dot_general | solution.py:79
  1021.5 29.8 %multiply_reduce_fusion.1 = (f32[2048]{0:T(1024)S(1)}, f32[128]{0:T(128)S(1)}, f32[128,2048]{1,0:T(8,128)}) fusion(f32[128,2048]{1,0:T(8,128)S(1)} %get-tuple-element.121, f32[128]{0:T(128)S(1)} %fusion.126, f32[2048]{0:T(1024)S(1)} %copy-done.85, bf16[128,16384]{1,0:T(8,128)(2,1)} %add_convert_fusion, bf16[2048,16384]{1,0:T(8,128)(2,1)} %all-gather.19.cloned.1.call-done), kind=kOutput, calls=%fused_computation.159 | convolution fusion | flops 8591505408 | bytes 73417728 | tf_op jit(solution)/shard_map/dot_general | solution.py:79
  1101.8 16.3 convolution_convert_fusion.1
  1119.3 34.7 %convolution_convert_fusion = bf16[2048,16384]{1,0:T(8,128)(2,1)} fusion(bf16[128,16384]{1,0:T(8,128)(2,1)} %add_convert_fusion, bf16[128,16384]{1,0:T(8,128)(2,1)} %add_convert_fusion.1, bf16[128,2048]{1,0:T(8,128)(2,1)S(1)} %copy-done.31, bf16[128,2048]{1,0:T(8,128)(2,1)S(1)} %copy-done.33), kind=kOutput, calls=%fused_computation.5 | convolution fusion | flops 17232297984 | bytes 76546048 | tf_op jit(solution)/shard_map/dot_general | solution.py:73
  1154.7 73.1 %reduce-scatter.9.cloned.1.call-done = bf16[256,3072]{1,0:T(8,128)(2,1)} async-done(((bf16[2048,3072]{1,0:T(8,128)(2,1)}), bf16[256,3072]{1,0:T(8,128)(2,1)}) %reduce-scatter.9.cloned.1.call-update) | async-done | bytes 1572880 | tf_op jit(solution)/shard_map/reduce_scatter | solution.py:296
  1227.9 209.2 %reduce-scatter.21.cloned.1.call-done = bf16[1024,2048]{1,0:T(8,128)(2,1)} async-done(((bf16[8192,2048]{1,0:T(8,128)(2,1)}), bf16[1024,2048]{1,0:T(8,128)(2,1)}) %reduce-scatter.21.cloned.1.call-update) | async-done | bytes 4194320 | tf_op jit(solution)/shard_map/reduce_scatter | solution.py:272
  1437.2 387.1 %reduce-scatter.17.cloned.1.call-done = bf16[256,16384]{1,0:T(8,128)(2,1)} async-done(((bf16[2048,16384]{1,0:T(8,128)(2,1)}), bf16[256,16384]{1,0:T(8,128)(2,1)}) %reduce-scatter.17.cloned.1.call-update) | async-done | bytes 8388624 | tf_op jit(solution)/shard_map/reduce_scatter | solution.py:280
  1852.4 16.4 fusion.21
  1868.8 13.3 fusion.22
  1893.2 74.8 %reduce-scatter.23.cloned.1.call-done = bf16[256,2048]{1,0:T(8,128)(2,1)} async-done(((bf16[1024,2048]{1,0:T(8,128)(2,1)}), bf16[256,2048]{1,0:T(8,128)(2,1)}) %reduce-scatter.23.cloned.1.call-update) | async-done | bytes 1048592 | tf_op jit(solution)/shard_map/reduce_scatter | solution.py:310
  1970.3 145.0 %reduce-scatter.19.cloned.1.call-done = bf16[64,16384]{1,0:T(8,128)(2,1)} async-done(((bf16[256,16384]{1,0:T(8,128)(2,1)}), bf16[64,16384]{1,0:T(8,128)(2,1)}) %reduce-scatter.19.cloned.1.call-update) | async-done | bytes 2097168 | tf_op jit(solution)/shard_map/reduce_scatter | solution.py:309
  2122.3 41.5 %all-reduce.12 = (f32[]{:T(128)}, f32[4224]{0:T(1024)S(1)}) all-reduce(f32[]{:T(128)S(6)} %add.317, f32[4224]{0:T(1024)S(1)} %add.318), channel_id=1, replica_groups=mesh['fsdp'=8,'dp'=4] {'fsdp','dp'}, use_global_device_ids=true, to_apply=%region_41.42 | all-reduce | flops 4225 | bytes 33800 | tf_op jit(solution)/shard_map/psum | solution.py:318
  (453 shorter events, 183.2 us)
Async XLA Ops:
  7.2 305.1 %copy-start = (bf16[256,2048]{1,0:T(8,128)(2,1)S(1)}, bf16[256,2048]{1,0:T(8,128)(2,1)}, u32[]{:S(2)}) copy-start(bf16[256,2048]{1,0:T(8,128)(2,1)} %param.19) | copy-start | bytes 3145732
  7.2 42.8 %all-gather.9.cloned.1.call-start = ((), (), s32[]{:S(2)}) async-start(), calls=%async_computation.8 | async-start | bytes 1966080 | tf_op jit(solution)/shard_map/all_gather | solution.py:118
  9.3 69.7 %all-gather.13.cloned.1.call-start = ((), (), s32[]{:S(2)}) async-start(), calls=%async_computation.10 | async-start | bytes 1310720 | tf_op jit(solution)/shard_map/all_gather | solution.py:119
  11.1 219.1 %all-gather.17.cloned.1.call-start = ((), (), s32[]{:S(2)}) async-start(), calls=%async_computation.12 | async-start | bytes 10485760 | tf_op jit(solution)/shard_map/all_gather | solution.py:120
  15.1 296.2 %all-gather.21.cloned.1.call-start = ((), (), s32[]{:S(2)}) async-start(), calls=%async_computation.14 | async-start | bytes 5242880 | tf_op jit(solution)/shard_map/all_gather | solution.py:121
  16.3 367.5 %all-gather.11.cloned.1.call-start = ((), (), s32[]{:S(2)}) async-start(), calls=%async_computation.9 | async-start | bytes 14155776 | tf_op jit(solution)/shard_map/all_gather | solution.py:154
  50.0 389.9 %all-gather.15.cloned.1.call-start = ((), (), s32[]{:S(2)}) async-start(), calls=%async_computation.11 | async-start | bytes 9437184 | tf_op jit(solution)/shard_map/all_gather | solution.py:155
  79.0 665.7 %all-gather.19.cloned.1.call-start = ((), (), s32[]{:S(2)}) async-start(), calls=%async_computation.13 | async-start | bytes 75497472 | tf_op jit(solution)/shard_map/all_gather | solution.py:191
  230.3 81.1 %copy-start.143 = (s32[2,3]{1,0:T(2,128)S(1)}, s32[2,3]{1,0:T(2,128)}, u32[]{:S(2)}) copy-start(s32[2,3]{1,0:T(2,128)} %param.22) | copy-start | bytes 76
  230.3 81.4 %copy-start.144 = (s32[1,256]{1,0:T(1,128)S(1)}, s32[1,256]{1,0:T(1,128)}, u32[]{:S(2)}) copy-start(s32[1,256]{1,0:T(1,128)} %param.21) | copy-start | bytes 3076
  230.3 677.0 %all-gather.23.cloned.1.call-start = ((), (), s32[]{:S(2)}) async-start(), calls=%async_computation.15 | async-start | bytes 37748736 | tf_op jit(solution)/shard_map/all_gather | solution.py:192
  311.3 842.7 %reduce-scatter.13.cloned.1.call-start = ((), (), s32[]{:S(2)}) async-start(), calls=%async_computation.18 | async-start | bytes 9437184 | tf_op jit(solution)/shard_map/reduce_scatter | solution.py:288
  313.7 132.0 %copy-start.16 = (bf16[256,2048]{1,0:T(8,128)(2,1)}, bf16[256,2048]{1,0:T(8,128)(2,1)S(1)}, u32[]{:S(2)}) copy-start(bf16[256,2048]{1,0:T(8,128)(2,1)S(1)} %gather_fusion) | copy-start | bytes 3145732
  319.1 86.5 %copy-start.77 = (f32[128,32]{0,1:T(8,128)}, f32[128,32]{0,1:T(8,128)S(1)}, u32[]{:S(2)}) copy-start(f32[128,32]{0,1:T(8,128)S(1)} %get-tuple-element.92) | copy-start | bytes 49156
  445.1 1403.7 %copy-start.5 = (f32[128,2048]{1,0:T(8,128)}, f32[128,2048]{1,0:T(8,128)S(1)}, u32[]{:S(2)}) copy-start(f32[128,2048]{1,0:T(8,128)S(1)} %get-tuple-element.119) | copy-start | bytes 3145732
  448.3 326.6 %copy-start.32 = (bf16[128,2048]{1,0:T(8,128)(2,1)}, bf16[128,2048]{1,0:T(8,128)(2,1)S(1)}, u32[]{:S(2)}) copy-start(bf16[128,2048]{1,0:T(8,128)(2,1)S(1)} %multiply_convert_fusion.5) | copy-start | bytes 1572868
  448.3 459.0 %copy-start.49 = (bf16[128,2048]{1,0:T(8,128)(2,1)S(1)}, bf16[128,2048]{1,0:T(8,128)(2,1)}, u32[]{:S(2)}) copy-start(bf16[128,2048]{1,0:T(8,128)(2,1)} %get-tuple-element.77) | copy-start | bytes 1572868
  1060.2 167.6 %reduce-scatter.9.cloned.1.call-start = ((), (), s32[]{:S(2)}) async-start(), calls=%async_computation.16 | async-start | bytes 14155776 | tf_op jit(solution)/shard_map/reduce_scatter | solution.py:296
  1100.6 336.5 %reduce-scatter.21.cloned.1.call-start = ((), (), s32[]{:S(2)}) async-start(), calls=%async_computation.22 | async-start | bytes 37748736 | tf_op jit(solution)/shard_map/reduce_scatter | solution.py:272
  1118.1 706.3 %reduce-scatter.17.cloned.1.call-start = ((), (), s32[]{:S(2)}) async-start(), calls=%async_computation.20 | async-start | bytes 75497472 | tf_op jit(solution)/shard_map/reduce_scatter | solution.py:280
  1153.9 728.3 %reduce-scatter.15.cloned.1.call-start = ((), (), s32[]{:S(2)}) async-start(), calls=%async_computation.19 | async-start | bytes 1310720 | tf_op jit(solution)/shard_map/reduce_scatter | solution.py:308
  1154.7 735.4 %reduce-scatter.11.cloned.1.call-start = ((), (), s32[]{:S(2)}) async-start(), calls=%async_computation.17 | async-start | bytes 1966080 | tf_op jit(solution)/shard_map/reduce_scatter | solution.py:307
  1227.9 740.1 %reduce-scatter.23.cloned.1.call-start = ((), (), s32[]{:S(2)}) async-start(), calls=%async_computation.23 | async-start | bytes 5242880 | tf_op jit(solution)/shard_map/reduce_scatter | solution.py:310
  1437.2 678.1 %reduce-scatter.19.cloned.1.call-start = ((), (), s32[]{:S(2)}) async-start(), calls=%async_computation.21 | async-start | bytes 10485760 | tf_op jit(solution)/shard_map/reduce_scatter | solution.py:309
  (137 other events, 1279.9 us)
Sparse Core Ops, SparseCore 0:
  10.2 39.7 all-gather.8
  52.1 26.7 all-gather.12
  81.1 149.1 all-gather.16
  232.3 78.9 all-gather.20
  313.1 70.6 all-gather.10
  385.5 54.3 all-gather.14
  441.8 302.8 all-gather.18
  746.5 160.7 all-gather.22
  1060.4 71.2 reduce-scatter.12
  1135.4 92.3 reduce-scatter.8
  1231.8 205.2 reduce-scatter.20
  1440.6 383.7 reduce-scatter.16
  1826.8 27.1 reduce-scatter.14
  1856.1 33.9 reduce-scatter.10
  1892.2 75.7 reduce-scatter.22
  1970.3 144.9 reduce-scatter.18
where the time goes:
time: 2200 us; the launch traced here: 2190 us
  waiting for transfers between devices  1710 us (78%)
  matrix products  314 us (14%)
  other arithmetic  67.6 us (3%)
  blocking collectives  41.5 us (2%)
  local copies, waits for them, and re-layouts  36.1 us (2%)
    reduce_scatter x1, waiting for transfers between devices, per_device(): lax.psum_scatter(column_product(jnp.concatenate(kept_norm_two, axis=0), j...  387 us
    all_gather x1, waiting for transfers between devices, per_device(): lax.all_gather(owned_rows[2], 'fsdp', axis=0, tiled=True)  296 us
    reduce_scatter x1, waiting for transfers between devices, per_device(): lax.psum_scatter(column_product(jnp.concatenate(kept_act, axis=0), jnp.co...  209 us
    all_gather x1, waiting for transfers between devices, per_device(): lax.all_gather(w_gate_up.astype(jnp.bfloat16), 'dp', axis=0, tiled=True)  151 us
    reduce_scatter x1, waiting for transfers between devices, per_device(): lax.psum_scatter(grad_gate_up, 'dp', scatter_dimension=0, tiled=True)  145 us
    dot_general x8, matrix products, contract_last(): lax.dot_general(left_side, right_side, (((1,), (1,)), ((), ())), preferre...  141 us
    all_gather x1, waiting for transfers between devices, per_device(): lax.all_gather(owned_rows[3], 'fsdp', axis=0, tiled=True)  132 us
    all_gather x1, waiting for transfers between devices, per_device(): lax.all_gather(w_down.astype(jnp.bfloat16), 'dp', axis=0, tiled=True)  80.9 us
  transfers between devices with their start and end apart: 16, of which 14 were waited for; matrix products, arithmetic and copies ran while one was open for 10% of the time, Pallas kernels for 0%

commit v1 on v0

v1 whole, which is shorter than its diff:
```python
import functools

import jax
import jax.numpy as jnp
from jax import lax
from jax.experimental import pallas as pl
from jax.experimental.pallas import tpu as pltpu
from jax.sharding import PartitionSpec as P

D = 2048
HEADS = 32
HD = 64
KVH = 8
FF = 8192
TOK_DEV = 256
MB = 2
SEQS = 3
STEP = 10
MB_TOK = 128


EPSILON = 1e-05
ROPE_BASE = 1000000.0
FIRST_DECAY = 0.9
SECOND_DECAY = 0.95
LEARN_RATE = 0.05
GAIN_RATE = 2.0
WEIGHT_DECAY = 0.1
ADAM_EPSILON = 1e-08
CLIP_NORM = 1.0
GAIN_LINES = (2 * D + 2 * HD) // 128
MASKED = -1e30


def rms_norm(values, gain_vec):
    return (
        values * lax.rsqrt(jnp.mean(values * values, axis=-1, keepdims=True) + EPSILON) * gain_vec
    )


def rope_tables(position):
    half_width = HD // 2
    frequency = ROPE_BASE ** (jnp.arange(half_width, dtype=jnp.float32) * (-2.0 / HD))
    angles = position[:, None] * frequency[None, :]
    return (jnp.cos(angles)[:, None, :], jnp.sin(angles)[:, None, :])


def rotate(values, cosine_table, sine_table):
    half_width = HD // 2
    first_part = values[..., :half_width]
    second_part = values[..., half_width:]
    return jnp.concatenate(
        [
            first_part * cosine_table - second_part * sine_table,
            second_part * cosine_table + first_part * sine_table,
        ],
        axis=-1,
    )


def layout(lengths_rows):
    seq_ends = jnp.cumsum(lengths_rows, axis=-1)
    places = jnp.arange(MB_TOK, dtype=jnp.int32)
    passed = (places[None, :, None] >= seq_ends[:, None, :]).astype(jnp.int32)
    segment = jnp.sum(passed, axis=-1)
    starts = jnp.sum(passed * lengths_rows[:, None, :], axis=-1)
    position = (places[None, :] - starts).astype(jnp.float32)
    valid_rows = (segment < SEQS - 1).astype(jnp.float32)
    allowed = (segment[:, :, None] == segment[:, None, :]) & (
        places[None, None, :] <= places[None, :, None]
    )
    return (position, valid_rows, allowed)


def swiglu(gate, up):
    return jax.nn.silu(gate) * up


def column_product(left_side, right_side):
    return lax.dot_general(
        left_side, right_side, (((0,), (0,)), ((), ())), preferred_element_type=jnp.float32
    )


def contract_last(left_side, right_side):
    return lax.dot_general(
        left_side, right_side, (((1,), (1,)), ((), ())), preferred_element_type=jnp.float32
    )


def product(left_side, right_side):
    return jnp.dot(left_side, right_side, preferred_element_type=jnp.float32)


def adam_step(weight, first_state, second, gradient, factor, step_rate, decay_rate):
    clipped = gradient * factor
    first_new = FIRST_DECAY * first_state + (1.0 - FIRST_DECAY) * clipped
    second_new = SECOND_DECAY * second + (1.0 - SECOND_DECAY) * clipped * clipped
    first_hat = first_new / (1.0 - FIRST_DECAY**STEP)
    second_hat = second_new / (1.0 - SECOND_DECAY**STEP)
    weight_new = weight - step_rate * (
        first_hat / (jnp.sqrt(second_hat) + ADAM_EPSILON) + decay_rate * weight
    )
    return (weight_new, first_new, second_new)


MESH = pl.DeviceIdType.MESH
ANY = pl.BlockSpec(memory_space=pl.ANY)
VMEM = pl.BlockSpec(memory_space=pltpu.VMEM)
PLANE = 8
TILE = 512
GLU_TILE = 256
SHORT = pl.CostEstimate(flops=0, bytes_accessed=1024, transcendentals=0)


def flip(index, bit):
    step = 2**bit
    return index + step * (1 - 2 * lax.rem(lax.div(index, step), 2))


def plane_others(me):
    others = []
    for number in range(1, PLANE):
        other = me
        for bit in range(3):
            if (number >> bit) & 1:
                other = flip(other, bit)
        others.append(other)
    return others


def greet(devices):
    barrier = pltpu.get_barrier_semaphore()
    for device in devices:
        pl.semaphore_signal(barrier, inc=1, device_id={"fsdp": device}, device_id_type=MESH)
    pl.semaphore_wait(barrier, len(devices))


def half_pieces(half_ref, wide_ref, me, other, count):
    half_width = half_ref.shape[1] // 2
    for side in range(2):
        first = pl.multiple_of(side * half_width * PLANE + me * half_width, 128)
        source = half_ref.at[pl.ds(pl.multiple_of(other * count, count), count)]
        yield (
            source.at[:, pl.ds(side * half_width, half_width)],
            wide_ref.at[:, pl.ds(first, half_width)],
        )


def put_half(half_ref, wide_ref, others, number, sems):
    me, other = lax.axis_index("fsdp"), others[number - 1]
    pairs = half_pieces(half_ref, wide_ref, me, other, wide_ref.shape[0])
    return [
        pltpu.make_async_remote_copy(
            src_ref=source,
            dst_ref=target,
            send_sem=sems.at[0, 2 * number + side],
            recv_sem=sems.at[1, 2 * number + side],
            device_id={"fsdp": other},
            device_id_type=MESH,
        )
        for side, (source, target) in enumerate(pairs)
    ]


def keep_half(half_ref, wide_ref, sems):
    me = lax.axis_index("fsdp")
    return [
        pltpu.make_async_copy(source, target, sems.at[side])
        for side, (source, target) in enumerate(
            half_pieces(half_ref, wide_ref, me, me, wide_ref.shape[0])
        )
    ]


def columns_kernel(half_ref, wide_ref, squares_ref, own_sem, sems):
    others = plane_others(lax.axis_index("fsdp"))
    greet(others)
    order = (6, 7, 2, 4, 3, 5, 1)
    for number in order:
        for copy in put_half(half_ref, wide_ref, others, number, sems):
            copy.start()
    keep = keep_half(half_ref, wide_ref, own_sem)
    for copy in keep:
        copy.start()
    squares_ref[...] = jnp.zeros_like(squares_ref)

    @pl.loop(0, half_ref.shape[0] // 128)
    def _(step):
        spot = pl.ds(pl.multiple_of(step * 128, 128), 128)
        values = half_ref[spot, :].astype(jnp.float32)
        squares_ref[...] += jnp.sum(values * values, axis=0, keepdims=True)

    for number in order:
        for copy in put_half(half_ref, wide_ref, others, number, sems):
            copy.wait()
    for copy in keep:
        copy.wait()


def half_scratch():
    return [pltpu.SemaphoreType.DMA((2,)), pltpu.SemaphoreType.DMA((2, 2 * PLANE))]


def exchange_half(half, count, number):
    return pl.pallas_call(
        columns_kernel,
        out_shape=[
            jax.ShapeDtypeStruct((count, half.shape[1] * PLANE), half.dtype),
            jax.ShapeDtypeStruct((1, half.shape[1]), jnp.float32),
        ],
        in_specs=[VMEM],
        out_specs=[ANY, VMEM],
        scratch_shapes=half_scratch(),
        compiler_params=pltpu.CompilerParams(collective_id=number, has_side_effects=True),
        cost_estimate=SHORT,
        name=f"exchange_half_{number}",
    )(half)


def sum_kernel(
    nd,
    x_ref,
    blocks_ref,
    out_ref,
    norm_ref,
    qkv_ref,
    gout_ref,
    swapped_ref,
    plane_in,
    line_in,
    total,
    mine,
    own_sem,
    plane_sems,
    line_sems,
    block_sems,
):
    me, line = lax.axis_index("fsdp"), lax.axis_index("dp")
    wide = swapped_ref.shape[2]
    q_width = wide - 2 * HD
    blocks = blocks_ref[...].astype(jnp.float32)
    squares = jnp.sum(blocks * blocks, axis=(0, 1, 2), keepdims=True).reshape(1, 1)
    lines = lax.broadcasted_iota(jnp.int32, x_ref.shape, 0)
    lane = lax.broadcasted_iota(jnp.int32, x_ref.shape, 1)
    spot = jnp.logical_and(lines == GAIN_LINES, lane == 0)
    mine[...] = x_ref[...] + jnp.where(spot, squares, 0.0)
    others = plane_others(me)
    steps = [lax.rem(line + step, nd) for step in range(1, nd)]
    barrier = pltpu.get_barrier_semaphore()
    for other in others:
        pl.semaphore_signal(barrier, inc=1, device_id={"fsdp": other}, device_id_type=MESH)
    for other in steps:
        pl.semaphore_signal(barrier, inc=1, device_id={"dp": other}, device_id_type=MESH)
    pl.semaphore_wait(barrier, len(others) + len(steps))

    def to_plane(number):
        return pltpu.make_async_remote_copy(
            src_ref=mine,
            dst_ref=plane_in.at[me],
            send_sem=plane_sems.at[0, number],
            recv_sem=plane_sems.at[1, number],
            device_id={"fsdp": others[number]},
            device_id_type=MESH,
        )

    def to_line(number):
        return pltpu.make_async_remote_copy(
            src_ref=total,
            dst_ref=line_in.at[line],
            send_sem=line_sems.at[0, number],
            recv_sem=line_sems.at[1, number],
            device_id={"dp": steps[number]},
            device_id_type=MESH,
        )

    def put_block(number):
        return pltpu.make_async_remote_copy(
            src_ref=blocks_ref.at[others[number], :, pl.ds(0, wide)],
            dst_ref=swapped_ref.at[me],
            send_sem=block_sems.at[0, number],
            recv_sem=block_sems.at[1, number],
            device_id={"fsdp": others[number]},
            device_id_type=MESH,
        )

    keep = [
        pltpu.make_async_copy(
            blocks_ref.at[me, :, pl.ds(0, wide)], swapped_ref.at[me], own_sem.at[PLANE]
        )
    ]
    for place in range(PLANE):
        keep.append(
            pltpu.make_async_copy(
                blocks_ref.at[place, :, pl.ds(wide, q_width)],
                gout_ref.at[:, pl.ds(place * q_width, q_width)],
                own_sem.at[place],
            )
        )
    for number in range(PLANE - 1):
        to_plane(number).start()
    for number in range(PLANE - 1):
        put_block(number).start()
    for copy in keep:
        copy.start()
    plane_in[me] = mine[...]
    for number in range(PLANE - 1):
        to_plane(number).wait()
    part = plane_in[0]
    for place in range(1, PLANE):
        part = part + plane_in[place]
    total[...] = part
    line_in[line] = part
    for number in range(nd - 1):
        to_line(number).start()
    for number in range(PLANE - 1):
        put_block(number).wait()
    for copy in keep:
        copy.wait()
    first_head = lax.broadcasted_iota(jnp.int32, (1, 2 * HD), 1) < HD
    for place in range(0, PLANE, 2):
        pair = []
        for block in (place, place + 1):
            values = swapped_ref[block].astype(jnp.float32)
            qkv_ref[:, block * q_width : (block + 1) * q_width] = swapped_ref[block, :, :q_width]
            pair.append(values[:, q_width:])
        columns = pl.ds(PLANE * q_width + place * HD, 2 * HD)
        both = jnp.where(first_head, pair[0], pltpu.roll(pair[1], HD, 1))
        qkv_ref[:, columns] = both.astype(qkv_ref.dtype)
        columns = pl.ds(PLANE * (q_width + HD) + place * HD, 2 * HD)
        both = jnp.where(first_head, pltpu.roll(pair[0], HD, 1), pair[1])
        qkv_ref[:, columns] = both.astype(qkv_ref.dtype)
    for number in range(nd - 1):
        to_line(number).wait()
    part = line_in[0]
    for place in range(1, nd):
        part = part + line_in[place]
    out_ref[...] = part
    gains = part[:GAIN_LINES]
    lane = lax.broadcasted_iota(jnp.int32, (1, 128), 1)
    squares = jnp.where(lane == 0, part[GAIN_LINES : GAIN_LINES + 1], 0.0)
    squares = squares + jnp.sum(gains * gains, axis=0, keepdims=True)
    norm = jnp.sqrt(jnp.sum(squares, axis=1, keepdims=True))
    factor = CLIP_NORM / jnp.maximum(norm, CLIP_NORM)
    line_number = lax.broadcasted_iota(jnp.int32, norm_ref.shape, 0)
    norm_ref[...] = jnp.where(line_number == 0, norm, factor)


def sum_everywhere(gain_sum, squares, blocks, wide, number):
    values = jnp.concatenate([gain_sum, squares.reshape(1)])
    nd = lax.axis_size("dp")
    count = values.shape[0]
    lines = -(-count // 1024) * 8
    padded = jnp.pad(values, (0, lines * 128 - count)).reshape(lines, 128)
    q_width = wide - 2 * HD
    summed, norm, grad_qkv, grad_out = pl.pallas_call(
        functools.partial(sum_kernel, nd),
        out_shape=[
            jax.ShapeDtypeStruct(padded.shape, jnp.float32),
            jax.ShapeDtypeStruct((8, 128), jnp.float32),
            jax.ShapeDtypeStruct((blocks.shape[1], PLANE * wide), blocks.dtype),
            jax.ShapeDtypeStruct((blocks.shape[1], PLANE * q_width), blocks.dtype),
        ],
        in_specs=[VMEM, VMEM],
        out_specs=[VMEM] * 4,
        scratch_shapes=[
            pltpu.VMEM((PLANE, blocks.shape[1], wide), blocks.dtype),
            pltpu.VMEM((PLANE,) + padded.shape, jnp.float32),
            pltpu.VMEM((nd,) + padded.shape, jnp.float32),
            pltpu.VMEM(padded.shape, jnp.float32),
            pltpu.VMEM(padded.shape, jnp.float32),
            pltpu.SemaphoreType.DMA((PLANE + 1,)),
            pltpu.SemaphoreType.DMA((2, PLANE - 1)),
            pltpu.SemaphoreType.DMA((2, nd - 1)),
            pltpu.SemaphoreType.DMA((2, PLANE - 1)),
        ],
        compiler_params=pltpu.CompilerParams(collective_id=number, has_side_effects=True),
        cost_estimate=SHORT,
        name=f"sum_everywhere_{number}",
    )(padded, blocks)
    return summed.reshape(-1)[: count - 1], norm, grad_qkv, grad_out


def greet_line(nd, others):
    line = lax.axis_index("dp")
    barrier = pltpu.get_barrier_semaphore()
    for other in others:
        pl.semaphore_signal(barrier, inc=1, device_id={"fsdp": other}, device_id_type=MESH)

    @pl.when(line < nd - 1)
    def _():
        pl.semaphore_signal(barrier, inc=1, device_id={"dp": line + 1}, device_id_type=MESH)

    @pl.when(line > 0)
    def _():
        pl.semaphore_signal(barrier, inc=1, device_id={"dp": line - 1}, device_id_type=MESH)

    neighbours = lax.div(line + nd - 1, nd) + lax.div(2 * nd - 2 - line, nd)
    pl.semaphore_wait(barrier, len(others) + neighbours)


class Gather:
    def __init__(self, own_ref, all_ref, send_sem, recv_sem):
        self.own_ref, self.all_ref = own_ref, all_ref
        self.send_sem, self.recv_sem = send_sem, recv_sem
        self.me = lax.axis_index("fsdp")
        self.sibling, self.x_next, self.y_next = flip(self.me, 0), flip(self.me, 1), flip(self.me, 2)
        self.diagonal = flip(self.x_next, 2)
        self.rows = own_ref.shape[0]
        self.sent = []

    def put(self, slot, owner, part, target, own=False):
        half = self.rows // 2
        if part is None:
            spot = self.all_ref.at[pl.ds(pl.multiple_of(owner * self.rows, half), self.rows)]
            source = self.own_ref
        else:
            first = pl.multiple_of(owner * self.rows + part * half, half)
            spot = self.all_ref.at[pl.ds(first, half)]
            source = self.own_ref.at[pl.ds(part * half, half)]
        return pltpu.make_async_remote_copy(
            src_ref=source if own else spot,
            dst_ref=spot,
            send_sem=self.send_sem.at[slot],
            recv_sem=self.recv_sem.at[slot],
            device_id={"fsdp": target},
            device_id_type=MESH,
        )

    def begin(self):
        for slot, part, target in (
            (0, 0, self.x_next),
            (2, 1, self.y_next),
            (4, None, self.sibling),
            (1, 1, self.x_next),
            (3, 0, self.y_next),
        ):
            copy = self.put(slot, self.me, part, target, own=True)
            copy.start()
            self.sent.append(copy)

    def take(self, slot):
        sibling = self.sibling
        owner, part, onward = {
            0: (self.x_next, 0, ((5, self.y_next), (7, sibling))),
            1: (self.x_next, 1, ((8, sibling),)),
            2: (self.y_next, 1, ((6, self.x_next), (9, sibling))),
            3: (self.y_next, 0, ((10, sibling),)),
            4: (sibling, None, ()),
            5: (self.diagonal, 0, ((11, sibling),)),
            6: (self.diagonal, 1, ((12, sibling),)),
            7: (flip(self.x_next, 0), 0, ()),
            8: (flip(self.x_next, 0), 1, ()),
            9: (flip(self.y_next, 0), 1, ()),
            10: (flip(self.y_next, 0), 0, ()),
            11: (flip(self.diagonal, 0), 0, ()),
            12: (flip(self.diagonal, 0), 1, ()),
        }[slot]
        self.put(slot, owner, part, sibling).wait_recv()
        for next_slot, target in onward:
            copy = self.put(next_slot, owner, part, target)
            copy.start()
            self.sent.append(copy)

    def finish(self):
        for copy in self.sent:
            copy.wait_send()


def gather_scratch():
    return [pltpu.SemaphoreType.DMA((13,)), pltpu.SemaphoreType.DMA((13,))]


class Scatter:
    def __init__(self, out_ref, block, refs):
        self.out_ref, self.block = out_ref, block
        (self.sib_out, self.sib_in, self.far_out, self.far_in, self.near_out, self.near_in) = refs[:6]
        self.late = refs[6]
        self.sib_sems, self.far_sems, self.near_sems = refs[7:9], refs[9:11], refs[11:13]
        self.me = lax.axis_index("fsdp")
        self.sibling, self.x_next, self.y_next = flip(self.me, 0), flip(self.me, 1), flip(self.me, 2)
        self.targets = (flip(self.x_next, 2), self.x_next, self.y_next, self.me)
        self.half = out_ref.shape[0] // 2

    def send(self, source, target, sems, slot, device):
        return pltpu.make_async_remote_copy(
            src_ref=source.at[slot],
            dst_ref=target.at[slot],
            send_sem=sems[0].at[slot],
            recv_sem=sems[1].at[slot],
            device_id={"fsdp": device},
            device_id_type=MESH,
        )

    def to_sibling(self, place):
        return self.send(self.sib_out, self.sib_in, self.sib_sems, place, self.sibling)

    def to_far(self, part):
        device = (self.x_next, self.y_next)[part]
        return self.send(self.far_out, self.far_in, self.far_sems, part, device)

    def to_near(self, place, part):
        device = (self.x_next, self.y_next)[place]
        return self.send(self.near_out, self.near_in, self.near_sems, 2 * place + part, device)

    def for_sibling(self, place):
        def write(columns, part):
            self.sib_out[place, :, columns] = part.astype(jnp.bfloat16)

        self.block(flip(self.targets[place], 0), write)
        self.to_sibling(place).start()

    def for_far(self):
        self.to_sibling(0).wait_recv()

        def write(columns, part):
            whole = (part + self.sib_in[0, :, columns].astype(jnp.float32)).astype(jnp.bfloat16)
            self.far_out[0, :, columns] = whole[: self.half]
            self.far_out[1, :, columns] = whole[self.half :]

        self.block(self.targets[0], write)
        self.to_far(0).start()
        self.to_far(1).start()

    def for_near(self, place):
        self.to_sibling(1 + place).wait_recv()
        other = 1 - place

        def write(columns, part):
            whole = part + self.sib_in[1 + place, :, columns].astype(jnp.float32)
            halves = (whole[: self.half], whole[self.half :])
            self.near_out[2 * place + place, :, columns] = halves[place].astype(jnp.bfloat16)
            self.late[place, :, columns] = halves[other]

        self.block(self.targets[1 + place], write)
        self.to_near(place, place).start()

    def finish_near(self, place):
        other = 1 - place
        self.to_far(other).wait_recv()
        whole = self.late[place] + self.far_in[other].astype(jnp.float32)
        self.near_out[2 * place + other] = whole.astype(jnp.bfloat16)
        self.to_near(place, other).start()

    def own(self):
        def write(columns, part):
            self.out_ref[:, columns] = part

        self.block(self.me, write)

    def finish(self):
        self.to_sibling(3).wait_recv()
        self.out_ref[...] = self.out_ref[...] + self.sib_in[3].astype(jnp.float32)
        for part, place in ((0, 0), (1, 1), (1, 0), (0, 1)):
            self.to_near(place, part).wait_recv()
            spot = pl.ds(part * self.half, self.half)
            part_in = self.near_in[2 * place + part].astype(jnp.float32)
            self.out_ref[spot, :] = self.out_ref[spot, :] + part_in
        for place in range(4):
            self.to_sibling(place).wait_send()
            self.to_near(place // 2, place % 2).wait_send()
        for part in range(2):
            self.to_far(part).wait_send()


def staged(kernel, n_in, places):
    def body(*refs):
        stage, sems = refs[-len(places) - 1 : -1], refs[-1]
        inputs, rest = list(refs[:n_in]), refs[n_in : -len(places) - 1]
        copies = [
            pltpu.make_async_copy(inputs[place], buffer, sems.at[index])
            for index, (place, buffer) in enumerate(zip(places, stage))
        ]
        for copy in copies:
            copy.start()
        for place, buffer in zip(places, stage):
            inputs[place] = buffer

        def ready():
            for copy in copies:
                copy.wait()

        kernel(ready, *inputs, *rest)

    return body


def staged_specs(arrays, places):
    specs = [ANY if place in places else VMEM for place in range(len(arrays))]
    scratch = [pltpu.VMEM(arrays[place].shape, arrays[place].dtype) for place in places]
    return specs, scratch + [pltpu.SemaphoreType.DMA((len(places),))]


def scatter_scratch(rows, width):
    low, half = jnp.bfloat16, rows // 2
    return [
        pltpu.VMEM((4, rows, width), low),
        pltpu.VMEM((4, rows, width), low),
        pltpu.VMEM((2, half, width), low),
        pltpu.VMEM((2, half, width), low),
        pltpu.VMEM((4, half, width), low),
        pltpu.VMEM((4, half, width), low),
        pltpu.VMEM((2, half, width), jnp.float32),
        pltpu.SemaphoreType.DMA((4,)),
        pltpu.SemaphoreType.DMA((4,)),
        pltpu.SemaphoreType.DMA((2,)),
        pltpu.SemaphoreType.DMA((2,)),
        pltpu.SemaphoreType.DMA((4,)),
        pltpu.SemaphoreType.DMA((4,)),
    ]


def block_product(left_refs, right_refs, rows, width, turned):
    def block(owner, write):
        @pl.loop(0, width // TILE)
        def _(step):
            columns = pl.ds(pl.multiple_of(step * TILE, TILE), TILE)
            spot = pl.ds(pl.multiple_of(owner * rows, rows), rows)
            total = None
            for left_ref, right_ref in zip(left_refs, right_refs):
                if turned:
                    part = contract_last(left_ref[spot, :], right_ref[columns, :])
                else:
                    part = product(left_ref[spot, :], right_ref[:, columns])
                total = part if total is None else total + part
            write(columns, total)

    return block


def scatter_kernel(turned, count, *refs):
    left_hbm, right_hbm, out_ref = refs[:count], refs[count : 2 * count], refs[2 * count]
    refs = refs[2 * count + 1 :]
    left_refs, right_refs = refs[:count], refs[count : 2 * count]
    left_sems, right_sems, refs = refs[2 * count], refs[2 * count + 1], refs[2 * count + 2 :]
    rows, width = out_ref.shape
    whole = block_product(left_refs, right_refs, rows, width, turned)

    def fetch(place, owner):
        spot = pl.ds(pl.multiple_of(owner * rows, rows), rows)
        return pltpu.make_async_copy(
            left_hbm[place].at[spot], left_refs[place].at[spot], left_sems.at[place, owner]
        )

    def block(owner, write):
        for place in range(count):
            fetch(place, owner).wait()
        whole(owner, write)

    scatter = Scatter(out_ref, block, refs)
    rights = [
        pltpu.make_async_copy(right_hbm[place], right_refs[place], right_sems.at[place])
        for place in range(count)
    ]
    for copy in rights:
        copy.start()
    far, x_next, y_next, me = scatter.targets
    for owner in (
        flip(far, 0),
        flip(x_next, 0),
        far,
        flip(y_next, 0),
        x_next,
        flip(me, 0),
        y_next,
        me,
    ):
        for place in range(count):
            fetch(place, owner).start()
    greet((scatter.sibling, scatter.x_next, scatter.y_next))
    for copy in rights:
        copy.wait()
    scatter.for_sibling(0)
    scatter.for_sibling(1)
    scatter.for_far()
    scatter.for_sibling(2)
    scatter.for_near(0)
    scatter.for_sibling(3)
    scatter.for_near(1)
    scatter.finish_near(0)
    scatter.finish_near(1)
    scatter.own()
    scatter.finish()


def pass_through(ready, gather, scatter, work, between):
    me, sibling, x_next, y_next = gather.me, gather.sibling, gather.x_next, gather.y_next
    diagonal = gather.diagonal
    greet((sibling, x_next, y_next))
    gather.begin()
    gather.all_ref[pl.ds(pl.multiple_of(me * gather.rows, gather.rows), gather.rows), :] = (
        gather.own_ref[...]
    )
    ready()
    work((me,))
    gather.take(0)
    gather.take(2)
    gather.take(4)
    work((sibling,))
    scatter.for_sibling(3)
    gather.take(1)
    gather.take(3)
    work((x_next, y_next))
    gather.take(5)
    gather.take(6)
    for slot in (7, 8, 9, 10):
        gather.take(slot)
    work((flip(x_next, 0), flip(y_next, 0)))
    scatter.for_sibling(1)
    scatter.for_sibling(2)
    scatter.for_near(0)
    scatter.for_near(1)
    gather.take(11)
    gather.take(12)
    work((flip(diagonal, 0),))
    scatter.for_sibling(0)
    work((diagonal,))
    scatter.for_far()
    scatter.own()
    between[0]()
    scatter.finish_near(0)
    scatter.finish_near(1)
    between[1]()
    scatter.finish()
    gather.finish()


def each_owner(owners, rows, one):
    if len(owners) == 1:
        one(owners[0])
        return

    @pl.loop(0, len(owners))
    def _(step):
        one(owners[0] + step * (owners[1] - owners[0]))


def lanes():
    lane = lax.broadcasted_iota(jnp.int32, (1, 2 * HD), 1)
    row_head = lax.broadcasted_iota(jnp.int32, (2 * HD, 2 * HD), 0) // HD
    column_head = lax.broadcasted_iota(jnp.int32, (2 * HD, 2 * HD), 1) // HD
    spread = jnp.where(row_head == column_head, 1.0 / HD, 0.0).astype(jnp.float32)

    def head_mean(values):
        return jnp.dot(
            values, spread, precision=lax.Precision.HIGHEST, preferred_element_type=jnp.float32
        )

    first_half = lax.rem(lane, HD) < HD // 2

    def turn_quarter(values):
        return jnp.where(
            first_half,
            -pltpu.roll(values, 2 * HD - HD // 2, 1),
            pltpu.roll(values, HD // 2, 1),
        )

    def sides(values):
        return [
            jnp.where(chosen, values, 0.0).astype(jnp.bfloat16)
            for chosen in (lane < HD, lane >= HD)
        ]

    return lane, sides, head_mean, turn_quarter


def twice(values):
    return jnp.concatenate([values, values], axis=0)


def stacked(ref, spot):
    width = 2 * HD
    return jnp.concatenate([ref[spot, :width], ref[spot, width : 2 * width]], axis=0)


def attend_kernel(
    ready,
    x_ref,
    wqkv_ref,
    wo_ref,
    cos_ref,
    sin_ref,
    mask_ref,
    gain_ref,
    out_ref,
    all_out_ref,
    proj_ref,
    q_ref,
    kk_ref,
    vv_ref,
    o_ref,
    lse_ref,
    all_ref,
    out_sem,
    gather_send,
    gather_recv,
    *refs,
):
    rows, width = out_ref.shape
    low = jnp.bfloat16
    pair_width = 2 * HD
    lane, sides, head_mean, turn_quarter = lanes()
    first_head = lane < HD
    scale = HD ** (-0.5)

    def normed(values, gain):
        return values * lax.rsqrt(head_mean(values * values) + EPSILON) * gain

    def one(owner):
        base = pl.multiple_of(owner * rows, rows)
        spot = pl.ds(base, rows)
        proj_ref[spot, :] = product(all_ref[spot, :], wqkv_ref[...])

        for part in range(MB):
            micro(pl.multiple_of(base + part * MB_TOK, MB_TOK), owner * MB + part)

    def micro(first, number):
        spot = pl.ds(first, MB_TOK)
        cosine, sine = cos_ref[spot, :], sin_ref[spot, :]
        allowed = twice(mask_ref[number]) > 0.5
        kv = proj_ref[spot, 2 * pair_width : 3 * pair_width]
        swapped = pltpu.roll(kv, HD, 1)
        values = jnp.where(first_head, swapped, kv)
        keys = normed(jnp.where(first_head, kv, swapped), gain_ref[1:2, :])
        keys = (keys * cosine + turn_quarter(keys) * sine).astype(low)
        kk_ref[spot, :] = keys
        vv_ref[spot, :] = values.astype(low)
        query = normed(stacked(proj_ref, spot), gain_ref[0:1, :])
        query = (query * twice(cosine) + turn_quarter(query) * twice(sine)).astype(low)
        q_ref[spot, :pair_width] = query[:MB_TOK]
        q_ref[spot, pair_width : 2 * pair_width] = query[MB_TOK:]
        probs, logs = [], []
        for one_query in sides(query.astype(jnp.float32) * scale):
            scores = jnp.where(allowed, contract_last(one_query, keys), MASKED)
            peak = jnp.max(scores, axis=-1, keepdims=True)
            powers = jnp.exp(scores - peak)
            total = jnp.sum(powers, axis=-1, keepdims=True)
            probs.append((powers * (1.0 / total)).astype(low))
            logs.append(peak + jnp.log(total))
        wide_values = jnp.concatenate(sides(values), axis=0)
        attended = product(jnp.concatenate(probs, axis=1), wide_values).astype(low)
        o_ref[spot, :pair_width] = attended[:MB_TOK]
        o_ref[spot, pair_width : 2 * pair_width] = attended[MB_TOK:]
        log_totals = jnp.where(lane == 0, logs[0][:MB_TOK], logs[1][:MB_TOK])
        log_totals = jnp.where(lane == 2, logs[0][MB_TOK:], log_totals)
        lse_ref[spot, :] = jnp.where(lane == 3, logs[1][MB_TOK:], log_totals)

    gather = Gather(x_ref, all_ref, gather_send, gather_recv)
    scatter = Scatter(out_ref, block_product((o_ref,), (wo_ref,), rows, width, False), refs)
    keep = pltpu.make_async_copy(all_ref, all_out_ref, out_sem)
    pass_through(
        ready,
        gather,
        scatter,
        lambda owners: each_owner(owners, rows, one),
        (keep.start, lambda: None),
    )
    keep.wait()


def attend_back_kernel(
    ready,
    x_ref,
    wqkv_ref,
    wo_ref,
    cos_ref,
    sin_ref,
    mask_ref,
    gain_ref,
    proj_ref,
    q_ref,
    kk_ref,
    vv_ref,
    o_ref,
    lse_ref,
    normed_hbm,
    out_ref,
    grad_ref,
    ggain_ref,
    all_ref,
    normed_ref,
    do_ref,
    dproj_ref,
    in_sem,
    gather_send,
    gather_recv,
    *refs,
):
    rows, width = out_ref.shape
    low = jnp.bfloat16
    pair_width = 2 * HD
    lane, sides, head_mean, turn_quarter = lanes()
    first_head = lane < HD
    scale = HD ** (-0.5)
    fetch = pltpu.make_async_copy(normed_hbm, normed_ref, in_sem)
    fetch.start()
    ggain_ref[...] = jnp.zeros_like(ggain_ref)

    def through_norm(grad, cosine, sine, raw, gain, row):
        grad = grad * cosine - turn_quarter(grad) * sine
        root = lax.rsqrt(head_mean(raw * raw) + EPSILON)
        normed = raw * root
        ggain_ref[row : row + 1, :] += jnp.sum(grad * normed, axis=0, keepdims=True)
        scaled = grad * gain
        return root * (scaled - normed * head_mean(scaled * normed))

    def one(owner):
        base = pl.multiple_of(owner * rows, rows)
        do_ref[...] = contract_last(all_ref[pl.ds(base, rows), :], wo_ref[...]).astype(low)

        for part in range(MB):
            here = pl.ds(part * MB_TOK, MB_TOK)
            micro(pl.multiple_of(base + part * MB_TOK, MB_TOK), here, owner * MB + part)

    def micro(first, here, number):
        spot = pl.ds(first, MB_TOK)
        cosine, sine = cos_ref[spot, :], sin_ref[spot, :]
        allowed = twice(mask_ref[number]) > 0.5
        keys, values = kk_ref[spot, :], vv_ref[spot, :]
        logs = lse_ref[spot, :]
        queries = sides(stacked(q_ref, spot).astype(jnp.float32) * scale)
        branches = sides(stacked(do_ref, here).astype(jnp.float32))
        probs_low, scores_back = [], []
        for side in range(2):
            log_total = jnp.concatenate(
                [logs[:, side : side + 1], logs[:, 2 + side : 3 + side]], axis=0
            )
            scores = jnp.where(allowed, contract_last(queries[side], keys), MASKED)
            probs = jnp.exp(scores - log_total)
            probs_grad = contract_last(branches[side], values)
            spread = jnp.sum(probs * probs_grad, axis=-1, keepdims=True)
            scores_back.append((probs * (probs_grad - spread)).astype(low))
            probs_low.append(probs.astype(low))
        wide_keys = jnp.concatenate(sides(keys.astype(jnp.float32)), axis=0)
        query_grad = product(jnp.concatenate(scores_back, axis=1), wide_keys) * scale
        key_grad = column_product(
            jnp.concatenate(scores_back, axis=0), jnp.concatenate(queries, axis=0)
        )
        value_grad = column_product(
            jnp.concatenate(probs_low, axis=0), jnp.concatenate(branches, axis=0)
        )
        raw = stacked(proj_ref, spot)
        grad = through_norm(query_grad, twice(cosine), twice(sine), raw, gain_ref[0:1, :], 0)
        dproj_ref[spot, :pair_width] = grad[:MB_TOK].astype(low)
        dproj_ref[spot, pair_width : 2 * pair_width] = grad[MB_TOK:].astype(low)
        kv = proj_ref[spot, 2 * pair_width : 3 * pair_width]
        raw = jnp.where(first_head, kv, pltpu.roll(kv, HD, 1))
        key_grad = key_grad + pltpu.roll(key_grad, HD, 1)
        value_grad = value_grad + pltpu.roll(value_grad, HD, 1)
        grad = through_norm(key_grad, cosine, sine, raw, gain_ref[1:2, :], 1)
        both = jnp.where(first_head, grad, value_grad).astype(low)
        dproj_ref[spot, 2 * pair_width : 3 * pair_width] = both

    wide, q_width = dproj_ref.shape[1], o_ref.shape[1]

    def out_grad():
        @pl.loop(0, width // TILE)
        def _(step):
            columns = pl.ds(pl.multiple_of(step * TILE, TILE), TILE)
            part = column_product(o_ref[...], all_ref[:, columns]).astype(low)
            for first in range(0, TILE, q_width):
                spot = pl.ds(pl.multiple_of(step * TILE + first, q_width), q_width)
                grad_ref[spot, wide:] = part[:, first : first + q_width]

    def qkv_grad():
        fetch.wait()

        @pl.loop(0, width // TILE)
        def _(step):
            columns = pl.ds(pl.multiple_of(step * TILE, TILE), TILE)
            part = column_product(dproj_ref[...], normed_ref[:, columns])
            grad_ref[columns, :wide] = jnp.transpose(part).astype(low)

    gather = Gather(x_ref, all_ref, gather_send, gather_recv)
    scatter = Scatter(out_ref, block_product((dproj_ref,), (wqkv_ref,), rows, width, True), refs)
    pass_through(
        ready, gather, scatter, lambda owners: each_owner(owners, rows, one), (out_grad, qkv_grad)
    )


def attend(own_rows, own_qkv, own_out, tables, number):
    rows, width = own_rows.shape
    count, wide, q_width = PLANE * rows, own_qkv.shape[1], own_out.shape[0]
    low = jnp.bfloat16
    arrays = (own_rows, own_qkv, own_out, *tables)
    places = tuple(range(1, len(arrays)))
    specs, stage = staged_specs(arrays, places)
    return pl.pallas_call(
        staged(attend_kernel, len(arrays), places),
        out_shape=[
            jax.ShapeDtypeStruct((rows, width), jnp.float32),
            jax.ShapeDtypeStruct((count, width), low),
            jax.ShapeDtypeStruct((count, wide), jnp.float32),
            jax.ShapeDtypeStruct((count, q_width), low),
            jax.ShapeDtypeStruct((count, 2 * HD), low),
            jax.ShapeDtypeStruct((count, 2 * HD), low),
            jax.ShapeDtypeStruct((count, q_width), low),
            jax.ShapeDtypeStruct((count, 2 * HD), jnp.float32),
        ],
        in_specs=specs,
        out_specs=[VMEM, ANY] + [VMEM] * 6,
        scratch_shapes=[pltpu.VMEM((count, width), low), pltpu.SemaphoreType.DMA]
        + gather_scratch()
        + scatter_scratch(rows, width)
        + stage,
        compiler_params=pltpu.CompilerParams(
            collective_id=number, has_side_effects=True, vmem_limit_bytes=56 * 2**20
        ),
        cost_estimate=SHORT,
        name=f"attend_{number}",
    )(*arrays)


def attend_back(own_rows, own_qkv, own_out, tables, kept, number):
    rows, width = own_rows.shape
    count, wide, q_width = PLANE * rows, own_qkv.shape[1], own_out.shape[0]
    low = jnp.bfloat16
    normed_all, proj, query, keys, values, attended, log_totals = kept
    arrays = (
        own_rows,
        own_qkv,
        own_out,
        *tables,
        proj,
        query,
        keys,
        values,
        attended,
        log_totals,
        normed_all,
    )
    places = tuple(range(1, len(arrays) - 1))
    specs, stage = staged_specs(arrays[:-1], places)
    return pl.pallas_call(
        staged(attend_back_kernel, len(arrays), places),
        out_shape=[
            jax.ShapeDtypeStruct((rows, width), jnp.float32),
            jax.ShapeDtypeStruct((width, wide + q_width), low),
            jax.ShapeDtypeStruct((8, 2 * HD), jnp.float32),
        ],
        in_specs=specs + [ANY],
        out_specs=[VMEM] * 3,
        scratch_shapes=[
            pltpu.VMEM((count, width), low),
            pltpu.VMEM((count, width), low),
            pltpu.VMEM((rows, q_width), low),
            pltpu.VMEM((count, wide), low),
            pltpu.SemaphoreType.DMA,
        ]
        + gather_scratch()
        + scatter_scratch(rows, width)
        + stage,
        compiler_params=pltpu.CompilerParams(
            collective_id=number, has_side_effects=True, vmem_limit_bytes=58 * 2**20
        ),
        cost_estimate=SHORT,
        name=f"attend_back_{number}",
    )(*arrays)


def product_scatter(left_sides, right_sides, number, turned=False):
    width = right_sides[0].shape[0] if turned else right_sides[0].shape[1]
    rows = left_sides[0].shape[0] // PLANE
    return pl.pallas_call(
        functools.partial(scatter_kernel, turned, len(left_sides)),
        out_shape=jax.ShapeDtypeStruct((rows, width), jnp.float32),
        in_specs=[ANY] * (2 * len(left_sides)),
        out_specs=VMEM,
        scratch_shapes=[pltpu.VMEM(side.shape, side.dtype) for side in left_sides + right_sides]
        + [
            pltpu.SemaphoreType.DMA((len(left_sides), PLANE)),
            pltpu.SemaphoreType.DMA((len(left_sides),)),
        ]
        + scatter_scratch(rows, width),
        compiler_params=pltpu.CompilerParams(
            collective_id=number, has_side_effects=True, vmem_limit_bytes=56 * 2**20
        ),
        cost_estimate=SHORT,
        name=f"product_scatter_{number}",
    )(*left_sides, *right_sides)


def start_kernel(
    nd,
    qkv_ref,
    out_rows_ref,
    wide_ref,
    df_ref,
    note_ref,
    own_qkv_ref,
    own_out_ref,
    half_a_ref,
    half_b_ref,
    df_all_ref,
    notes_ref,
    own_sem,
    gather_send,
    gather_recv,
    block_send,
    block_recv,
    note_send,
    note_recv,
    piece_send,
    piece_recv,
    line_send,
    line_recv,
):
    me, line = lax.axis_index("fsdp"), lax.axis_index("dp")
    others = plane_others(me)
    count = qkv_ref.shape[1]
    half_width = half_a_ref.shape[2] // 2
    hidden = 2 * half_width
    whole = hidden * PLANE
    gather = Gather(df_ref, df_all_ref, gather_send, gather_recv)
    greet_line(nd, others)

    def line_spot(array, owner):
        rows = pl.ds(pl.multiple_of(owner * count, count), count)
        return own_qkv_ref.at[:, rows] if array == 0 else own_out_ref.at[rows]

    def along(array, owner, side, source=None):
        spot = line_spot(array, owner)
        return pltpu.make_async_remote_copy(
            src_ref=spot if source is None else source,
            dst_ref=spot,
            send_sem=line_send.at[array, side, owner],
            recv_sem=line_recv.at[array, owner],
            device_id={"dp": line + 1 if side == 0 else line - 1},
            device_id_type=MESH,
        )

    def send_own(array, source=None):
        @pl.when(line < nd - 1)
        def _():
            along(array, line, 0, source).start()

        @pl.when(line > 0)
        def _():
            along(array, line, 1, source).start()

    def line_step(array, step):
        @pl.when(line >= step)
        def _():
            along(array, line - step, 0).wait_recv()

            @pl.when(line < nd - 1)
            def _():
                along(array, line - step, 0).start()

        @pl.when(line + step < nd)
        def _():
            along(array, line + step, 1).wait_recv()

            @pl.when(line > 0)
            def _():
                along(array, line + step, 1).start()

    def put_block(number):
        other = others[number - 1]
        return pltpu.make_async_remote_copy(
            src_ref=qkv_ref.at[other],
            dst_ref=own_qkv_ref.at[me, pl.ds(pl.multiple_of(line * count, count), count)],
            send_sem=block_send.at[number],
            recv_sem=block_recv.at[number],
            device_id={"fsdp": other},
            device_id_type=MESH,
        )

    def put_note(number):
        return pltpu.make_async_remote_copy(
            src_ref=note_ref,
            dst_ref=notes_ref.at[me],
            send_sem=note_send.at[number],
            recv_sem=note_recv.at[number],
            device_id={"fsdp": others[number - 1]},
            device_id_type=MESH,
        )

    def pieces(other):
        for half, half_ref in enumerate((half_a_ref, half_b_ref)):
            for side in range(2):
                first = side * whole + other * hidden + half * half_width
                source = wide_ref.at[:, pl.ds(pl.multiple_of(first, 128), half_width)]
                yield source, half_ref.at[me, :, pl.ds(side * half_width, half_width)]

    def put_pieces(number):
        return [
            pltpu.make_async_remote_copy(
                src_ref=source,
                dst_ref=target,
                send_sem=piece_send.at[4 * number + index],
                recv_sem=piece_recv.at[4 * number + index],
                device_id={"fsdp": others[number - 1]},
                device_id_type=MESH,
            )
            for index, (source, target) in enumerate(pieces(others[number - 1]))
        ]

    own_block = own_qkv_ref.at[me, pl.ds(pl.multiple_of(line * count, count), count)]
    rows = df_ref.shape[0]
    kept = [
        (qkv_ref.at[me], own_block),
        (out_rows_ref, line_spot(1, line)),
        (note_ref, notes_ref.at[me]),
        (df_ref, df_all_ref.at[pl.ds(pl.multiple_of(me * rows, rows), rows)]),
    ] + list(pieces(me))
    keep = [
        pltpu.make_async_copy(source, target, own_sem.at[index])
        for index, (source, target) in enumerate(kept)
    ]
    order = (6, 7, 2, 4, 3, 5, 1)
    for number in order:
        put_block(number).start()
        put_note(number).start()
    keep[0].start()
    send_own(1, out_rows_ref)
    gather.begin()
    for copy in keep[1:]:
        copy.start()
    for number in order:
        put_block(number).wait_recv()
    keep[0].wait()
    send_own(0)
    for steps, slots in (
        ((), (0, 2)),
        (((1, 1),), (4, 1, 3)),
        (((0, 1),), (5, 6)),
        (((1, 2),), ()),
        (((0, 2),), (7, 9, 8, 10)),
        (((1, 3), (0, 3)), (11, 12)),
    ):
        for array, step in steps:
            if step < nd:
                line_step(array, step)
        for slot in slots:
            gather.take(slot)
        if slots == (5, 6):
            for number in order:
                for copy in put_pieces(number):
                    copy.start()
    for step in range(4, nd):
        line_step(1, step)
        line_step(0, step)
    for number in order:
        put_block(number).wait_send()
        put_note(number).wait()
        for copy in put_pieces(number):
            copy.wait()
    gather.finish()
    for copy in keep[1:]:
        copy.wait()
    for array in (1, 0):
        source = out_rows_ref if array == 1 else None

        @pl.when(line < nd - 1)
        def _():
            along(array, line, 0, source).wait_send()

        @pl.when(line > 0)
        def _():
            along(array, line, 1, source).wait_send()

        for step in range(1, nd):

            @pl.when(jnp.logical_and(line >= step, line < nd - 1))
            def _():
                along(array, line - step, 0).wait_send()

            @pl.when(jnp.logical_and(line + step < nd, line > 0))
            def _():
                along(array, line + step, 1).wait_send()


def start(qkv_blocks, out_rows, wide_rows, df_own, note, number):
    nd = lax.axis_size("dp")
    count, whole = wide_rows.shape
    half = whole // 4 // PLANE
    low = wide_rows.dtype
    return pl.pallas_call(
        functools.partial(start_kernel, nd),
        out_shape=[
            jax.ShapeDtypeStruct((PLANE, nd * count, qkv_blocks.shape[2]), low),
            jax.ShapeDtypeStruct((nd * count, out_rows.shape[1]), low),
            jax.ShapeDtypeStruct((PLANE, count, 2 * half), low),
            jax.ShapeDtypeStruct((PLANE, count, 2 * half), low),
            jax.ShapeDtypeStruct((PLANE * df_own.shape[0], df_own.shape[1]), low),
            jax.ShapeDtypeStruct((PLANE,) + note.shape, note.dtype),
        ],
        in_specs=[ANY] * 5,
        out_specs=[ANY] * 6,
        scratch_shapes=[pltpu.SemaphoreType.DMA((8,))]
        + gather_scratch()
        + [pltpu.SemaphoreType.DMA((PLANE,))] * 4
        + [pltpu.SemaphoreType.DMA((4 * PLANE,))] * 2
        + [pltpu.SemaphoreType.DMA((2, 2, nd)), pltpu.SemaphoreType.DMA((2, nd))],
        compiler_params=pltpu.CompilerParams(collective_id=number, has_side_effects=True),
        cost_estimate=SHORT,
        name=f"start_{number}",
    )(qkv_blocks, out_rows, wide_rows, df_own, note)


def glu_block(
    rows_ref, df_ref, wgu, wd, act_ref, dgu_ref, down_sum, wide_sum, results=None
):
    half = wd.shape[0]
    count, width = rows_ref.shape

    @pl.loop(0, count // 256)
    def _(step):
        spot = pl.ds(pl.multiple_of(step * 256, 256), 256)
        for first in range(0, half, GLU_TILE):
            units = slice(first, first + GLU_TILE)
            up_units = slice(half + first, half + first + GLU_TILE)
            gate = product(rows_ref[spot, :], wgu[:, units])
            up = product(rows_ref[spot, :], wgu[:, up_units])
            back = contract_last(df_ref[spot, :], wd[units, :])
            sigmoid = jax.nn.sigmoid(gate)
            silu = gate * sigmoid
            act_ref[spot, units] = (silu * up).astype(jnp.bfloat16)
            gate_back = back * up * sigmoid * (1.0 + gate * (1.0 - sigmoid))
            dgu_ref[spot, units] = gate_back.astype(jnp.bfloat16)
            dgu_ref[spot, up_units] = (back * silu).astype(jnp.bfloat16)

    @pl.loop(0, width // TILE)
    def _(step):
        columns = pl.ds(pl.multiple_of(step * TILE, TILE), TILE)
        down = column_product(act_ref[...], df_ref[:, columns])
        wide = column_product(rows_ref[:, columns], dgu_ref[...])
        if results is None:
            down_sum[:, columns] += down
            wide_sum[columns, :] += wide
        else:
            down_ref, wide_ref = results
            down_ref[:, columns] = (down_sum[:, columns] + down).astype(down_ref.dtype)
            wide_ref[columns, :] = (wide_sum[columns, :] + wide).astype(wide_ref.dtype)


def gather_glu_kernel(
    x_ref,
    wgu_hbm,
    wd_hbm,
    df_hbm,
    all_out_ref,
    act_ref,
    dgu_ref,
    down_ref,
    wide_ref,
    all_ref,
    wgu_ref,
    wd_ref,
    df_ref,
    down_sum,
    wide_sum,
    in_sem,
    out_sem,
    gather_send,
    gather_recv,
):
    rows = x_ref.shape[0]
    half = wd_ref.shape[0]
    fetch = [
        pltpu.make_async_copy(wgu_hbm, wgu_ref, in_sem.at[0]),
        pltpu.make_async_copy(wd_hbm.at[pl.ds(0, half)], wd_ref, in_sem.at[1]),
        pltpu.make_async_copy(df_hbm, df_ref, in_sem.at[2]),
    ]
    for copy in fetch:
        copy.start()
    gather = Gather(x_ref, all_ref, gather_send, gather_recv)
    me, x_next, y_next = gather.me, gather.x_next, gather.y_next
    greet((gather.sibling, x_next, y_next))
    gather.begin()
    all_ref[pl.ds(pl.multiple_of(me * rows, rows), rows), :] = x_ref[...]
    down_sum[...] = jnp.zeros_like(down_sum)
    wide_sum[...] = jnp.zeros_like(wide_sum)
    for copy in fetch:
        copy.wait()

    def work(owner, results=None):
        first = owner - lax.rem(owner, 2)
        spot = pl.ds(pl.multiple_of(first * rows, 2 * rows), 2 * rows)
        glu_block(
            all_ref.at[spot],
            df_ref.at[spot],
            wgu_ref,
            wd_ref,
            act_ref.at[spot],
            dgu_ref.at[spot],
            down_sum,
            wide_sum,
            results,
        )

    gather.take(4)
    work(me)
    for slot in (0, 2, 1, 3, 7, 8):
        gather.take(slot)
    work(x_next)
    for slot in (5, 6, 9, 10):
        gather.take(slot)
    work(y_next)
    gather.take(11)
    gather.take(12)
    keep = pltpu.make_async_copy(all_ref, all_out_ref, out_sem)
    keep.start()
    work(gather.diagonal, (down_ref, wide_ref))
    gather.finish()
    keep.wait()


def gather_glu(own_rows, wgu, own_down, df_all, number):
    rows, width = own_rows.shape
    count, half = PLANE * rows, wgu.shape[1] // 2
    low = jnp.bfloat16
    return pl.pallas_call(
        gather_glu_kernel,
        out_shape=[
            jax.ShapeDtypeStruct((count, width), low),
            jax.ShapeDtypeStruct((count, half), low),
            jax.ShapeDtypeStruct((count, 2 * half), low),
            jax.ShapeDtypeStruct((half, width), low),
            jax.ShapeDtypeStruct((width, 2 * half), low),
        ],
        in_specs=[VMEM, ANY, ANY, ANY],
        out_specs=[ANY] + [VMEM] * 4,
        scratch_shapes=[
            pltpu.VMEM((count, width), low),
            pltpu.VMEM(wgu.shape, low),
            pltpu.VMEM((half, width), low),
            pltpu.VMEM((count, width), low),
            pltpu.VMEM((half, width), jnp.float32),
            pltpu.VMEM((width, 2 * half), jnp.float32),
            pltpu.SemaphoreType.DMA((3,)),
            pltpu.SemaphoreType.DMA,
        ]
        + gather_scratch(),
        compiler_params=pltpu.CompilerParams(
            collective_id=number, has_side_effects=True, vmem_limit_bytes=58 * 2**20
        ),
        cost_estimate=SHORT,
        name=f"gather_glu_{number}",
    )(own_rows, wgu, own_down, df_all)


def glu_kernel(
    x_ref, df_ref, wgu_ref, wd_ref, first_ref, act_ref, dgu_ref, grad_ref, down_sum, wide_sum
):
    step = pl.program_id(0)
    half = wd_ref.shape[0]

    @pl.when(step == 0)
    def _():
        down_sum[...] = jnp.zeros_like(down_sum)
        wide_sum[...] = jnp.zeros_like(wide_sum)

    glu_block(
        x_ref, df_ref, wgu_ref, wd_ref, act_ref, dgu_ref, down_sum, wide_sum
    )

    @pl.when(step == pl.num_programs(0) - 1)
    def _():
        nd, _, both = grad_ref.shape
        count, units = wide_sum.shape[0] // PLANE // nd, 2 * half // nd
        low = grad_ref.dtype
        for owner in range(nd):
            for place in range(PLANE):
                first = (place * nd + owner) * count
                part = wide_sum[first : first + count, :].astype(low)
                grad_ref[owner, place * count : (place + 1) * count, :] = part
            source, first = first_ref, owner * units
            if first >= half:
                source, first = down_sum, first - half
            for side in range(2):
                part = source[first : first + units, side * both : (side + 1) * both].astype(low)
                start = PLANE * count + side * units
                grad_ref[owner, start : start + units, :] = part


def glu(rows_all, df_all, wgu, own_down, down_first, number):
    nd = lax.axis_size("dp")
    count, width = rows_all.shape
    half = wgu.shape[1] // 2
    low = jnp.bfloat16
    step = 512
    once = pl.Buffered(1)
    return pl.pallas_call(
        glu_kernel,
        grid=(count // step,),
        out_shape=[
            jax.ShapeDtypeStruct((count, half), low),
            jax.ShapeDtypeStruct((count, 2 * half), low),
            jax.ShapeDtypeStruct((nd, 2 * width // nd, 2 * half), low),
        ],
        in_specs=[
            pl.BlockSpec((step, width), lambda i: (i, 0)),
            pl.BlockSpec((step, width), lambda i: (i, 0)),
            pl.BlockSpec((width, 2 * half), lambda i: (0, 0), pipeline_mode=once),
            pl.BlockSpec((half, width), lambda i: (1, 0), pipeline_mode=once),
            pl.BlockSpec((half, width), lambda i: (0, 0), pipeline_mode=once),
        ],
        out_specs=[
            pl.BlockSpec((step, half), lambda i: (i, 0)),
            pl.BlockSpec((step, 2 * half), lambda i: (i, 0)),
            pl.BlockSpec(
                (nd, 2 * width // nd, 2 * half), lambda i: (0, 0, 0), pipeline_mode=once
            ),
        ],
        scratch_shapes=[
            pltpu.VMEM((half, width), jnp.float32),
            pltpu.VMEM((width, 2 * half), jnp.float32),
        ],
        compiler_params=pltpu.CompilerParams(vmem_limit_bytes=56 * 2**20),
        cost_estimate=SHORT,
        name=f"glu_{number}",
    )(rows_all, df_all, wgu, own_down, down_first)


def attention(normed_low, own_qkv, own_out, lengths_all, query_gain, key_gain):
    position, _, allowed = layout(lengths_all)
    half_width = HD // 2
    frequency = ROPE_BASE ** (jnp.arange(half_width, dtype=jnp.float32) * (-2.0 / HD))
    angles = position.reshape(-1, 1) * frequency[None, :]
    tables = (
        jnp.tile(jnp.cos(angles), (1, 4)),
        jnp.tile(jnp.sin(angles), (1, 4)),
        allowed.astype(jnp.float32),
        jnp.pad(
            jnp.stack([jnp.tile(query_gain, 2), jnp.tile(key_gain, 2)]), ((0, 6), (0, 0))
        ),
    )
    sums, *kept = attend(normed_low, own_qkv, own_out, tables, 3)

    def back(branch_own):
        normed_one_grad, part_attn, gain_grads = attend_back(
            branch_own, own_qkv, own_out, tables, kept, 9
        )
        query_gain_grad = gain_grads[0, :HD] + gain_grads[0, HD:]
        return normed_one_grad, part_attn, query_gain_grad, gain_grads[1, :HD]

    return sums, back


def last_kernel(
    ready,
    hidden_ref,
    valid_ref,
    act_a_ref,
    act_b_ref,
    wd_ref,
    half_ref,
    out_ref,
    wide_ref,
    sum_ref,
    own_sem,
    sems,
    *refs,
):
    others = plane_others(lax.axis_index("fsdp"))
    rows, width = out_ref.shape
    half_rows = wd_ref.shape[0] // 2
    block = block_product(
        (act_a_ref, act_b_ref),
        (wd_ref.at[pl.ds(0, half_rows)], wd_ref.at[pl.ds(half_rows, half_rows)]),
        rows,
        width,
        False,
    )
    scatter = Scatter(sum_ref, block, refs)
    greet(others)
    order = (6, 7, 2, 4, 3, 5, 1)
    for number in order:
        for copy in put_half(half_ref, wide_ref, others, number, sems):
            copy.start()
    keep = keep_half(half_ref, wide_ref, own_sem)
    for copy in keep:
        copy.start()
    ready()
    scatter.for_sibling(0)
    scatter.for_sibling(1)
    scatter.for_far()
    scatter.for_sibling(2)
    scatter.for_near(0)
    scatter.for_sibling(3)
    scatter.for_near(1)
    scatter.finish_near(0)
    scatter.finish_near(1)
    scatter.own()
    scatter.finish()
    out_ref[...] = (hidden_ref[...] + valid_ref[...] * sum_ref[...]).astype(out_ref.dtype)
    for number in order:
        for copy in put_half(half_ref, wide_ref, others, number, sems):
            copy.wait()
    for copy in keep:
        copy.wait()


def last(hidden, valid_col, act_a, act_b, own_down, half, count, number):
    rows, width = hidden.shape
    arrays = (hidden, valid_col, act_a, act_b, own_down)
    places = (0, 2, 3, 4)
    specs, stage = staged_specs(arrays, places)
    return pl.pallas_call(
        staged(last_kernel, len(arrays) + 1, places),
        out_shape=[
            jax.ShapeDtypeStruct((rows, width), jnp.bfloat16),
            jax.ShapeDtypeStruct((count, half.shape[1] * PLANE), half.dtype),
        ],
        in_specs=specs + [ANY],
        out_specs=[VMEM, ANY],
        scratch_shapes=[pltpu.VMEM((rows, width), jnp.float32)]
        + half_scratch()
        + scatter_scratch(rows, width)
        + stage,
        compiler_params=pltpu.CompilerParams(
            collective_id=number, has_side_effects=True, vmem_limit_bytes=56 * 2**20
        ),
        cost_estimate=SHORT,
        name=f"last_{number}",
    )(*arrays, half)


def adam_kernel(chunks, n_grads, per, norm_ref, *refs):
    grads, refs = refs[:n_grads], refs[n_grads:]
    groups = [refs[place * per : (place + 1) * per] for place in range(6)]
    in_buf, grad_buf, out_buf, in_sems, out_sems = refs[6 * per :]
    depth = in_buf.shape[0]
    factor = norm_ref[1:2, 0:1]
    first_scale = 1.0 / (1.0 - FIRST_DECAY**STEP)
    second_scale = 1.0 / (1.0 - SECOND_DECAY**STEP)

    def fetch(number):
        which, rows, columns, pieces = chunks[number]
        slot, width = number % depth, columns.size
        copies = [
            pltpu.make_async_copy(
                groups[place][which].at[rows, columns],
                in_buf.at[slot, place, :, pl.ds(0, width)],
                in_sems.at[slot, place],
            )
            for place in range(3)
        ]
        for place, (array, source, first) in enumerate(pieces):
            target = grad_buf.at[slot, :, pl.ds(first, source[1].size)]
            copies.append(
                pltpu.make_async_copy(
                    grads[array].at[source], target, in_sems.at[slot, 3 + place]
                )
            )
        return copies

    def put(number):
        which, rows, columns, _ = chunks[number]
        slot, width = number % depth, columns.size
        return [
            pltpu.make_async_copy(
                out_buf.at[slot, place, :, pl.ds(0, width)],
                groups[3 + place][which].at[rows, columns],
                out_sems.at[slot, place],
            )
            for place in range(3)
        ]

    def update(slot, width):
        columns = slice(0, width)

        @pl.loop(0, in_buf.shape[2] // 16)
        def _(step):
            rows = pl.ds(pl.multiple_of(step * 16, 16), 16)
            clipped = grad_buf[slot, rows, columns].astype(jnp.float32) * factor
            weight = in_buf[slot, 0, rows, columns]
            first = FIRST_DECAY * in_buf[slot, 1, rows, columns] + (1.0 - FIRST_DECAY) * clipped
            second = SECOND_DECAY * in_buf[slot, 2, rows, columns]
            second = second + (1.0 - SECOND_DECAY) * clipped * clipped
            root = jnp.sqrt(second * second_scale) + ADAM_EPSILON
            change = first * first_scale / root + WEIGHT_DECAY * weight
            out_buf[slot, 0, rows, columns] = weight - LEARN_RATE * change
            out_buf[slot, 1, rows, columns] = first
            out_buf[slot, 2, rows, columns] = second

    for number in range(min(depth, len(chunks))):
        for copy in fetch(number):
            copy.start()
    for number in range(len(chunks)):
        for copy in fetch(number):
            copy.wait()
        if number >= depth:
            for copy in put(number - depth):
                copy.wait()
        update(number % depth, chunks[number][2].size)
        for copy in put(number):
            copy.start()
        if number + depth < len(chunks):
            for copy in fetch(number + depth):
                copy.start()
    for number in range(max(0, len(chunks) - depth), len(chunks)):
        for copy in put(number):
            copy.wait()


def adam_matrices(norm, grad_qkv, grad_out, grad_a, grad_b, sums_b, weights, firsts, seconds):
    rows, width, depth = 64, 2048, 6
    half = grad_a.shape[1] // 2 // PLANE
    count = weights[3].shape[0]
    behind = sums_b.shape[0] - 2 * count

    def pieces(which, row, column, size):
        here = pl.ds(row, rows)
        if which < 2:
            return [(which, (here, pl.ds(column, size)), 0)]
        if which == 3:
            return [
                (4, (pl.ds(behind + side * count + row, rows), pl.ds(0, width // 2)), side * width // 2)
                for side in range(2)
            ]
        first = column // 2
        return [
            (2 + part, (here, pl.ds(first + unit * half, half)), (2 * unit + part) * half)
            for unit in range(width // 2 // half)
            for part in range(2)
        ]

    chunks = []
    for which, weight in enumerate(weights):
        for row in range(0, weight.shape[0], rows):
            for column in range(0, weight.shape[1], width):
                size = min(width, weight.shape[1] - column)
                parts = pieces(which, row, column, size)
                chunks.append((which, pl.ds(row, rows), pl.ds(column, size), parts))
    grads = (grad_qkv, grad_out, grad_a, grad_b, sums_b)
    per = len(weights)
    outs = pl.pallas_call(
        functools.partial(adam_kernel, chunks, len(grads), per),
        out_shape=[jax.ShapeDtypeStruct(weight.shape, jnp.float32) for weight in weights] * 3,
        in_specs=[VMEM] + [ANY] * (len(grads) + 3 * per),
        out_specs=[ANY] * (3 * per),
        scratch_shapes=[
            pltpu.VMEM((depth, 3, rows, width), jnp.float32),
            pltpu.VMEM((depth, rows, width), jnp.bfloat16),
            pltpu.VMEM((depth, 3, rows, width), jnp.float32),
            pltpu.SemaphoreType.DMA((depth, 7)),
            pltpu.SemaphoreType.DMA((depth, 3)),
        ],
        compiler_params=pltpu.CompilerParams(vmem_limit_bytes=60 * 2**20),
        name="adam_matrices",
    )(norm, *grads, *weights, *firsts, *seconds)
    return outs[:per], outs[per : 2 * per], outs[2 * per :]


def scatter_rows(values, axis):
    return lax.psum_scatter(values, "dp", scatter_dimension=axis, tiled=True)


def per_device_plane(
    nf,
    nd,
    tokens,
    cotangent,
    order,
    lengths,
    w_qkv,
    w_out,
    w_gate_up,
    w_down,
    gains,
    first_qkv,
    first_out,
    first_gate_up,
    first_down,
    first_gains,
    second_qkv,
    second_out,
    second_gate_up,
    second_down,
    second_gains,
):
    low = jnp.bfloat16
    q_width = HEADS // nf * HD
    kv_all = KVH * HD
    hidden_own = FF // nf
    rows_own = w_qkv.shape[0]

    order_row = order[0]
    places = jnp.arange(TOK_DEV, dtype=jnp.int32)
    inverse = jnp.zeros((TOK_DEV,), jnp.int32).at[order_row].set(places)
    rows_in = tokens[order_row].astype(jnp.float32)
    back_rows = cotangent[order_row].astype(jnp.float32)
    attn_gain = gains[:D]
    ffn_gain = gains[D : 2 * D]
    query_gain = gains[2 * D : 2 * D + HD]
    key_gain = gains[2 * D + HD :]

    _, valid_rows, _ = layout(lengths)
    valid_col = valid_rows.reshape(TOK_DEV, 1)

    qkv_low = w_qkv.astype(low)

    def head_blocks(rows, width):
        return jnp.swapaxes(rows.reshape(rows_own, -1, width), 0, 1)

    qkv_blocks = jnp.concatenate(
        [
            head_blocks(qkv_low[:, :D], q_width),
            head_blocks(qkv_low[:, D : D + kv_all], HD),
            head_blocks(qkv_low[:, D + kv_all :], HD),
        ],
        axis=2,
    )
    wide = q_width + 2 * HD
    own_down = lax.all_gather(w_down.astype(low), "dp", axis=0, tiled=True)
    own_qkv, own_out, half_a, half_b, down_back, notes = start(
        qkv_blocks,
        w_out.astype(low),
        w_gate_up.astype(low),
        (valid_col * back_rows).astype(low),
        jnp.pad(lengths, ((0, 8 - MB), (0, 128 - SEQS))),
        1,
    )
    own_qkv = own_qkv.reshape(D, wide)
    lengths_all = notes[:, :MB, :SEQS].reshape(nf * MB, SEQS)
    half_a, own_down = lax.optimization_barrier((half_a, own_down))
    own_a = lax.all_gather(half_a, "dp", axis=1, tiled=True).reshape(D, hidden_own)
    own_b = lax.all_gather(half_b, "dp", axis=1, tiled=True).reshape(D, hidden_own)

    normed_one, norm_one_pull = jax.vjp(rms_norm, rows_in, attn_gain)
    attention_sums, attention_back = attention(
        normed_one.astype(low), own_qkv, own_out, lengths_all, query_gain, key_gain
    )
    hidden = rows_in + valid_col * attention_sums

    normed_two, norm_two_pull = jax.vjp(rms_norm, hidden, ffn_gain)
    norm_two_all, act_a, back_a, down_a, part_a = gather_glu(
        normed_two.astype(low), own_a, own_down, down_back, 5
    )
    sums_a = scatter_rows(part_a.reshape(nf, nd * rows_own, hidden_own), 1)
    act_b, back_b, part_b = glu(norm_two_all, down_back, own_b, own_down, down_a, 6)
    sums_b = scatter_rows(part_b, 0)[0]
    normed_two_grad = product_scatter((back_a, back_b), (own_a, own_b), 8, turned=True)
    hidden_norm_grad, ffn_gain_grad = norm_two_pull(normed_two_grad)
    hidden_grad = back_rows + hidden_norm_grad

    branch_own = (valid_col * hidden_grad).astype(low)
    branch_own, sums_a = lax.optimization_barrier((branch_own, sums_a))
    normed_one_grad, part_attn, query_gain_grad, key_gain_grad = attention_back(branch_own)
    sums_attn = scatter_rows(part_attn.reshape(nf, nd * rows_own, wide + q_width), 1)
    normed_one_grad, act_a = lax.optimization_barrier((normed_one_grad, act_a))
    output, grad_a = last(
        hidden,
        valid_col,
        act_a,
        act_b,
        own_down,
        sums_a.reshape(nf * rows_own, hidden_own),
        rows_own,
        7,
    )
    output, sums_b = lax.optimization_barrier((output, sums_b))
    grad_b, squares_b = exchange_half(sums_b, rows_own, 11)
    rows_grad, attn_gain_grad = norm_one_pull(normed_one_grad)
    input_grad = (hidden_grad + rows_grad)[inverse]
    output_all = output[inverse]

    early = jnp.sum(jnp.square(sums_a.astype(jnp.float32)))
    input_grad, output_all, early, sums_attn, squares_b = lax.optimization_barrier(
        (input_grad, output_all, early, sums_attn, squares_b)
    )
    early_squares = early + jnp.sum(squares_b)
    gain_sum = jnp.concatenate([attn_gain_grad, ffn_gain_grad, query_gain_grad, key_gain_grad])
    gain_total, norm, grad_qkv, grad_out = sum_everywhere(
        gain_sum, early_squares, sums_attn, wide, 13
    )
    global_norm, factor = norm[0, 0], norm[1, 0]
    new_matrices, next_firsts, next_seconds = adam_matrices(
        norm,
        grad_qkv,
        grad_out,
        grad_a,
        grad_b,
        sums_b,
        (w_qkv, w_out, w_gate_up, w_down),
        (first_qkv, first_out, first_gate_up, first_down),
        (second_qkv, second_out, second_gate_up, second_down),
    )
    new_gains, next_first_gains, next_second_gains = adam_step(
        gains, first_gains, second_gains, gain_total, factor, GAIN_RATE, 0.0
    )
    return (
        output_all,
        input_grad,
        global_norm,
        *new_matrices,
        new_gains,
        *next_firsts,
        next_first_gains,
        *next_seconds,
        next_second_gains,
    )


def gather_tokens(rows):
    return lax.all_gather(rows, "fsdp", axis=0, tiled=True)


def scatter_tokens(rows):
    return lax.psum_scatter(
        rows.astype(jnp.bfloat16), "fsdp", scatter_dimension=0, tiled=True
    ).astype(jnp.float32)


def swap(blocks):
    return lax.all_to_all(blocks, "fsdp", split_axis=0, concat_axis=0, tiled=True)


def per_device_plain(
    nf,
    nd,
    tokens,
    cotangent,
    order,
    lengths,
    w_qkv,
    w_out,
    w_gate_up,
    w_down,
    gains,
    first_qkv,
    first_out,
    first_gate_up,
    first_down,
    first_gains,
    second_qkv,
    second_out,
    second_gate_up,
    second_down,
    second_gains,
):
    low = jnp.bfloat16
    kvl = max(KVH // nf, 1)
    rep = max(nf // KVH, 1)
    heads_own = HEADS // nf
    group = heads_own // kvl
    q_width, kv_width = heads_own * HD, kvl * HD
    kv_all = KVH * HD
    hidden_own = FF // nf
    rows_own = w_qkv.shape[0]
    n_mb = nf * MB

    def head_blocks(rows, width):
        return jnp.swapaxes(rows.reshape(rows_own, -1, width), 0, 1)

    qkv_low = w_qkv.astype(low)
    qkv_blocks = jnp.concatenate(
        [
            head_blocks(qkv_low[:, :D], q_width),
            jnp.repeat(head_blocks(qkv_low[:, D : D + kv_all], kv_width), rep, axis=0),
            jnp.repeat(head_blocks(qkv_low[:, D + kv_all :], kv_width), rep, axis=0),
        ],
        axis=2,
    )
    wide = q_width + 2 * kv_width
    own_qkv = lax.all_gather(swap(qkv_blocks), "dp", axis=1, tiled=True).reshape(D, wide)
    own_out = lax.all_gather(w_out.astype(low), "dp", axis=0, tiled=True)
    gate_up_blocks = jnp.transpose(
        w_gate_up.astype(low).reshape(rows_own, 2, nf, hidden_own), (2, 0, 1, 3)
    ).reshape(nf, rows_own, 2 * hidden_own)
    own_gate_up = lax.all_gather(swap(gate_up_blocks), "dp", axis=1, tiled=True).reshape(
        D, 2 * hidden_own
    )
    own_down = lax.all_gather(w_down.astype(low), "dp", axis=0, tiled=True)

    order_row = order[0]
    places = jnp.arange(TOK_DEV, dtype=jnp.int32)
    inverse = jnp.zeros((TOK_DEV,), jnp.int32).at[order_row].set(places)
    rows_in = tokens[order_row].astype(jnp.float32)
    back_rows = cotangent[order_row].astype(jnp.float32)
    attn_gain = gains[:D]
    ffn_gain = gains[D : 2 * D]
    query_gain = gains[2 * D : 2 * D + HD]
    key_gain = gains[2 * D + HD :]
    score_scale = HD ** (-0.5)

    lengths_all = gather_tokens(lengths)
    position, _, allowed = layout(lengths_all)
    _, valid_rows, _ = layout(lengths)
    valid_col = valid_rows.reshape(TOK_DEV, 1)
    allowed = allowed[:, None, None]
    cosine_table, sine_table = rope_tables(position.reshape(-1))

    normed_one, norm_one_pull = jax.vjp(rms_norm, rows_in, attn_gain)
    norm_one_all = gather_tokens(normed_one.astype(low))
    projected = product(norm_one_all, own_qkv)
    n_rows = norm_one_all.shape[0]
    query_raw = projected[:, :q_width].reshape(n_rows, heads_own, HD)
    key_raw = projected[:, q_width : q_width + kv_width].reshape(n_rows, kvl, HD)
    values_low = projected[:, q_width + kv_width :].reshape(n_mb, MB_TOK, kvl, HD).astype(low)

    def turn_heads(query_in, key_in, query_scale, key_scale):
        return (
            rotate(rms_norm(query_in, query_scale), cosine_table, sine_table),
            rotate(rms_norm(key_in, key_scale), cosine_table, sine_table),
        )

    turned, turn_pull = jax.vjp(turn_heads, query_raw, key_raw, query_gain, key_gain)
    queries_low = turned[0].astype(low).reshape(n_mb, MB_TOK, kvl, group, HD)
    keys_low = turned[1].astype(low).reshape(n_mb, MB_TOK, kvl, HD)
    scores = (
        jnp.einsum("mtkgd,mukd->mkgtu", queries_low, keys_low, preferred_element_type=jnp.float32)
        * score_scale
    )
    scores = jnp.where(allowed, scores, MASKED)
    row_peak = jnp.max(scores, axis=-1, keepdims=True)
    powers = jnp.exp(scores - row_peak)
    totals = jnp.sum(powers, axis=-1, keepdims=True)
    probs = powers / totals
    probs_low = probs.astype(low)
    attended = jnp.einsum(
        "mkgtu,mukd->mtkgd", probs_low, values_low, preferred_element_type=jnp.float32
    )
    attended_low = attended.reshape(n_rows, q_width).astype(low)
    hidden = rows_in + valid_col * scatter_tokens(product(attended_low, own_out))

    normed_two, norm_two_pull = jax.vjp(rms_norm, hidden, ffn_gain)
    norm_two_all = gather_tokens(normed_two.astype(low))
    down_back = gather_tokens((valid_col * back_rows).astype(low))
    gate_up = product(norm_two_all, own_gate_up)
    activation, glu_pull = jax.vjp(swiglu, gate_up[:, :hidden_own], gate_up[:, hidden_own:])
    activation_low = activation.astype(low)
    output = hidden + valid_col * scatter_tokens(product(activation_low, own_down))
    gate_back, up_back = glu_pull(contract_last(down_back, own_down))
    gate_up_back = jnp.concatenate([gate_back.astype(low), up_back.astype(low)], axis=1)
    normed_two_grad = scatter_tokens(contract_last(gate_up_back, own_gate_up))
    grad_down = lax.psum_scatter(
        column_product(activation_low, down_back).astype(low),
        "dp",
        scatter_dimension=0,
        tiled=True,
    ).astype(jnp.float32)
    grad_gate_up = lax.psum_scatter(
        column_product(norm_two_all, gate_up_back)
        .astype(low)
        .reshape(nf, nd * rows_own, 2 * hidden_own),
        "dp",
        scatter_dimension=1,
        tiled=True,
    )
    grad_gate_up = jnp.transpose(
        swap(grad_gate_up).reshape(nf, rows_own, 2, hidden_own), (1, 2, 0, 3)
    ).reshape(rows_own, 2 * FF)
    grad_gate_up = grad_gate_up.astype(jnp.float32)
    hidden_norm_grad, ffn_gain_grad = norm_two_pull(normed_two_grad)
    hidden_grad = back_rows + hidden_norm_grad

    branch_back = gather_tokens((valid_col * hidden_grad).astype(low))
    attended_back = contract_last(branch_back, own_out).astype(low)
    grad_out = lax.psum_scatter(
        column_product(attended_low, branch_back).astype(low),
        "dp",
        scatter_dimension=0,
        tiled=True,
    ).astype(jnp.float32)
    attended_five = attended_back.reshape(n_mb, MB_TOK, kvl, group, HD)
    probs_grad = jnp.einsum(
        "mtkgd,mukd->mkgtu", attended_five, values_low, preferred_element_type=jnp.float32
    )
    spread = jnp.sum(probs * probs_grad, axis=-1, keepdims=True)
    score_back = (probs * (probs_grad - spread)).astype(low)
    query_grad = (
        jnp.einsum("mkgtu,mukd->mtkgd", score_back, keys_low, preferred_element_type=jnp.float32)
        * score_scale
    )
    key_grad = (
        jnp.einsum("mkgtu,mtkgd->mukd", score_back, queries_low, preferred_element_type=jnp.float32)
        * score_scale
    )
    value_grad = jnp.einsum(
        "mkgtu,mtkgd->mukd", probs_low, attended_five, preferred_element_type=jnp.float32
    )
    query_in_grad, key_in_grad, query_gain_grad, key_gain_grad = turn_pull(
        (query_grad.reshape(n_rows, heads_own, HD), key_grad.reshape(n_rows, kvl, HD))
    )
    projected_back = jnp.concatenate(
        [
            query_in_grad.reshape(n_rows, q_width),
            key_in_grad.reshape(n_rows, kv_width),
            value_grad.reshape(n_rows, kv_width),
        ],
        axis=1,
    ).astype(low)
    normed_one_grad = scatter_tokens(contract_last(projected_back, own_qkv))
    grad_qkv = lax.psum_scatter(
        column_product(norm_one_all, projected_back)
        .astype(low)
        .reshape(nf, nd * rows_own, wide),
        "dp",
        scatter_dimension=1,
        tiled=True,
    )
    grad_blocks = swap(grad_qkv).astype(jnp.float32)

    def head_rows(blocks, times):
        merged = jnp.sum(blocks.reshape(nf // times, times, rows_own, -1), axis=1)
        return jnp.swapaxes(merged, 0, 1).reshape(rows_own, -1)

    grad_qkv = jnp.concatenate(
        [
            head_rows(grad_blocks[:, :, :q_width], 1),
            head_rows(grad_blocks[:, :, q_width : q_width + kv_width], rep),
            head_rows(grad_blocks[:, :, q_width + kv_width :], rep),
        ],
        axis=1,
    )
    rows_grad, attn_gain_grad = norm_one_pull(normed_one_grad)
    input_grad = (hidden_grad + rows_grad)[inverse]
    output_all = output.astype(low)[inverse]

    owned = (grad_qkv, grad_out, grad_gate_up, grad_down)
    local_squares = (
        jnp.sum(owned[0] * owned[0])
        + jnp.sum(owned[1] * owned[1])
        + jnp.sum(owned[2] * owned[2])
        + jnp.sum(owned[3] * owned[3])
    )
    gain_sum = jnp.concatenate([attn_gain_grad, ffn_gain_grad, query_gain_grad, key_gain_grad])
    gain_total, square_total = lax.psum((gain_sum, local_squares), ("fsdp", "dp"))
    global_norm = jnp.sqrt(square_total + jnp.sum(gain_total * gain_total))
    factor = CLIP_NORM / jnp.maximum(global_norm, CLIP_NORM)
    new_qkv, next_first_qkv, next_second_qkv = adam_step(
        w_qkv, first_qkv, second_qkv, owned[0], factor, LEARN_RATE, WEIGHT_DECAY
    )
    new_out, next_first_out, next_second_out = adam_step(
        w_out, first_out, second_out, owned[1], factor, LEARN_RATE, WEIGHT_DECAY
    )
    new_gate_up, next_first_gate_up, next_second_gate_up = adam_step(
        w_gate_up, first_gate_up, second_gate_up, owned[2], factor, LEARN_RATE, WEIGHT_DECAY
    )
    new_down, next_first_down, next_second_down = adam_step(
        w_down, first_down, second_down, owned[3], factor, LEARN_RATE, WEIGHT_DECAY
    )
    new_gains, next_first_gains, next_second_gains = adam_step(
        gains, first_gains, second_gains, gain_total, factor, GAIN_RATE, 0.0
    )
    return (
        output_all,
        input_grad,
        global_norm,
        new_qkv,
        new_out,
        new_gate_up,
        new_down,
        new_gains,
        next_first_qkv,
        next_first_out,
        next_first_gate_up,
        next_first_down,
        next_first_gains,
        next_second_qkv,
        next_second_out,
        next_second_gate_up,
        next_second_down,
        next_second_gains,
    )


def solution(mesh):
    nf, nd = mesh.shape["fsdp"], mesh.shape["dp"]
    fits = nf == PLANE and KVH == PLANE and nd % 2 == 0
    per_device = per_device_plane if fits else per_device_plain
    in_specs = (
        P(("fsdp", "dp"), None),
        P(("fsdp", "dp"), None),
        P(("fsdp", "dp"), None),
        P(("fsdp", "dp"), None),
        P(("fsdp", "dp"), None),
        P(("fsdp", "dp"), None),
        P(("fsdp", "dp"), None),
        P(("fsdp", "dp"), None),
        P(),
        P(("fsdp", "dp"), None),
        P(("fsdp", "dp"), None),
        P(("fsdp", "dp"), None),
        P(("fsdp", "dp"), None),
        P(),
        P(("fsdp", "dp"), None),
        P(("fsdp", "dp"), None),
        P(("fsdp", "dp"), None),
        P(("fsdp", "dp"), None),
        P(),
    )
    out_specs = (
        P(("fsdp", "dp"), None),
        P(("fsdp", "dp"), None),
        P(),
        P(("fsdp", "dp"), None),
        P(("fsdp", "dp"), None),
        P(("fsdp", "dp"), None),
        P(("fsdp", "dp"), None),
        P(),
        P(("fsdp", "dp"), None),
        P(("fsdp", "dp"), None),
        P(("fsdp", "dp"), None),
        P(("fsdp", "dp"), None),
        P(),
        P(("fsdp", "dp"), None),
        P(("fsdp", "dp"), None),
        P(("fsdp", "dp"), None),
        P(("fsdp", "dp"), None),
        P(),
    )
    return jax.shard_map(
        functools.partial(per_device, nf, nd), mesh=mesh, in_specs=in_specs, out_specs=out_specs, check_vma=False
    )
```

time: 2200 us -> 632 us (0.29)
  waiting for transfers between devices: 1710 us -> 10.6 us
  Pallas kernels: 0 us -> 547 us
  matrix products: 314 us -> 0 us
  blocking collectives: 41.5 us -> 0 us
  other arithmetic: 67.6 us -> 31.6 us
    reduce_scatter x8 -> x3, waiting for transfers between devices: 895 us -> 9.76 us  [scatter_rows(): return lax.psum_scatter(values, 'dp', scatter_dimension=axis, tiled=True)]
    all_gather x8 -> x3, waiting for transfers between devices: 816 us -> 0.04 us  [the longest x1 0.02 us: per_device_plane(): own_down = lax.all_gather(w_down.astype(low), 'dp', axis=0, tiled=True)]
    pallas_call x0 -> x10, Pallas kernels: none -> 547 us  [the longest x1 116 us: start(): pl.pallas_call(functools.partial(start_kernel, nd), out_shape=[jax.ShapeD...]
    dot_general x32 -> x0, matrix products: 314 us -> none  [the longest x8 141 us: contract_last(): lax.dot_general(left_side, right_side, (((1,), (1,)), ((), ())), preferre...]
    psum x1 -> x0, blocking collectives: 41.5 us -> none  [per_device(): lax.psum((gain_sum, local_squares), ('fsdp', 'dp'))]
  transfers between devices with their start and end apart: 16 -> 6, of which waited for: 14 -> 1; matrix products, arithmetic and copies ran while one was open for 10% -> 6% of each run, Pallas kernels for 0% -> 83%
where the time goes in v1:
time: 632 us; the launch traced here: 623 us
  Pallas kernels  547 us (87%)
  other arithmetic  31.6 us (5%)
  local copies, waits for them, and re-layouts  17.9 us (3%)
  between operations  16.1 us (3%)
  waiting for transfers between devices  10.6 us (2%)
    pallas_call x1, Pallas kernels, start(): pl.pallas_call(functools.partial(start_kernel, nd), out_shape=[jax.ShapeD...  116 us
    pallas_call x1, Pallas kernels, attend(): pl.pallas_call(staged(attend_kernel, len(arrays), places), out_shape=[jax...  90.1 us
    pallas_call x1, Pallas kernels, attend_back(): pl.pallas_call(staged(attend_back_kernel, len(arrays), places), out_shape...  89.6 us
    pallas_call x1, Pallas kernels, gather_glu(): pl.pallas_call(gather_glu_kernel, out_shape=[jax.ShapeDtypeStruct((count,...  58.2 us
    pallas_call x1, Pallas kernels, last(): pl.pallas_call(staged(last_kernel, len(arrays) + 1, places), out_shape=[j...  51.3 us
    pallas_call x1, Pallas kernels, product_scatter(): pl.pallas_call(functools.partial(scatter_kernel, turned, len(left_sides))...  50.7 us
    pallas_call x1, Pallas kernels, glu(): pl.pallas_call(glu_kernel, grid=(count // step,), out_shape=[jax.ShapeDty...  41.2 us
    pallas_call x1, Pallas kernels, adam_matrices(): pl.pallas_call(functools.partial(adam_kernel, chunks, len(grads), per), o...  18.4 us
  transfers between devices with their start and end apart: 6, of which 1 were waited for; matrix products, arithmetic and copies ran while one was open for 6% of the time, Pallas kernels for 83%

profile of v1, /device:TPU:0, one launch (start us, length us, event | category | flops | bytes accessed | tf_op | source)
XLA Modules:
  0.0 623.0 jit_solution(16391054412913266352)
XLA Ops:
  7.3 2.9 convert_element_type.90
  12.2 3.7 convert_element_type.83.wide_ref
  16.0 1.4 gather_fusion
  19.7 115.6 %start_1.1 = (bf16[8,256,384]{2,1,0:T(8,128)(2,1)}, bf16[256,2048]{1,0:T(8,128)(2,1)}, bf16[8,64,1024]{2,1,0:T(8,128)(2,1)}, bf16[8,64,1024]{2,1,0:T(8,128)(2,1)...) custom-call(bf16[8,64,384]{2,1,0:T(8,128)(2,1)} %pad_maximum_fusion.qkv_ref, ...), custom_call_target="tpu_custom_call" | custom-call | bytes 1024 | tf_op jit(solution)/shard_map/start_1/pallas_call | solution.py:1279
  136.3 1.4 gather_fusion.1
  146.1 90.1 %attend_3.1 = (f32[256,2048]{1,0:T(8,128)}, bf16[2048,2048]{1,0:T(8,128)(2,1)}, f32[2048,384]{1,0:T(8,128)}, bf16[2048,256]{1,0:T(8,128)(2,1)}, bf16[2048,128]{1...) custom-call(bf16[256,2048]{1,0:T(8,128)(2,1)} %fusion.2.refs_0_, ...), custom_call_target="tpu_custom_call" | custom-call | bytes 1024 | tf_op jit(solution)/shard_map/attend_3/pallas_call | solution.py:988
  236.2 2.1 multiply_reduce_fusion.3
  238.3 1.4 multiply_convert_fusion.1.x_ref
  239.7 58.2 %gather_glu_5.1 = (bf16[2048,2048]{1,0:T(8,128)(2,1)}, bf16[2048,512]{1,0:T(8,128)(2,1)}, bf16[2048,1024]{1,0:T(8,128)(2,1)}, bf16[512,2048]{1,0:T(8,128)(2,1)}, bf16[2048,1024]{1,0:T(8,128)(2,1)}) custom-call(bf16[256,2048]{1,0:T(8,128)(2,1)} %multiply_convert_fusion.1.x_ref, bf16[2048,1024]{1,0:T(8,128)(2,1)} %bitcast.46, ...), custom_call_target="tpu_custom_call" | custom-call | bytes 1024 | tf_op jit(solution)/shard_map/gather_glu_5/pallas_call | solution.py:1414
  298.0 41.2 %glu_6.1 = (bf16[2048,512]{1,0:T(8,128)(2,1)}, bf16[2048,1024]{1,0:T(8,128)(2,1)}, bf16[4,1024,1024]{2,1,0:T(8,128)(2,1)}) custom-call(bf16[2048,2048]{1,0:T(8,128)(2,1)} %get-tuple-element.85.x_ref, bf16[2048,2048]{1,0:T(8,128)(2,1)} %get-tuple-element.83.df_hbm.df_ref, bf16[2048,1024]{1,0:T(8,128)(2,1)} %bitcast.48, ...), custom_call_target="tpu_custom_call" | custom-call | bytes 1024 | tf_op jit(solution)/shard_map/glu_6/pallas_call | solution.py:1485
  339.3 50.7 %product_scatter_8.1 = f32[256,2048]{1,0:T(8,128)} custom-call(bf16[2048,1024]{1,0:T(8,128)(2,1)} %get-tuple-element.84.refs_0_, bf16[2048,1024]{1,0:T(8,128)(2,1)} %get-tuple-element.88.refs_1_, bf16[2048,1024]{1,0:T(8,128)(2,1)} %bitcast.47, bf16[2048,1024]{1,0:T(8,128)(2,1)} %bitcast.49), custom_call_target="tpu_custom_call" | custom-call | bytes 1024 | tf_op jit(solution)/shard_map/product_scatter_8/pallas_call | solution.py:1064
  390.0 2.3 multiply_reduce_fusion
  392.5 1.7 multiply_convert_fusion.refs_0_
  394.2 89.6 %attend_back_9.1 = (f32[256,2048]{1,0:T(8,128)}, bf16[2048,640]{1,0:T(8,128)(2,1)}, f32[8,128]{1,0:T(8,128)}) custom-call(bf16[256,2048]{1,0:T(8,128)(2,1)} %multiply_convert_fusion.refs_0_, bf16[2048,384]{1,0:T(8,128)(2,1)} %bitcast.53, bf16[256,2048]{1,0:T(8,128)(2,1)} %get-tuple-element.77.refs_2_, f32[2048,128]{1,0:T(8,128)} %copy.56.refs_3_, ...), custom_call_target="tpu_custom_call" | custom-call | bytes 1024 | tf_op jit(solution)/shard_map/attend_back_9/pallas_call | solution.py:1034
  483.8 1.4 scatter_custom_fusion
  487.6 3.6 fusion.5
  491.2 2.7 gather_fusion.2
  493.9 51.3 %last_7.1 = (bf16[256,2048]{1,0:T(8,128)(2,1)}, bf16[64,8192]{1,0:T(8,128)(2,1)}) custom-call(f32[256,2048]{1,0:T(8,128)} %copy-done.2, f32[256,1]{1,0:T(8,128)} %copy.60.refs_1_, bf16[2048,512]{1,0:T(8,128)(2,1)} %get-tuple-element.101.refs_2_, bf16[2048,512]{1,0:T(8,128)(2,1)} %get-tuple-element.102.refs_3_, ...), custom_call_target="tpu_custom_call" | custom-call | bytes 1024 | tf_op jit(solution)/shard_map/last_7/pallas_call | solution.py:1601
  547.3 2.3 gather_fusion.3
  549.6 17.6 %exchange_half_11.1 = (bf16[64,8192]{1,0:T(8,128)(2,1)}, f32[1,1024]{1,0:T(1,128)}) custom-call(bf16[1024,1024]{1,0:T(8,128)(2,1)} %bitcast.50), custom_call_target="tpu_custom_call" | custom-call | bytes 1024 | tf_op jit(solution)/shard_map/exchange_half_11/pallas_call | solution.py:206
  567.3 9.8 %reduce-scatter.8.cloned.1.call-done.blocks_ref = bf16[8,64,640]{2,1,0:T(8,128)(2,1)} async-done(((bf16[8,256,640]{2,1,0:T(8,128)(2,1)}), bf16[8,64,640]{2,1,0:T(8,128)(2,1)}) %reduce-scatter.8.cloned.1.call-update) | async-done | bytes 655376 | tf_op jit(solution)/shard_map/reduce_scatter | solution.py:1749
  580.3 14.0 %sum_everywhere_13.1 = (f32[40,128]{1,0:T(8,128)}, f32[8,128]{1,0:T(8,128)}, bf16[64,3072]{1,0:T(8,128)(2,1)}, bf16[64,2048]{1,0:T(8,128)(2,1)}) custom-call(f32[40,128]{1,0:T(8,128)} %pad_bitcast_fusion.x_ref, bf16[8,64,640]{2,1,0:T(8,128)(2,1)} %reduce-scatter.8.cloned.1.call-done.blocks_ref), custom_call_target="tpu_custom_call" | custom-call | bytes 1024 | tf_op jit(solution)/shard_map/sum_everywhere_13/pallas_call | solution.py:356
  595.6 2.0 multiply_subtract_fusion
  597.6 18.4 %adam_matrices.1 = (f32[64,3072]{1,0:T(8,128)}, f32[64,2048]{1,0:T(8,128)}, f32[64,16384]{1,0:T(8,128)}, f32[256,2048]{1,0:T(8,128)}, f32[64,3072]{1,0:T(8,128)}...) custom-call(f32[8,128]{1,0:T(8,128)} %get-tuple-element.116.norm_ref, ...), custom_call_target="tpu_custom_call" | custom-call | tf_op jit(solution)/shard_map/adam_matrices/pallas_call | solution.py:1730
  (111 shorter events, 21.8 us)
Async XLA Ops:
  7.2 8.8 %copy-start = (bf16[256,2048]{1,0:T(8,128)(2,1)S(1)}, bf16[256,2048]{1,0:T(8,128)(2,1)}, u32[]{:S(2)}) copy-start(bf16[256,2048]{1,0:T(8,128)(2,1)} %param.20) | copy-start | bytes 3145732
  7.2 3.0 copy-start.18
  7.2 3.9 copy-start.14
  7.2 4.6 copy-start.13
  7.2 128.0 %all-gather.4.cloned.1.call-start = ((), (), s32[]{:S(2)}) async-start(), calls=%async_computation.3 | async-start | bytes 5242880 | tf_op jit(solution)/shard_map/all_gather | solution.py:1808
  10.2 229.6 %all-gather.6.cloned.1.call-start = ((), (), s32[]{:S(2)}) async-start(), calls=%async_computation.4 | async-start | bytes 5242880 | tf_op jit(solution)/shard_map/all_gather | solution.py:1820
  12.2 3.7 copy-start.19
  17.3 117.9 %copy-start.8 = (bf16[256,2048]{1,0:T(8,128)(2,1)}, bf16[256,2048]{1,0:T(8,128)(2,1)S(1)}, u32[]{:S(2)}) copy-start(bf16[256,2048]{1,0:T(8,128)(2,1)S(1)} %gather_fusion) | copy-start | bytes 3145732
  19.7 116.4 %copy-start.15 = (f32[4224]{0:T(1024)S(1)}, f32[4224]{0:T(1024)}, u32[]{:S(2)}) copy-start(f32[4224]{0:T(1024)} %param.27) | copy-start | bytes 50692
  19.7 116.7 %copy-start.3 = (bf16[256,2048]{1,0:T(8,128)(2,1)S(1)}, bf16[256,2048]{1,0:T(8,128)(2,1)}, u32[]{:S(2)}) copy-start(bf16[256,2048]{1,0:T(8,128)(2,1)} %param.19) | copy-start | bytes 3145732
  135.3 162.7 %all-gather.8.cloned.1.call-start = ((), (), s32[]{:S(2)}) async-start(), calls=%async_computation.5 | async-start | bytes 5242880 | tf_op jit(solution)/shard_map/all_gather | solution.py:1821
  136.0 258.2 %reduce-scatter.4.cloned.1.call-start = ((), (), s32[]{:S(2)}) async-start(), calls=%async_computation.6 | async-start | bytes 5242880 | tf_op jit(solution)/shard_map/reduce_scatter | solution.py:1749
  137.7 7.1 %copy-start.5 = (bf16[256,2048]{1,0:T(8,128)(2,1)}, bf16[256,2048]{1,0:T(8,128)(2,1)S(1)}, u32[]{:S(2)}) copy-start(bf16[256,2048]{1,0:T(8,128)(2,1)S(1)} %gather_fusion.1) | copy-start | bytes 3145732
  146.1 90.1 %copy-start.6 = (bf16[256,2048]{1,0:T(8,128)(2,1)S(1)}, bf16[256,2048]{1,0:T(8,128)(2,1)}, u32[]{:S(2)}) copy-start(bf16[256,2048]{1,0:T(8,128)(2,1)} %copy-done.5) | copy-start | bytes 3145732
  238.3 154.0 %copy-start.2 = (f32[256,2048]{1,0:T(8,128)}, f32[256,2048]{1,0:T(8,128)S(1)}, u32[]{:S(2)}) copy-start(f32[256,2048]{1,0:T(8,128)S(1)} %get-tuple-element.144.refs_0_) | copy-start | bytes 6291460
  298.0 249.3 %reduce-scatter.6.cloned.1.call-start = ((), (), s32[]{:S(2)}) async-start(), calls=%async_computation.7 | async-start | bytes 10485760 | tf_op jit(solution)/shard_map/reduce_scatter | solution.py:1749
  339.3 237.8 %reduce-scatter.8.cloned.1.call-start = ((), (), s32[]{:S(2)}) async-start(), calls=%async_computation.8 | async-start | bytes 3276800 | tf_op jit(solution)/shard_map/reduce_scatter | solution.py:1749
  390.0 2.3 copy-start.7
  390.0 2.5 copy-start.9
  483.7 2.3 copy-start.10
  493.9 51.4 %copy-start.12 = (bf16[8,64,1024]{2,1,0:T(8,128)(2,1)S(1)}, bf16[8,64,1024]{2,1,0:T(8,128)(2,1)}, u32[]{:S(2)}) copy-start(bf16[8,64,1024]{2,1,0:T(8,128)(2,1)} %reduce-scatter.4.cloned.1.call-done) | copy-start | bytes 3145732
  549.6 46.0 %copy-start.16 = (f32[4224]{0:T(1024)S(1)}, f32[4224]{0:T(1024)}, u32[]{:S(2)}) copy-start(f32[4224]{0:T(1024)} %param.32) | copy-start | bytes 50692
  549.6 46.0 %copy-start.17 = (f32[4224]{0:T(1024)S(1)}, f32[4224]{0:T(1024)}, u32[]{:S(2)}) copy-start(f32[4224]{0:T(1024)} %param.37) | copy-start | bytes 50692
  597.6 18.4 %copy-start.1 = (bf16[256,2048]{1,0:T(8,128)(2,1)S(1)}, bf16[256,2048]{1,0:T(8,128)(2,1)}, u32[]{:S(2)}) copy-start(bf16[256,2048]{1,0:T(8,128)(2,1)} %param.20) | copy-start | bytes 3145732
  (2 other events, 3.6 us)
Sparse Core Ops, SparseCore 0:
  10.3 113.3 all-gather.3
  135.4 80.7 all-gather.5
  217.8 79.2 all-gather.7
  299.2 75.2 reduce-scatter.3
  376.9 144.9 reduce-scatter.5
  524.2 52.8 reduce-scatter.7

commit v2 on v1

--- a/solution.py
+++ b/solution.py
@@ -1620,124 +1620,131 @@
 
 def adam_kernel(chunks, n_grads, per, norm_ref, *refs):
     grads, refs = refs[:n_grads], refs[n_grads:]
-    groups = [refs[place * per : (place + 1) * per] for place in range(6)]
-    in_buf, grad_buf, out_buf, in_sems, out_sems = refs[6 * per :]
-    depth = in_buf.shape[0]
+    states = [refs[place * per : (place + 1) * per] for place in range(3)]
+    outs = [refs[(3 + place) * per : (4 + place) * per] for place in range(3)]
+    refs = refs[6 * per :]
+    grad_bufs, refs = refs[:n_grads], refs[n_grads:]
+    bufs = [refs[place * per : (place + 1) * per] for place in range(3)]
+    grad_sems, in_sems, out_sems = refs[3 * per :]
     factor = norm_ref[1:2, 0:1]
     first_scale = 1.0 / (1.0 - FIRST_DECAY**STEP)
     second_scale = 1.0 / (1.0 - SECOND_DECAY**STEP)
 
     def fetch(number):
-        which, rows, columns, pieces = chunks[number]
-        slot, width = number % depth, columns.size
+        which, rows, sources, _ = chunks[number]
         copies = [
             pltpu.make_async_copy(
-                groups[place][which].at[rows, columns],
-                in_buf.at[slot, place, :, pl.ds(0, width)],
-                in_sems.at[slot, place],
+                grads[array].at[spot], grad_bufs[array].at[spot], grad_sems.at[number, place]
+            )
+            for place, (array, spot) in enumerate(sources)
+        ]
+        for place in range(3):
+            copies.append(
+                pltpu.make_async_copy(
+                    states[place][which].at[rows],
+                    bufs[place][which].at[rows],
+                    in_sems.at[number, place],
+                )
+            )
+        return copies
+
+    def put(number):
+        which, rows, _, _ = chunks[number]
+        return [
+            pltpu.make_async_copy(
+                bufs[place][which].at[rows], outs[place][which].at[rows], out_sems.at[number, place]
             )
             for place in range(3)
         ]
-        for place, (array, source, first) in enumerate(pieces):
-            target = grad_buf.at[slot, :, pl.ds(first, source[1].size)]
-            copies.append(
-                pltpu.make_async_copy(
-                    grads[array].at[source], target, in_sems.at[slot, 3 + place]
-                )
-            )
-        return copies
-
-    def put(number):
-        which, rows, columns, _ = chunks[number]
-        slot, width = number % depth, columns.size
-        return [
-            pltpu.make_async_copy(
-                out_buf.at[slot, place, :, pl.ds(0, width)],
-                groups[3 + place][which].at[rows, columns],
-                out_sems.at[slot, place],
-            )
-            for place in range(3)
-        ]
-
-    def update(slot, width):
-        columns = slice(0, width)
-
-        @pl.loop(0, in_buf.shape[2] // 16)
-        def _(step):
-            rows = pl.ds(pl.multiple_of(step * 16, 16), 16)
-            clipped = grad_buf[slot, rows, columns].astype(jnp.float32) * factor
-            weight = in_buf[slot, 0, rows, columns]
-            first = FIRST_DECAY * in_buf[slot, 1, rows, columns] + (1.0 - FIRST_DECAY) * clipped
-            second = SECOND_DECAY * in_buf[slot, 2, rows, columns]
-            second = second + (1.0 - SECOND_DECAY) * clipped * clipped
-            root = jnp.sqrt(second * second_scale) + ADAM_EPSILON
-            change = first * first_scale / root + WEIGHT_DECAY * weight
-            out_buf[slot, 0, rows, columns] = weight - LEARN_RATE * change
-            out_buf[slot, 1, rows, columns] = first
-            out_buf[slot, 2, rows, columns] = second
-
-    for number in range(min(depth, len(chunks))):
+
+    def update(which, rows, columns, grad):
+        weights, firsts, seconds = (bufs[place][which] for place in range(3))
+        clipped = grad.astype(jnp.float32) * factor
+        weight = weights[rows, columns]
+        first = FIRST_DECAY * firsts[rows, columns] + (1.0 - FIRST_DECAY) * clipped
+        second = SECOND_DECAY * seconds[rows, columns] + (1.0 - SECOND_DECAY) * clipped * clipped
+        root = jnp.sqrt(second * second_scale) + ADAM_EPSILON
+        change = first * first_scale / root + WEIGHT_DECAY * weight
+        weights[rows, columns] = weight - LEARN_RATE * change
+        firsts[rows, columns] = first
+        seconds[rows, columns] = second
+
+    for number in range(len(chunks)):
         for copy in fetch(number):
             copy.start()
     for number in range(len(chunks)):
+        which, rows, _, loops = chunks[number]
         for copy in fetch(number):
             copy.wait()
-        if number >= depth:
-            for copy in put(number - depth):
-                copy.wait()
-        update(number % depth, chunks[number][2].size)
+        for array, grad_rows, steps, columns_of, grad_columns_of, width in loops:
+
+            @pl.loop(0, steps)
+            def _(step):
+                columns = pl.ds(pl.multiple_of(columns_of(step), 128), width)
+                grad_columns = pl.ds(pl.multiple_of(grad_columns_of(step), 128), width)
+                update(which, rows, columns, grad_bufs[array][grad_rows, grad_columns])
+
         for copy in put(number):
             copy.start()
-        if number + depth < len(chunks):
-            for copy in fetch(number + depth):
-                copy.start()
-    for number in range(max(0, len(chunks) - depth), len(chunks)):
+    for number in range(len(chunks)):
         for copy in put(number):
             copy.wait()
 
 
 def adam_matrices(norm, grad_qkv, grad_out, grad_a, grad_b, sums_b, weights, firsts, seconds):
-    rows, width, depth = 64, 2048, 6
     half = grad_a.shape[1] // 2 // PLANE
+    whole = weights[2].shape[1] // 2
     count = weights[3].shape[0]
     behind = sums_b.shape[0] - 2 * count
-
-    def pieces(which, row, column, size):
-        here = pl.ds(row, rows)
-        if which < 2:
-            return [(which, (here, pl.ds(column, size)), 0)]
-        if which == 3:
-            return [
-                (4, (pl.ds(behind + side * count + row, rows), pl.ds(0, width // 2)), side * width // 2)
-                for side in range(2)
-            ]
-        first = column // 2
-        return [
-            (2 + part, (here, pl.ds(first + unit * half, half)), (2 * unit + part) * half)
-            for unit in range(width // 2 // half)
-            for part in range(2)
-        ]
-
+    side_width = sums_b.shape[1]
+    width = 512
     chunks = []
-    for which, weight in enumerate(weights):
-        for row in range(0, weight.shape[0], rows):
-            for column in range(0, weight.shape[1], width):
-                size = min(width, weight.shape[1] - column)
-                parts = pieces(which, row, column, size)
-                chunks.append((which, pl.ds(row, rows), pl.ds(column, size), parts))
+
+    def straight(step):
+        return step * width
+
+    for row in range(0, weights[2].shape[0], 16):
+        rows = pl.ds(row, 16)
+        loops = []
+        for part in range(2):
+
+            def columns_of(step, part=part):
+                side, unit = lax.div(step, PLANE), lax.rem(step, PLANE)
+                return side * whole + unit * 2 * half + part * half
+
+            loops.append((2 + part, rows, 2 * PLANE, columns_of, lambda step: step * half, half))
+        chunks.append((2, rows, [(2, rows), (3, rows)], loops))
+    for row in range(0, count, 64):
+        sources, loops = [], []
+        for side in range(2):
+            spot = pl.ds(behind + side * count + row, 64)
+            sources.append((4, spot))
+
+            def columns_of(step, side=side):
+                return side * side_width + step * width
+
+            loops.append((4, spot, side_width // width, columns_of, straight, width))
+        chunks.append((3, pl.ds(row, 64), sources, loops))
+    for which in range(2):
+        for row in range(0, weights[which].shape[0], 32):
+            rows = pl.ds(row, 32)
+            steps = weights[which].shape[1] // width
+            loops = [(which, rows, steps, straight, straight, width)]
+            chunks.append((which, rows, [(which, rows)], loops))
     grads = (grad_qkv, grad_out, grad_a, grad_b, sums_b)
     per = len(weights)
+    number = len(chunks)
     outs = pl.pallas_call(
         functools.partial(adam_kernel, chunks, len(grads), per),
         out_shape=[jax.ShapeDtypeStruct(weight.shape, jnp.float32) for weight in weights] * 3,
         in_specs=[VMEM] + [ANY] * (len(grads) + 3 * per),
         out_specs=[ANY] * (3 * per),
-        scratch_shapes=[
-            pltpu.VMEM((depth, 3, rows, width), jnp.float32),
-            pltpu.VMEM((depth, rows, width), jnp.bfloat16),
-            pltpu.VMEM((depth, 3, rows, width), jnp.float32),
-            pltpu.SemaphoreType.DMA((depth, 7)),
-            pltpu.SemaphoreType.DMA((depth, 3)),
+        scratch_shapes=[pltpu.VMEM(grad.shape, grad.dtype) for grad in grads]
+        + [pltpu.VMEM(weight.shape, jnp.float32) for weight in weights] * 3
+        + [
+            pltpu.SemaphoreType.DMA((number, 2)),
+            pltpu.SemaphoreType.DMA((number, 3)),
+            pltpu.SemaphoreType.DMA((number, 3)),
         ],
         compiler_params=pltpu.CompilerParams(vmem_limit_bytes=60 * 2**20),
         name="adam_matrices",
@@ -1858,11 +1865,10 @@
     input_grad = (hidden_grad + rows_grad)[inverse]
     output_all = output[inverse]
 
-    early = jnp.sum(jnp.square(sums_a.astype(jnp.float32)))
-    input_grad, output_all, early, sums_attn, squares_b = lax.optimization_barrier(
-        (input_grad, output_all, early, sums_attn, squares_b)
-    )
-    early_squares = early + jnp.sum(squares_b)
+    early_squares = jnp.sum(jnp.square(sums_a.astype(jnp.float32))) + jnp.sum(squares_b)
+    input_grad, output_all, early_squares, sums_attn = lax.optimization_barrier(
+        (input_grad, output_all, early_squares, sums_attn)
+    )
     gain_sum = jnp.concatenate([attn_gain_grad, ffn_gain_grad, query_gain_grad, key_gain_grad])
     gain_total, norm, grad_qkv, grad_out = sum_everywhere(
         gain_sum, early_squares, sums_attn, wide, 13

time: 632 us -> 628 us (level)
  transfers between devices with their start and end apart: 6 -> 6, of which waited for: 1 -> 1; matrix products, arithmetic and copies ran while one was open for 6% -> 7% of each run, Pallas kernels for 83% -> 83%
where the time goes in v2:
time: 628 us; the launch traced here: 620 us
  Pallas kernels  546 us (87%)
  other arithmetic  31.6 us (5%)
  local copies, waits for them, and re-layouts  17.9 us (3%)
  between operations  16.3 us (3%)
  waiting for transfers between devices  7.99 us (1%)
    pallas_call x1, Pallas kernels, start(): pl.pallas_call(functools.partial(start_kernel, nd), out_shape=[jax.ShapeD...  116 us
    pallas_call x1, Pallas kernels, attend(): pl.pallas_call(staged(attend_kernel, len(arrays), places), out_shape=[jax...  90.1 us
    pallas_call x1, Pallas kernels, attend_back(): pl.pallas_call(staged(attend_back_kernel, len(arrays), places), out_shape...  89.6 us
    pallas_call x1, Pallas kernels, gather_glu(): pl.pallas_call(gather_glu_kernel, out_shape=[jax.ShapeDtypeStruct((count,...  58.2 us
    pallas_call x1, Pallas kernels, last(): pl.pallas_call(staged(last_kernel, len(arrays) + 1, places), out_shape=[j...  51.4 us
    pallas_call x1, Pallas kernels, product_scatter(): pl.pallas_call(functools.partial(scatter_kernel, turned, len(left_sides))...  50.7 us
    pallas_call x1, Pallas kernels, glu(): pl.pallas_call(glu_kernel, grid=(count // step,), out_shape=[jax.ShapeDty...  41.2 us
    pallas_call x1, Pallas kernels, exchange_half(): pl.pallas_call(columns_kernel, out_shape=[jax.ShapeDtypeStruct((count, ha...  17.6 us
  transfers between devices with their start and end apart: 6, of which 1 were waited for; matrix products, arithmetic and copies ran while one was open for 7% of the time, Pallas kernels for 83%

profile of v2, /device:TPU:0, one launch (start us, length us, event | category | flops | bytes accessed | tf_op | source)
XLA Modules:
  0.0 619.7 jit_solution(6169575795697562786)
XLA Ops:
  7.3 2.9 convert_element_type.90
  12.2 3.7 convert_element_type.83.wide_ref
  16.0 1.4 gather_fusion
  19.7 115.6 %start_1.1 = (bf16[8,256,384]{2,1,0:T(8,128)(2,1)}, bf16[256,2048]{1,0:T(8,128)(2,1)}, bf16[8,64,1024]{2,1,0:T(8,128)(2,1)}, bf16[8,64,1024]{2,1,0:T(8,128)(2,1)...) custom-call(bf16[8,64,384]{2,1,0:T(8,128)(2,1)} %pad_maximum_fusion.qkv_ref, ...), custom_call_target="tpu_custom_call" | custom-call | bytes 1024 | tf_op jit(solution)/shard_map/start_1/pallas_call | solution.py:1279
  136.3 1.4 gather_fusion.1
  146.1 90.1 %attend_3.1 = (f32[256,2048]{1,0:T(8,128)}, bf16[2048,2048]{1,0:T(8,128)(2,1)}, f32[2048,384]{1,0:T(8,128)}, bf16[2048,256]{1,0:T(8,128)(2,1)}, bf16[2048,128]{1...) custom-call(bf16[256,2048]{1,0:T(8,128)(2,1)} %fusion.2.refs_0_, ...), custom_call_target="tpu_custom_call" | custom-call | bytes 1024 | tf_op jit(solution)/shard_map/attend_3/pallas_call | solution.py:988
  236.2 2.1 multiply_reduce_fusion.3
  238.3 1.4 multiply_convert_fusion.1.x_ref
  239.7 58.2 %gather_glu_5.1 = (bf16[2048,2048]{1,0:T(8,128)(2,1)}, bf16[2048,512]{1,0:T(8,128)(2,1)}, bf16[2048,1024]{1,0:T(8,128)(2,1)}, bf16[512,2048]{1,0:T(8,128)(2,1)}, bf16[2048,1024]{1,0:T(8,128)(2,1)}) custom-call(bf16[256,2048]{1,0:T(8,128)(2,1)} %multiply_convert_fusion.1.x_ref, bf16[2048,1024]{1,0:T(8,128)(2,1)} %bitcast.46, ...), custom_call_target="tpu_custom_call" | custom-call | bytes 1024 | tf_op jit(solution)/shard_map/gather_glu_5/pallas_call | solution.py:1414
  298.0 41.2 %glu_6.1 = (bf16[2048,512]{1,0:T(8,128)(2,1)}, bf16[2048,1024]{1,0:T(8,128)(2,1)}, bf16[4,1024,1024]{2,1,0:T(8,128)(2,1)}) custom-call(bf16[2048,2048]{1,0:T(8,128)(2,1)} %get-tuple-element.84.x_ref, bf16[2048,2048]{1,0:T(8,128)(2,1)} %get-tuple-element.82.df_hbm.df_ref, bf16[2048,1024]{1,0:T(8,128)(2,1)} %bitcast.48, ...), custom_call_target="tpu_custom_call" | custom-call | bytes 1024 | tf_op jit(solution)/shard_map/glu_6/pallas_call | solution.py:1485
  339.3 50.7 %product_scatter_8.1 = f32[256,2048]{1,0:T(8,128)} custom-call(bf16[2048,1024]{1,0:T(8,128)(2,1)} %get-tuple-element.83.refs_0_, bf16[2048,1024]{1,0:T(8,128)(2,1)} %get-tuple-element.87.refs_1_, bf16[2048,1024]{1,0:T(8,128)(2,1)} %bitcast.47, bf16[2048,1024]{1,0:T(8,128)(2,1)} %bitcast.49), custom_call_target="tpu_custom_call" | custom-call | bytes 1024 | tf_op jit(solution)/shard_map/product_scatter_8/pallas_call | solution.py:1064
  390.0 2.3 multiply_reduce_fusion
  392.5 1.7 multiply_convert_fusion.refs_0_
  394.2 89.6 %attend_back_9.1 = (f32[256,2048]{1,0:T(8,128)}, bf16[2048,640]{1,0:T(8,128)(2,1)}, f32[8,128]{1,0:T(8,128)}) custom-call(bf16[256,2048]{1,0:T(8,128)(2,1)} %multiply_convert_fusion.refs_0_, bf16[2048,384]{1,0:T(8,128)(2,1)} %bitcast.53, bf16[256,2048]{1,0:T(8,128)(2,1)} %get-tuple-element.76.refs_2_, f32[2048,128]{1,0:T(8,128)} %copy.56.refs_3_, ...), custom_call_target="tpu_custom_call" | custom-call | bytes 1024 | tf_op jit(solution)/shard_map/attend_back_9/pallas_call | solution.py:1034
  483.8 1.4 scatter_custom_fusion
  487.6 3.6 fusion.5
  491.2 2.7 gather_fusion.2
  493.9 51.4 %last_7.1 = (bf16[256,2048]{1,0:T(8,128)(2,1)}, bf16[64,8192]{1,0:T(8,128)(2,1)}) custom-call(f32[256,2048]{1,0:T(8,128)} %copy-done.2, f32[256,1]{1,0:T(8,128)} %copy.60.refs_1_, bf16[2048,512]{1,0:T(8,128)(2,1)} %get-tuple-element.100.refs_2_, bf16[2048,512]{1,0:T(8,128)(2,1)} %get-tuple-element.101.refs_3_, ...), custom_call_target="tpu_custom_call" | custom-call | bytes 1024 | tf_op jit(solution)/shard_map/last_7/pallas_call | solution.py:1601
  547.3 2.3 gather_fusion.3
  549.6 17.6 %exchange_half_11.1 = (bf16[64,8192]{1,0:T(8,128)(2,1)}, f32[1,1024]{1,0:T(1,128)}) custom-call(bf16[1024,1024]{1,0:T(8,128)(2,1)} %bitcast.50), custom_call_target="tpu_custom_call" | custom-call | bytes 1024 | tf_op jit(solution)/shard_map/exchange_half_11/pallas_call | solution.py:206
  569.9 7.2 %reduce-scatter.8.cloned.1.call-done.blocks_ref = bf16[8,64,640]{2,1,0:T(8,128)(2,1)} async-done(((bf16[8,256,640]{2,1,0:T(8,128)(2,1)}), bf16[8,64,640]{2,1,0:T(8,128)(2,1)}) %reduce-scatter.8.cloned.1.call-update) | async-done | bytes 655376 | tf_op jit(solution)/shard_map/reduce_scatter | solution.py:1756
  577.7 14.0 %sum_everywhere_13.1 = (f32[40,128]{1,0:T(8,128)}, f32[8,128]{1,0:T(8,128)}, bf16[64,3072]{1,0:T(8,128)(2,1)}, bf16[64,2048]{1,0:T(8,128)(2,1)}) custom-call(f32[40,128]{1,0:T(8,128)} %pad_bitcast_fusion.x_ref, bf16[8,64,640]{2,1,0:T(8,128)(2,1)} %reduce-scatter.8.cloned.1.call-done.blocks_ref), custom_call_target="tpu_custom_call" | custom-call | bytes 1024 | tf_op jit(solution)/shard_map/sum_everywhere_13/pallas_call | solution.py:356
  593.0 2.0 multiply_subtract_fusion
  595.0 17.4 %adam_matrices.1 = (f32[64,3072]{1,0:T(8,128)}, f32[64,2048]{1,0:T(8,128)}, f32[64,16384]{1,0:T(8,128)}, f32[256,2048]{1,0:T(8,128)}, f32[64,3072]{1,0:T(8,128)}...) custom-call(f32[8,128]{1,0:T(8,128)} %get-tuple-element.114.norm_ref, ...), custom_call_target="tpu_custom_call" | custom-call | tf_op jit(solution)/shard_map/adam_matrices/pallas_call | solution.py:1737
  (111 shorter events, 21.8 us)
Async XLA Ops:
  7.2 8.8 %copy-start = (bf16[256,2048]{1,0:T(8,128)(2,1)S(1)}, bf16[256,2048]{1,0:T(8,128)(2,1)}, u32[]{:S(2)}) copy-start(bf16[256,2048]{1,0:T(8,128)(2,1)} %param.20) | copy-start | bytes 3145732
  7.2 3.0 copy-start.18
  7.2 3.9 copy-start.14
  7.2 4.6 copy-start.13
  7.2 128.0 %all-gather.4.cloned.1.call-start = ((), (), s32[]{:S(2)}) async-start(), calls=%async_computation.3 | async-start | bytes 5242880 | tf_op jit(solution)/shard_map/all_gather | solution.py:1815
  10.2 229.6 %all-gather.6.cloned.1.call-start = ((), (), s32[]{:S(2)}) async-start(), calls=%async_computation.4 | async-start | bytes 5242880 | tf_op jit(solution)/shard_map/all_gather | solution.py:1827
  12.2 3.7 copy-start.19
  17.3 117.9 %copy-start.8 = (bf16[256,2048]{1,0:T(8,128)(2,1)}, bf16[256,2048]{1,0:T(8,128)(2,1)S(1)}, u32[]{:S(2)}) copy-start(bf16[256,2048]{1,0:T(8,128)(2,1)S(1)} %gather_fusion) | copy-start | bytes 3145732
  19.7 116.4 %copy-start.15 = (f32[4224]{0:T(1024)S(1)}, f32[4224]{0:T(1024)}, u32[]{:S(2)}) copy-start(f32[4224]{0:T(1024)} %param.27) | copy-start | bytes 50692
  19.7 116.7 %copy-start.3 = (bf16[256,2048]{1,0:T(8,128)(2,1)S(1)}, bf16[256,2048]{1,0:T(8,128)(2,1)}, u32[]{:S(2)}) copy-start(bf16[256,2048]{1,0:T(8,128)(2,1)} %param.19) | copy-start | bytes 3145732
  135.3 162.7 %all-gather.8.cloned.1.call-start = ((), (), s32[]{:S(2)}) async-start(), calls=%async_computation.5 | async-start | bytes 5242880 | tf_op jit(solution)/shard_map/all_gather | solution.py:1828
  136.0 258.2 %reduce-scatter.4.cloned.1.call-start = ((), (), s32[]{:S(2)}) async-start(), calls=%async_computation.6 | async-start | bytes 5242880 | tf_op jit(solution)/shard_map/reduce_scatter | solution.py:1756
  137.7 7.1 %copy-start.5 = (bf16[256,2048]{1,0:T(8,128)(2,1)}, bf16[256,2048]{1,0:T(8,128)(2,1)S(1)}, u32[]{:S(2)}) copy-start(bf16[256,2048]{1,0:T(8,128)(2,1)S(1)} %gather_fusion.1) | copy-start | bytes 3145732
  146.1 90.1 %copy-start.6 = (bf16[256,2048]{1,0:T(8,128)(2,1)S(1)}, bf16[256,2048]{1,0:T(8,128)(2,1)}, u32[]{:S(2)}) copy-start(bf16[256,2048]{1,0:T(8,128)(2,1)} %copy-done.5) | copy-start | bytes 3145732
  238.3 154.0 %copy-start.2 = (f32[256,2048]{1,0:T(8,128)}, f32[256,2048]{1,0:T(8,128)S(1)}, u32[]{:S(2)}) copy-start(f32[256,2048]{1,0:T(8,128)S(1)} %get-tuple-element.142.refs_0_) | copy-start | bytes 6291460
  298.0 249.3 %reduce-scatter.6.cloned.1.call-start = ((), (), s32[]{:S(2)}) async-start(), calls=%async_computation.7 | async-start | bytes 10485760 | tf_op jit(solution)/shard_map/reduce_scatter | solution.py:1756
  339.3 237.8 %reduce-scatter.8.cloned.1.call-start = ((), (), s32[]{:S(2)}) async-start(), calls=%async_computation.8 | async-start | bytes 3276800 | tf_op jit(solution)/shard_map/reduce_scatter | solution.py:1756
  390.0 2.3 copy-start.7
  390.0 2.5 copy-start.9
  483.7 2.3 copy-start.10
  493.9 51.4 %copy-start.12 = (bf16[8,64,1024]{2,1,0:T(8,128)(2,1)S(1)}, bf16[8,64,1024]{2,1,0:T(8,128)(2,1)}, u32[]{:S(2)}) copy-start(bf16[8,64,1024]{2,1,0:T(8,128)(2,1)} %reduce-scatter.4.cloned.1.call-done) | copy-start | bytes 3145732
  549.6 43.4 %copy-start.16 = (f32[4224]{0:T(1024)S(1)}, f32[4224]{0:T(1024)}, u32[]{:S(2)}) copy-start(f32[4224]{0:T(1024)} %param.32) | copy-start | bytes 50692
  549.6 43.4 %copy-start.17 = (f32[4224]{0:T(1024)S(1)}, f32[4224]{0:T(1024)}, u32[]{:S(2)}) copy-start(f32[4224]{0:T(1024)} %param.37) | copy-start | bytes 50692
  595.0 17.4 %copy-start.1 = (bf16[256,2048]{1,0:T(8,128)(2,1)S(1)}, bf16[256,2048]{1,0:T(8,128)(2,1)}, u32[]{:S(2)}) copy-start(bf16[256,2048]{1,0:T(8,128)(2,1)} %param.20) | copy-start | bytes 3145732
  (2 other events, 3.6 us)
Sparse Core Ops, SparseCore 0:
  10.3 113.3 all-gather.3
  135.4 80.7 all-gather.5
  217.8 79.2 all-gather.7
  299.2 75.2 reduce-scatter.3
  376.9 144.9 reduce-scatter.5
  524.2 52.8 reduce-scatter.7

commit v3 on v2

--- a/solution.py
+++ b/solution.py
@@ -1084,7 +1084,7 @@
     nd,
     qkv_ref,
     out_rows_ref,
-    wide_ref,
+    wide_hbm,
     df_ref,
     note_ref,
     own_qkv_ref,
@@ -1104,6 +1104,9 @@
     piece_recv,
     line_send,
     line_recv,
+    wide_full,
+    wide_ref,
+    wide_sem,
 ):
     me, line = lax.axis_index("fsdp"), lax.axis_index("dp")
     others = plane_others(me)
@@ -1111,12 +1114,16 @@
     half_width = half_a_ref.shape[2] // 2
     hidden = 2 * half_width
     whole = hidden * PLANE
+    fetch = pltpu.make_async_copy(wide_hbm, wide_full, wide_sem)
+    fetch.start()
     gather = Gather(df_ref, df_all_ref, gather_send, gather_recv)
     greet_line(nd, others)
 
     def line_spot(array, owner):
         rows = pl.ds(pl.multiple_of(owner * count, count), count)
-        return own_qkv_ref.at[:, rows] if array == 0 else own_out_ref.at[rows]
+        if array == 1:
+            return own_out_ref.at[rows]
+        return own_qkv_ref.at[pl.ds(array // 2 * (PLANE // 2), PLANE // 2), rows]
 
     def along(array, owner, side, source=None):
         spot = line_spot(array, owner)
@@ -1198,15 +1205,18 @@
 
     own_block = own_qkv_ref.at[me, pl.ds(pl.multiple_of(line * count, count), count)]
     rows = df_ref.shape[0]
-    kept = [
-        (qkv_ref.at[me], own_block),
-        (out_rows_ref, line_spot(1, line)),
-        (note_ref, notes_ref.at[me]),
-        (df_ref, df_all_ref.at[pl.ds(pl.multiple_of(me * rows, rows), rows)]),
-    ] + list(pieces(me))
+
+    def local(index, source, target):
+        return pltpu.make_async_copy(source, target, own_sem.at[index])
+
     keep = [
-        pltpu.make_async_copy(source, target, own_sem.at[index])
-        for index, (source, target) in enumerate(kept)
+        local(0, qkv_ref.at[me], own_block),
+        local(1, out_rows_ref, line_spot(1, line)),
+        local(2, note_ref, notes_ref.at[me]),
+        local(3, df_ref, df_all_ref.at[pl.ds(pl.multiple_of(me * rows, rows), rows)]),
+    ]
+    keep_pieces = [
+        local(4 + index, source, target) for index, (source, target) in enumerate(pieces(me))
     ]
     order = (6, 7, 2, 4, 3, 5, 1)
     for number in order:
@@ -1221,13 +1231,21 @@
         put_block(number).wait_recv()
     keep[0].wait()
     send_own(0)
+    send_own(2)
+    fetch.wait()
+
+    @pl.loop(0, wide_full.shape[1] // TILE)
+    def _(step):
+        columns = pl.ds(pl.multiple_of(step * TILE, TILE), TILE)
+        wide_ref[:, columns] = wide_full[:, columns].astype(wide_ref.dtype)
+
     for steps, slots in (
         ((), (0, 2)),
         (((1, 1),), (4, 1, 3)),
-        (((0, 1),), (5, 6)),
+        (((0, 1), (2, 1)), (5, 6)),
         (((1, 2),), ()),
-        (((0, 2),), (7, 9, 8, 10)),
-        (((1, 3), (0, 3)), (11, 12)),
+        (((0, 2), (2, 2)), (7, 9, 8, 10)),
+        (((1, 3), (0, 3), (2, 3)), (11, 12)),
     ):
         for array, step in steps:
             if step < nd:
@@ -1238,18 +1256,20 @@
             for number in order:
                 for copy in put_pieces(number):
                     copy.start()
+            for copy in keep_pieces:
+                copy.start()
     for step in range(4, nd):
-        line_step(1, step)
-        line_step(0, step)
+        for array in (1, 0, 2):
+            line_step(array, step)
     for number in order:
         put_block(number).wait_send()
         put_note(number).wait()
         for copy in put_pieces(number):
             copy.wait()
     gather.finish()
-    for copy in keep[1:]:
+    for copy in keep[1:] + keep_pieces:
         copy.wait()
-    for array in (1, 0):
+    for array in (1, 0, 2):
         source = out_rows_ref if array == 1 else None
 
         @pl.when(line < nd - 1)
@@ -1275,7 +1295,7 @@
     nd = lax.axis_size("dp")
     count, whole = wide_rows.shape
     half = whole // 4 // PLANE
-    low = wide_rows.dtype
+    low = jnp.bfloat16
     return pl.pallas_call(
         functools.partial(start_kernel, nd),
         out_shape=[
@@ -1292,8 +1312,15 @@
         + gather_scratch()
         + [pltpu.SemaphoreType.DMA((PLANE,))] * 4
         + [pltpu.SemaphoreType.DMA((4 * PLANE,))] * 2
-        + [pltpu.SemaphoreType.DMA((2, 2, nd)), pltpu.SemaphoreType.DMA((2, nd))],
-        compiler_params=pltpu.CompilerParams(collective_id=number, has_side_effects=True),
+        + [pltpu.SemaphoreType.DMA((3, 2, nd)), pltpu.SemaphoreType.DMA((3, nd))]
+        + [
+            pltpu.VMEM(wide_rows.shape, wide_rows.dtype),
+            pltpu.VMEM(wide_rows.shape, low),
+            pltpu.SemaphoreType.DMA,
+        ],
+        compiler_params=pltpu.CompilerParams(
+            collective_id=number, has_side_effects=True, vmem_limit_bytes=56 * 2**20
+        ),
         cost_estimate=SHORT,
         name=f"start_{number}",
     )(qkv_blocks, out_rows, wide_rows, df_own, note)
@@ -1816,7 +1843,7 @@
     own_qkv, own_out, half_a, half_b, down_back, notes = start(
         qkv_blocks,
         w_out.astype(low),
-        w_gate_up.astype(low),
+        w_gate_up,
         (valid_col * back_rows).astype(low),
         jnp.pad(lengths, ((0, 8 - MB), (0, 128 - SEQS))),
         1,

time: 628 us -> 626 us (level)
  transfers between devices with their start and end apart: 6 -> 6, of which waited for: 1 -> 1; matrix products, arithmetic and copies ran while one was open for 7% -> 6% of each run, Pallas kernels for 83% -> 84%
where the time goes in v3:
time: 626 us; the launch traced here: 617 us
  Pallas kernels  548 us (88%)
  other arithmetic  27.8 us (4%)
  local copies, waits for them, and re-layouts  18.1 us (3%)
  between operations  16.4 us (3%)
  waiting for transfers between devices  6.83 us (1%)
    pallas_call x1, Pallas kernels, start(): pl.pallas_call(functools.partial(start_kernel, nd), out_shape=[jax.ShapeD...  118 us
    pallas_call x1, Pallas kernels, attend_back(): pl.pallas_call(staged(attend_back_kernel, len(arrays), places), out_shape...  90.2 us
    pallas_call x1, Pallas kernels, attend(): pl.pallas_call(staged(attend_kernel, len(arrays), places), out_shape=[jax...  88.6 us
    pallas_call x1, Pallas kernels, gather_glu(): pl.pallas_call(gather_glu_kernel, out_shape=[jax.ShapeDtypeStruct((count,...  58.8 us
    pallas_call x1, Pallas kernels, last(): pl.pallas_call(staged(last_kernel, len(arrays) + 1, places), out_shape=[j...  51.2 us
    pallas_call x1, Pallas kernels, product_scatter(): pl.pallas_call(functools.partial(scatter_kernel, turned, len(left_sides))...  50.6 us
    pallas_call x1, Pallas kernels, glu(): pl.pallas_call(glu_kernel, grid=(count // step,), out_shape=[jax.ShapeDty...  41.2 us
    pallas_call x1, Pallas kernels, exchange_half(): pl.pallas_call(columns_kernel, out_shape=[jax.ShapeDtypeStruct((count, ha...  17.7 us
  transfers between devices with their start and end apart: 6, of which 1 were waited for; matrix products, arithmetic and copies ran while one was open for 6% of the time, Pallas kernels for 84%

profile of v3, /device:TPU:0, one launch (start us, length us, event | category | flops | bytes accessed | tf_op | source)
XLA Modules:
  0.0 617.2 jit_solution(18367881811038126174)
XLA Ops:
  7.3 2.9 convert_element_type.86
  12.3 1.4 gather_fusion
  16.0 118.0 %start_1.1 = (bf16[8,256,384]{2,1,0:T(8,128)(2,1)}, bf16[256,2048]{1,0:T(8,128)(2,1)}, bf16[8,64,1024]{2,1,0:T(8,128)(2,1)}, bf16[8,64,1024]{2,1,0:T(8,128)(2,1)...) custom-call(bf16[8,64,384]{2,1,0:T(8,128)(2,1)} %pad_maximum_fusion.qkv_ref, ...), custom_call_target="tpu_custom_call" | custom-call | bytes 1024 | tf_op jit(solution)/shard_map/start_1/pallas_call | solution.py:1299
  135.3 1.4 gather_fusion.1
  142.4 1.3 and_convert_fusion.refs_5_
  145.0 88.6 %attend_3.1 = (f32[256,2048]{1,0:T(8,128)}, bf16[2048,2048]{1,0:T(8,128)(2,1)}, f32[2048,384]{1,0:T(8,128)}, bf16[2048,256]{1,0:T(8,128)(2,1)}, bf16[2048,128]{1...) custom-call(bf16[256,2048]{1,0:T(8,128)(2,1)} %fusion.2.refs_0_, ...), custom_call_target="tpu_custom_call" | custom-call | bytes 1024 | tf_op jit(solution)/shard_map/attend_3/pallas_call | solution.py:988
  233.6 2.1 multiply_reduce_fusion.3
  235.7 1.4 multiply_convert_fusion.1.x_ref
  237.2 58.8 %gather_glu_5.1 = (bf16[2048,2048]{1,0:T(8,128)(2,1)}, bf16[2048,512]{1,0:T(8,128)(2,1)}, bf16[2048,1024]{1,0:T(8,128)(2,1)}, bf16[512,2048]{1,0:T(8,128)(2,1)}, bf16[2048,1024]{1,0:T(8,128)(2,1)}) custom-call(bf16[256,2048]{1,0:T(8,128)(2,1)} %multiply_convert_fusion.1.x_ref, bf16[2048,1024]{1,0:T(8,128)(2,1)} %bitcast.46, ...), custom_call_target="tpu_custom_call" | custom-call | bytes 1024 | tf_op jit(solution)/shard_map/gather_glu_5/pallas_call | solution.py:1441
  296.1 41.2 %glu_6.1 = (bf16[2048,512]{1,0:T(8,128)(2,1)}, bf16[2048,1024]{1,0:T(8,128)(2,1)}, bf16[4,1024,1024]{2,1,0:T(8,128)(2,1)}) custom-call(bf16[2048,2048]{1,0:T(8,128)(2,1)} %get-tuple-element.84.x_ref, bf16[2048,2048]{1,0:T(8,128)(2,1)} %get-tuple-element.82.df_hbm.df_ref, bf16[2048,1024]{1,0:T(8,128)(2,1)} %bitcast.48, ...), custom_call_target="tpu_custom_call" | custom-call | bytes 1024 | tf_op jit(solution)/shard_map/glu_6/pallas_call | solution.py:1512
  337.4 50.6 %product_scatter_8.1 = f32[256,2048]{1,0:T(8,128)} custom-call(bf16[2048,1024]{1,0:T(8,128)(2,1)} %get-tuple-element.83.refs_0_, bf16[2048,1024]{1,0:T(8,128)(2,1)} %get-tuple-element.87.refs_1_, bf16[2048,1024]{1,0:T(8,128)(2,1)} %bitcast.47, bf16[2048,1024]{1,0:T(8,128)(2,1)} %bitcast.49), custom_call_target="tpu_custom_call" | custom-call | bytes 1024 | tf_op jit(solution)/shard_map/product_scatter_8/pallas_call | solution.py:1064
  388.0 2.3 multiply_reduce_fusion
  390.5 1.7 multiply_convert_fusion.refs_0_
  392.2 90.2 %attend_back_9.1 = (f32[256,2048]{1,0:T(8,128)}, bf16[2048,640]{1,0:T(8,128)(2,1)}, f32[8,128]{1,0:T(8,128)}) custom-call(bf16[256,2048]{1,0:T(8,128)(2,1)} %multiply_convert_fusion.refs_0_, bf16[2048,384]{1,0:T(8,128)(2,1)} %bitcast.53, bf16[256,2048]{1,0:T(8,128)(2,1)} %get-tuple-element.76.refs_2_, f32[2048,128]{1,0:T(8,128)} %copy.56.refs_3_, ...), custom_call_target="tpu_custom_call" | custom-call | bytes 1024 | tf_op jit(solution)/shard_map/attend_back_9/pallas_call | solution.py:1034
  482.5 1.4 scatter_custom_fusion
  486.3 3.6 fusion.5
  489.9 2.7 gather_fusion.2
  492.6 51.2 %last_7.1 = (bf16[256,2048]{1,0:T(8,128)(2,1)}, bf16[64,8192]{1,0:T(8,128)(2,1)}) custom-call(f32[256,2048]{1,0:T(8,128)} %copy-done.2, f32[256,1]{1,0:T(8,128)} %copy.60.refs_1_, bf16[2048,512]{1,0:T(8,128)(2,1)} %get-tuple-element.100.refs_2_, bf16[2048,512]{1,0:T(8,128)(2,1)} %get-tuple-element.101.refs_3_, ...), custom_call_target="tpu_custom_call" | custom-call | bytes 1024 | tf_op jit(solution)/shard_map/last_7/pallas_call | solution.py:1628
  545.9 2.3 gather_fusion.3
  548.2 17.7 %exchange_half_11.1 = (bf16[64,8192]{1,0:T(8,128)(2,1)}, f32[1,1024]{1,0:T(1,128)}) custom-call(bf16[1024,1024]{1,0:T(8,128)(2,1)} %bitcast.50), custom_call_target="tpu_custom_call" | custom-call | bytes 1024 | tf_op jit(solution)/shard_map/exchange_half_11/pallas_call | solution.py:206
  568.5 6.0 reduce-scatter.8.cloned.1.call-done.blocks_ref
  575.2 14.0 %sum_everywhere_13.1 = (f32[40,128]{1,0:T(8,128)}, f32[8,128]{1,0:T(8,128)}, bf16[64,3072]{1,0:T(8,128)(2,1)}, bf16[64,2048]{1,0:T(8,128)(2,1)}) custom-call(f32[40,128]{1,0:T(8,128)} %pad_bitcast_fusion.x_ref, bf16[8,64,640]{2,1,0:T(8,128)(2,1)} %reduce-scatter.8.cloned.1.call-done.blocks_ref), custom_call_target="tpu_custom_call" | custom-call | bytes 1024 | tf_op jit(solution)/shard_map/sum_everywhere_13/pallas_call | solution.py:356
  590.5 2.0 multiply_subtract_fusion
  592.5 17.4 %adam_matrices.1 = (f32[64,3072]{1,0:T(8,128)}, f32[64,2048]{1,0:T(8,128)}, f32[64,16384]{1,0:T(8,128)}, f32[256,2048]{1,0:T(8,128)}, f32[64,3072]{1,0:T(8,128)}...) custom-call(f32[8,128]{1,0:T(8,128)} %get-tuple-element.114.norm_ref, ...), custom_call_target="tpu_custom_call" | custom-call | tf_op jit(solution)/shard_map/adam_matrices/pallas_call | solution.py:1764
  (110 shorter events, 20.6 us)
Async XLA Ops:
  7.2 5.1 copy-start
  7.2 3.0 copy-start.18
  7.2 3.9 copy-start.14
  7.2 4.6 copy-start.13
  7.2 126.8 %all-gather.4.cloned.1.call-start = ((), (), s32[]{:S(2)}) async-start(), calls=%async_computation.3 | async-start | bytes 5242880 | tf_op jit(solution)/shard_map/all_gather | solution.py:1842
  10.2 2.1 copy-start.19
  10.2 227.0 %all-gather.6.cloned.1.call-start = ((), (), s32[]{:S(2)}) async-start(), calls=%async_computation.4 | async-start | bytes 5242880 | tf_op jit(solution)/shard_map/all_gather | solution.py:1854
  13.7 120.4 %copy-start.8 = (bf16[256,2048]{1,0:T(8,128)(2,1)}, bf16[256,2048]{1,0:T(8,128)(2,1)S(1)}, u32[]{:S(2)}) copy-start(bf16[256,2048]{1,0:T(8,128)(2,1)S(1)} %gather_fusion) | copy-start | bytes 3145732
  134.1 162.0 %all-gather.8.cloned.1.call-start = ((), (), s32[]{:S(2)}) async-start(), calls=%async_computation.5 | async-start | bytes 5242880 | tf_op jit(solution)/shard_map/all_gather | solution.py:1855
  134.8 257.4 %reduce-scatter.4.cloned.1.call-start = ((), (), s32[]{:S(2)}) async-start(), calls=%async_computation.6 | async-start | bytes 5242880 | tf_op jit(solution)/shard_map/reduce_scatter | solution.py:1783
  136.6 7.1 %copy-start.5 = (bf16[256,2048]{1,0:T(8,128)(2,1)}, bf16[256,2048]{1,0:T(8,128)(2,1)S(1)}, u32[]{:S(2)}) copy-start(bf16[256,2048]{1,0:T(8,128)(2,1)S(1)} %gather_fusion.1) | copy-start | bytes 3145732
  145.0 88.6 %copy-start.6 = (bf16[256,2048]{1,0:T(8,128)(2,1)S(1)}, bf16[256,2048]{1,0:T(8,128)(2,1)}, u32[]{:S(2)}) copy-start(bf16[256,2048]{1,0:T(8,128)(2,1)} %copy-done.5) | copy-start | bytes 3145732
  235.7 154.6 %copy-start.2 = (f32[256,2048]{1,0:T(8,128)}, f32[256,2048]{1,0:T(8,128)S(1)}, u32[]{:S(2)}) copy-start(f32[256,2048]{1,0:T(8,128)S(1)} %get-tuple-element.142.refs_0_) | copy-start | bytes 6291460
  296.0 249.9 %reduce-scatter.6.cloned.1.call-start = ((), (), s32[]{:S(2)}) async-start(), calls=%async_computation.7 | async-start | bytes 10485760 | tf_op jit(solution)/shard_map/reduce_scatter | solution.py:1783
  337.3 237.2 %reduce-scatter.8.cloned.1.call-start = ((), (), s32[]{:S(2)}) async-start(), calls=%async_computation.8 | async-start | bytes 3276800 | tf_op jit(solution)/shard_map/reduce_scatter | solution.py:1783
  388.0 2.3 copy-start.7
  388.0 2.5 copy-start.9
  482.5 2.3 copy-start.10
  484.7 1.6 copy-start.11
  492.6 51.2 %copy-start.12 = (bf16[8,64,1024]{2,1,0:T(8,128)(2,1)S(1)}, bf16[8,64,1024]{2,1,0:T(8,128)(2,1)}, u32[]{:S(2)}) copy-start(bf16[8,64,1024]{2,1,0:T(8,128)(2,1)} %reduce-scatter.4.cloned.1.call-done) | copy-start | bytes 3145732
  543.8 2.0 copy-start.4
  548.2 42.3 %copy-start.16 = (f32[4224]{0:T(1024)S(1)}, f32[4224]{0:T(1024)}, u32[]{:S(2)}) copy-start(f32[4224]{0:T(1024)} %param.32) | copy-start | bytes 50692
  548.2 42.3 %copy-start.17 = (f32[4224]{0:T(1024)S(1)}, f32[4224]{0:T(1024)}, u32[]{:S(2)}) copy-start(f32[4224]{0:T(1024)} %param.37) | copy-start | bytes 50692
  592.5 17.4 %copy-start.1 = (bf16[256,2048]{1,0:T(8,128)(2,1)S(1)}, bf16[256,2048]{1,0:T(8,128)(2,1)}, u32[]{:S(2)}) copy-start(bf16[256,2048]{1,0:T(8,128)(2,1)} %param.20) | copy-start | bytes 3145732
  (2 other events, 2.1 us)
Sparse Core Ops, SparseCore 0:
  10.3 115.0 all-gather.3
  134.2 79.3 all-gather.5
  215.2 79.2 all-gather.7
  296.7 75.3 reduce-scatter.3
  374.4 144.9 reduce-scatter.5
  521.7 52.8 reduce-scatter.7

commit v4 on v3

--- a/solution.py
+++ b/solution.py
@@ -1234,10 +1234,17 @@
     send_own(2)
     fetch.wait()
 
-    @pl.loop(0, wide_full.shape[1] // TILE)
+    part_width = half_width // nd
+
+    @pl.loop(0, 2 * PLANE)
     def _(step):
-        columns = pl.ds(pl.multiple_of(step * TILE, TILE), TILE)
-        wide_ref[:, columns] = wide_full[:, columns].astype(wide_ref.dtype)
+        for owner in range(nd):
+            for half in range(2):
+                first = step * hidden + (2 * owner + half) * part_width
+                target = step * hidden + half * half_width + owner * part_width
+                columns = pl.ds(pl.multiple_of(first, 128), part_width)
+                target = pl.ds(pl.multiple_of(target, 128), part_width)
+                wide_ref[:, target] = wide_full[:, columns].astype(wide_ref.dtype)
 
     for steps, slots in (
         ((), (0, 2)),
@@ -1469,43 +1476,68 @@
 
 
 def glu_kernel(
-    x_ref, df_ref, wgu_ref, wd_ref, first_ref, act_ref, dgu_ref, grad_ref, down_sum, wide_sum
+    x_ref,
+    df_ref,
+    first_ref,
+    both_hbm,
+    act_ref,
+    dgu_ref,
+    grad_ref,
+    wgu_ref,
+    wd_ref,
+    down_sum,
+    wide_sum,
+    sems,
 ):
     step = pl.program_id(0)
     half = wd_ref.shape[0]
+    nd, _, both = grad_ref.shape
+    count, units = wide_sum.shape[0] // PLANE // nd, half // nd
 
     @pl.when(step == 0)
     def _():
+        copies = []
+        for owner in range(nd):
+            for place in range(PLANE):
+                source = both_hbm.at[owner, pl.ds(place * count, count)]
+                target = wgu_ref.at[pl.ds((place * nd + owner) * count, count)]
+                copies.append(pltpu.make_async_copy(source, target, sems.at[owner, place]))
+            for side in range(2):
+                source = both_hbm.at[owner, pl.ds(PLANE * count + side * units, units)]
+                target = wd_ref.at[pl.ds(owner * units, units), pl.ds(side * both, both)]
+                copies.append(
+                    pltpu.make_async_copy(source, target, sems.at[owner, PLANE + side])
+                )
+        for copy in copies:
+            copy.start()
         down_sum[...] = jnp.zeros_like(down_sum)
         wide_sum[...] = jnp.zeros_like(wide_sum)
-
-    glu_block(
-        x_ref, df_ref, wgu_ref, wd_ref, act_ref, dgu_ref, down_sum, wide_sum
-    )
+        for copy in copies:
+            copy.wait()
+
+    glu_block(x_ref, df_ref, wgu_ref, wd_ref, act_ref, dgu_ref, down_sum, wide_sum)
 
     @pl.when(step == pl.num_programs(0) - 1)
     def _():
-        nd, _, both = grad_ref.shape
-        count, units = wide_sum.shape[0] // PLANE // nd, 2 * half // nd
         low = grad_ref.dtype
         for owner in range(nd):
             for place in range(PLANE):
                 first = (place * nd + owner) * count
                 part = wide_sum[first : first + count, :].astype(low)
                 grad_ref[owner, place * count : (place + 1) * count, :] = part
-            source, first = first_ref, owner * units
-            if first >= half:
-                source, first = down_sum, first - half
+            spot = slice(owner * units, (owner + 1) * units)
             for side in range(2):
-                part = source[first : first + units, side * both : (side + 1) * both].astype(low)
-                start = PLANE * count + side * units
-                grad_ref[owner, start : start + units, :] = part
-
-
-def glu(rows_all, df_all, wgu, own_down, down_first, number):
+                columns = slice(side * both, (side + 1) * both)
+                start = PLANE * count + side * 2 * units
+                grad_ref[owner, start : start + units, :] = first_ref[spot, columns]
+                part = down_sum[spot, columns].astype(low)
+                grad_ref[owner, start + units : start + 2 * units, :] = part
+
+
+def glu(rows_all, df_all, gathered, down_first, number):
     nd = lax.axis_size("dp")
     count, width = rows_all.shape
-    half = wgu.shape[1] // 2
+    half, both = down_first.shape[0], gathered.shape[2]
     low = jnp.bfloat16
     step = 512
     once = pl.Buffered(1)
@@ -1516,13 +1548,14 @@
             jax.ShapeDtypeStruct((count, half), low),
             jax.ShapeDtypeStruct((count, 2 * half), low),
             jax.ShapeDtypeStruct((nd, 2 * width // nd, 2 * half), low),
+            jax.ShapeDtypeStruct((width, both), low),
+            jax.ShapeDtypeStruct((half, width), low),
         ],
         in_specs=[
             pl.BlockSpec((step, width), lambda i: (i, 0)),
             pl.BlockSpec((step, width), lambda i: (i, 0)),
-            pl.BlockSpec((width, 2 * half), lambda i: (0, 0), pipeline_mode=once),
-            pl.BlockSpec((half, width), lambda i: (1, 0), pipeline_mode=once),
             pl.BlockSpec((half, width), lambda i: (0, 0), pipeline_mode=once),
+            ANY,
         ],
         out_specs=[
             pl.BlockSpec((step, half), lambda i: (i, 0)),
@@ -1530,15 +1563,18 @@
             pl.BlockSpec(
                 (nd, 2 * width // nd, 2 * half), lambda i: (0, 0, 0), pipeline_mode=once
             ),
+            pl.BlockSpec((width, both), lambda i: (0, 0), pipeline_mode=once),
+            pl.BlockSpec((half, width), lambda i: (0, 0), pipeline_mode=once),
         ],
         scratch_shapes=[
             pltpu.VMEM((half, width), jnp.float32),
             pltpu.VMEM((width, 2 * half), jnp.float32),
+            pltpu.SemaphoreType.DMA((nd, PLANE + 2)),
         ],
         compiler_params=pltpu.CompilerParams(vmem_limit_bytes=56 * 2**20),
         cost_estimate=SHORT,
         name=f"glu_{number}",
-    )(rows_all, df_all, wgu, own_down, down_first)
+    )(rows_all, df_all, down_first, gathered)
 
 
 def attention(normed_low, own_qkv, own_out, lengths_all, query_gain, key_gain):
@@ -1572,7 +1608,8 @@
     valid_ref,
     act_a_ref,
     act_b_ref,
-    wd_ref,
+    wd_a_ref,
+    wd_b_ref,
     half_ref,
     out_ref,
     wide_ref,
@@ -1583,14 +1620,7 @@
 ):
     others = plane_others(lax.axis_index("fsdp"))
     rows, width = out_ref.shape
-    half_rows = wd_ref.shape[0] // 2
-    block = block_product(
-        (act_a_ref, act_b_ref),
-        (wd_ref.at[pl.ds(0, half_rows)], wd_ref.at[pl.ds(half_rows, half_rows)]),
-        rows,
-        width,
-        False,
-    )
+    block = block_product((act_a_ref, act_b_ref), (wd_a_ref, wd_b_ref), rows, width, False)
     scatter = Scatter(sum_ref, block, refs)
     greet(others)
     order = (6, 7, 2, 4, 3, 5, 1)
@@ -1620,10 +1650,10 @@
         copy.wait()
 
 
-def last(hidden, valid_col, act_a, act_b, own_down, half, count, number):
+def last(hidden, valid_col, act_a, act_b, down_a, down_b, half, count, number):
     rows, width = hidden.shape
-    arrays = (hidden, valid_col, act_a, act_b, own_down)
-    places = (0, 2, 3, 4)
+    arrays = (hidden, valid_col, act_a, act_b, down_a, down_b)
+    places = (0, 2, 3, 4, 5)
     specs, stage = staged_specs(arrays, places)
     return pl.pallas_call(
         staged(last_kernel, len(arrays) + 1, places),
@@ -1703,13 +1733,14 @@
         which, rows, _, loops = chunks[number]
         for copy in fetch(number):
             copy.wait()
-        for array, grad_rows, steps, columns_of, grad_columns_of, width in loops:
+        for steps, parts in loops:
 
             @pl.loop(0, steps)
             def _(step):
-                columns = pl.ds(pl.multiple_of(columns_of(step), 128), width)
-                grad_columns = pl.ds(pl.multiple_of(grad_columns_of(step), 128), width)
-                update(which, rows, columns, grad_bufs[array][grad_rows, grad_columns])
+                for array, grad_rows, columns_of, grad_columns_of, width in parts:
+                    columns = pl.ds(pl.multiple_of(columns_of(step), 128), width)
+                    grad_columns = pl.ds(pl.multiple_of(grad_columns_of(step), 128), width)
+                    update(which, rows, columns, grad_bufs[array][grad_rows, grad_columns])
 
         for copy in put(number):
             copy.start()
@@ -1720,7 +1751,8 @@
 
 def adam_matrices(norm, grad_qkv, grad_out, grad_a, grad_b, sums_b, weights, firsts, seconds):
     half = grad_a.shape[1] // 2 // PLANE
-    whole = weights[2].shape[1] // 2
+    nd = lax.axis_size("dp")
+    unit = half // nd
     count = weights[3].shape[0]
     behind = sums_b.shape[0] - 2 * count
     side_width = sums_b.shape[1]
@@ -1732,14 +1764,18 @@
 
     for row in range(0, weights[2].shape[0], 16):
         rows = pl.ds(row, 16)
-        loops = []
+        parts = []
         for part in range(2):
-
-            def columns_of(step, part=part):
-                side, unit = lax.div(step, PLANE), lax.rem(step, PLANE)
-                return side * whole + unit * 2 * half + part * half
-
-            loops.append((2 + part, rows, 2 * PLANE, columns_of, lambda step: step * half, half))
+            for owner in range(nd):
+
+                def columns_of(step, part=part, owner=owner):
+                    return step * 2 * half + (2 * owner + part) * unit
+
+                def grad_columns_of(step, owner=owner):
+                    return step * half + owner * unit
+
+                parts.append((2 + part, rows, columns_of, grad_columns_of, unit))
+        loops = [(2 * PLANE, parts)]
         chunks.append((2, rows, [(2, rows), (3, rows)], loops))
     for row in range(0, count, 64):
         sources, loops = [], []
@@ -1750,13 +1786,13 @@
             def columns_of(step, side=side):
                 return side * side_width + step * width
 
-            loops.append((4, spot, side_width // width, columns_of, straight, width))
+            loops.append((side_width // width, [(4, spot, columns_of, straight, width)]))
         chunks.append((3, pl.ds(row, 64), sources, loops))
     for which in range(2):
         for row in range(0, weights[which].shape[0], 32):
             rows = pl.ds(row, 32)
             steps = weights[which].shape[1] // width
-            loops = [(which, rows, steps, straight, straight, width)]
+            loops = [(steps, [(which, rows, straight, straight, width)])]
             chunks.append((which, rows, [(which, rows)], loops))
     grads = (grad_qkv, grad_out, grad_a, grad_b, sums_b)
     per = len(weights)
@@ -1839,7 +1875,9 @@
         axis=2,
     )
     wide = q_width + 2 * HD
-    own_down = lax.all_gather(w_down.astype(low), "dp", axis=0, tiled=True)
+    down_low = w_down.astype(low)
+    units = down_low.shape[0] // 2
+    down_a = lax.all_gather(down_low[:units], "dp", axis=0, tiled=True)
     own_qkv, own_out, half_a, half_b, down_back, notes = start(
         qkv_blocks,
         w_out.astype(low),
@@ -1850,9 +1888,14 @@
     )
     own_qkv = own_qkv.reshape(D, wide)
     lengths_all = notes[:, :MB, :SEQS].reshape(nf * MB, SEQS)
-    half_a, own_down = lax.optimization_barrier((half_a, own_down))
+    half_a, down_a = lax.optimization_barrier((half_a, down_a))
     own_a = lax.all_gather(half_a, "dp", axis=1, tiled=True).reshape(D, hidden_own)
-    own_b = lax.all_gather(half_b, "dp", axis=1, tiled=True).reshape(D, hidden_own)
+    with_down = jnp.concatenate(
+        [half_b.reshape(nf * rows_own, hidden_own), down_low[units:, :hidden_own]]
+        + [down_low[units:, hidden_own:]],
+        axis=0,
+    )
+    gathered_b = lax.all_gather(with_down, "dp", axis=0)
 
     normed_one, norm_one_pull = jax.vjp(rms_norm, rows_in, attn_gain)
     attention_sums, attention_back = attention(
@@ -1861,11 +1904,11 @@
     hidden = rows_in + valid_col * attention_sums
 
     normed_two, norm_two_pull = jax.vjp(rms_norm, hidden, ffn_gain)
-    norm_two_all, act_a, back_a, down_a, part_a = gather_glu(
-        normed_two.astype(low), own_a, own_down, down_back, 5
+    norm_two_all, act_a, back_a, grad_down_a, part_a = gather_glu(
+        normed_two.astype(low), own_a, down_a, down_back, 5
     )
     sums_a = scatter_rows(part_a.reshape(nf, nd * rows_own, hidden_own), 1)
-    act_b, back_b, part_b = glu(norm_two_all, down_back, own_b, own_down, down_a, 6)
+    act_b, back_b, part_b, own_b, down_b = glu(norm_two_all, down_back, gathered_b, grad_down_a, 6)
     sums_b = scatter_rows(part_b, 0)[0]
     normed_two_grad = product_scatter((back_a, back_b), (own_a, own_b), 8, turned=True)
     hidden_norm_grad, ffn_gain_grad = norm_two_pull(normed_two_grad)
@@ -1881,7 +1924,8 @@
         valid_col,
         act_a,
         act_b,
-        own_down,
+        down_a,
+        down_b,
         sums_a.reshape(nf * rows_own, hidden_own),
         rows_own,
         7,
@@ -2194,7 +2238,7 @@
 
 def solution(mesh):
     nf, nd = mesh.shape["fsdp"], mesh.shape["dp"]
-    fits = nf == PLANE and KVH == PLANE and nd % 2 == 0
+    fits = nf == PLANE and KVH == PLANE and nd > 1 and FF // nf % (256 * nd) == 0
     per_device = per_device_plane if fits else per_device_plain
     in_specs = (
         P(("fsdp", "dp"), None),

time: 626 us -> 629 us (level)
  Pallas kernels: 548 us -> 518 us
  waiting for transfers between devices: 6.83 us -> 35.5 us
    pallas_call x1, Pallas kernels: 118 us -> 83.6 us  [start(): pl.pallas_call(functools.partial(start_kernel, nd), out_shape=[jax.ShapeD...]
    all_gather x2, waiting for transfers between devices: 0.04 us -> 32.7 us  [the longest x1 32.7 us: per_device_plane(): gathered_b = lax.all_gather(with_down, 'dp', axis=0)]
  transfers between devices with their start and end apart: 6 -> 6, of which waited for: 1 -> 2; matrix products, arithmetic and copies ran while one was open for 6% -> 7% of each run, Pallas kernels for 84% -> 79%
where the time goes in v4:
time: 629 us; the launch traced here: 620 us
  Pallas kernels  518 us (82%)
  waiting for transfers between devices  35.5 us (6%)
  other arithmetic  28 us (4%)
  local copies, waits for them, and re-layouts  21.6 us (3%)
  between operations  16.1 us (3%)
    pallas_call x1, Pallas kernels, attend_back(): pl.pallas_call(staged(attend_back_kernel, len(arrays), places), out_shape...  90.7 us
    pallas_call x1, Pallas kernels, attend(): pl.pallas_call(staged(attend_kernel, len(arrays), places), out_shape=[jax...  89.5 us
    pallas_call x1, Pallas kernels, start(): pl.pallas_call(functools.partial(start_kernel, nd), out_shape=[jax.ShapeD...  83.6 us
    pallas_call x1, Pallas kernels, gather_glu(): pl.pallas_call(gather_glu_kernel, out_shape=[jax.ShapeDtypeStruct((count,...  58.1 us
    pallas_call x1, Pallas kernels, product_scatter(): pl.pallas_call(functools.partial(scatter_kernel, turned, len(left_sides))...  51.8 us
    pallas_call x1, Pallas kernels, last(): pl.pallas_call(staged(last_kernel, len(arrays) + 1, places), out_shape=[j...  51.2 us
    pallas_call x1, Pallas kernels, glu(): pl.pallas_call(glu_kernel, grid=(count // step,), out_shape=[jax.ShapeDty...  44 us
    all_gather x1, waiting for transfers between devices, per_device_plane(): gathered_b = lax.all_gather(with_down, 'dp', axis=0)  32.7 us
  transfers between devices with their start and end apart: 6, of which 2 were waited for; matrix products, arithmetic and copies ran while one was open for 7% of the time, Pallas kernels for 79%

profile of v4, /device:TPU:0, one launch (start us, length us, event | category | flops | bytes accessed | tf_op | source)
XLA Modules:
  0.0 619.8 jit_solution(17267631763540695416)
XLA Ops:
  7.3 1.9 convert_element_type.86
  12.8 1.4 gather_fusion
  17.4 83.6 %start_1.1 = (bf16[8,256,384]{2,1,0:T(8,128)(2,1)}, bf16[256,2048]{1,0:T(8,128)(2,1)}, bf16[8,64,1024]{2,1,0:T(8,128)(2,1)}, bf16[8,64,1024]{2,1,0:T(8,128)(2,1)...) custom-call(bf16[8,64,384]{2,1,0:T(8,128)(2,1)} %pad_maximum_fusion.1.qkv_ref, ...), custom_call_target="tpu_custom_call" | custom-call | bytes 1024 | tf_op jit(solution)/shard_map/start_1/pallas_call | solution.py:1306
  103.9 1.4 gather_fusion.1
  113.6 89.5 %attend_3.1 = (f32[256,2048]{1,0:T(8,128)}, bf16[2048,2048]{1,0:T(8,128)(2,1)}, f32[2048,384]{1,0:T(8,128)}, bf16[2048,256]{1,0:T(8,128)(2,1)}, bf16[2048,128]{1...) custom-call(bf16[256,2048]{1,0:T(8,128)(2,1)} %fusion.2.refs_0_, ...), custom_call_target="tpu_custom_call" | custom-call | bytes 1024 | tf_op jit(solution)/shard_map/attend_3/pallas_call | solution.py:988
  203.1 2.1 multiply_reduce_fusion.3
  205.2 1.4 multiply_convert_fusion.1.x_ref
  206.6 58.1 %gather_glu_5.1 = (bf16[2048,2048]{1,0:T(8,128)(2,1)}, bf16[2048,512]{1,0:T(8,128)(2,1)}, bf16[2048,1024]{1,0:T(8,128)(2,1)}, bf16[512,2048]{1,0:T(8,128)(2,1)}, bf16[2048,1024]{1,0:T(8,128)(2,1)}) custom-call(bf16[256,2048]{1,0:T(8,128)(2,1)} %multiply_convert_fusion.1.x_ref, bf16[2048,1024]{1,0:T(8,128)(2,1)} %bitcast.47, ...), custom_call_target="tpu_custom_call" | custom-call | bytes 1024 | tf_op jit(solution)/shard_map/gather_glu_5/pallas_call | solution.py:1448
  264.8 32.7 %all-gather.9.cloned.1.call-done = bf16[3072,1024]{1,0:T(8,128)(2,1)} async-done(((bf16[768,1024]{1,0:T(8,128)(2,1)}), bf16[3072,1024]{1,0:T(8,128)(2,1)}) %all-gather.9.cloned.1.call-update) | async-done | bytes 6291472 | tf_op jit(solution)/shard_map/all_gather | solution.py:1898
  297.5 44.0 %glu_6.1 = (bf16[2048,512]{1,0:T(8,128)(2,1)}, bf16[2048,1024]{1,0:T(8,128)(2,1)}, bf16[4,1024,1024]{2,1,0:T(8,128)(2,1)}, bf16[2048,1024]{1,0:T(8,128)(2,1)}, bf16[512,2048]{1,0:T(8,128)(2,1)}) custom-call(bf16[2048,2048]{1,0:T(8,128)(2,1)} %get-tuple-element.86.x_ref, bf16[2048,2048]{1,0:T(8,128)(2,1)} %get-tuple-element.84.df_hbm.df_ref, ...), custom_call_target="tpu_custom_call" | custom-call | bytes 1024 | tf_op jit(solution)/shard_map/glu_6/pallas_call | solution.py:1544
  341.5 51.8 %product_scatter_8.1 = f32[256,2048]{1,0:T(8,128)} custom-call(bf16[2048,1024]{1,0:T(8,128)(2,1)} %get-tuple-element.85.refs_0_, bf16[2048,1024]{1,0:T(8,128)(2,1)} %get-tuple-element.89.refs_1_, bf16[2048,1024]{1,0:T(8,128)(2,1)} %bitcast.48, bf16[2048,1024]{1,0:T(8,128)(2,1)} %get-tuple-element.90.refs_3_), custom_call_target="tpu_custom_call" | custom-call | bytes 1024 | tf_op jit(solution)/shard_map/product_scatter_8/pallas_call | solution.py:1064
  393.4 2.3 multiply_reduce_fusion
  395.8 1.7 multiply_convert_fusion.refs_0_
  397.5 90.7 %attend_back_9.1 = (f32[256,2048]{1,0:T(8,128)}, bf16[2048,640]{1,0:T(8,128)(2,1)}, f32[8,128]{1,0:T(8,128)}) custom-call(bf16[256,2048]{1,0:T(8,128)(2,1)} %multiply_convert_fusion.refs_0_, bf16[2048,384]{1,0:T(8,128)(2,1)} %bitcast.52, bf16[256,2048]{1,0:T(8,128)(2,1)} %get-tuple-element.78.refs_2_, f32[2048,128]{1,0:T(8,128)} %copy.56.refs_3_, ...), custom_call_target="tpu_custom_call" | custom-call | bytes 1024 | tf_op jit(solution)/shard_map/attend_back_9/pallas_call | solution.py:1034
  488.3 1.4 scatter_custom_fusion
  492.1 3.6 fusion.5
  495.8 2.7 gather_fusion.2
  498.4 51.2 %last_7.1 = (bf16[256,2048]{1,0:T(8,128)(2,1)}, bf16[64,8192]{1,0:T(8,128)(2,1)}) custom-call(f32[256,2048]{1,0:T(8,128)} %copy-done.2, f32[256,1]{1,0:T(8,128)} %copy.60.refs_1_, bf16[2048,512]{1,0:T(8,128)(2,1)} %get-tuple-element.103.refs_2_, bf16[2048,512]{1,0:T(8,128)(2,1)} %get-tuple-element.104.refs_3_, ...), custom_call_target="tpu_custom_call" | custom-call | bytes 1024 | tf_op jit(solution)/shard_map/last_7/pallas_call | solution.py:1658
  551.7 2.3 gather_fusion.3
  554.0 17.7 %exchange_half_11.1 = (bf16[64,8192]{1,0:T(8,128)(2,1)}, f32[1,1024]{1,0:T(1,128)}) custom-call(bf16[1024,1024]{1,0:T(8,128)(2,1)} %bitcast.49), custom_call_target="tpu_custom_call" | custom-call | bytes 1024 | tf_op jit(solution)/shard_map/exchange_half_11/pallas_call | solution.py:206
  574.4 2.7 reduce-scatter.8.cloned.1.call-done.blocks_ref
  577.8 14.0 %sum_everywhere_13.1 = (f32[40,128]{1,0:T(8,128)}, f32[8,128]{1,0:T(8,128)}, bf16[64,3072]{1,0:T(8,128)(2,1)}, bf16[64,2048]{1,0:T(8,128)(2,1)}) custom-call(f32[40,128]{1,0:T(8,128)} %pad_bitcast_fusion.x_ref, bf16[8,64,640]{2,1,0:T(8,128)(2,1)} %reduce-scatter.8.cloned.1.call-done.blocks_ref), custom_call_target="tpu_custom_call" | custom-call | bytes 1024 | tf_op jit(solution)/shard_map/sum_everywhere_13/pallas_call | solution.py:356
  593.0 2.0 multiply_subtract_fusion
  595.0 17.7 %adam_matrices.1 = (f32[64,3072]{1,0:T(8,128)}, f32[64,2048]{1,0:T(8,128)}, f32[64,16384]{1,0:T(8,128)}, f32[256,2048]{1,0:T(8,128)}, f32[64,3072]{1,0:T(8,128)}...) custom-call(f32[8,128]{1,0:T(8,128)} %get-tuple-element.118.norm_ref, ...), custom_call_target="tpu_custom_call" | custom-call | tf_op jit(solution)/shard_map/adam_matrices/pallas_call | solution.py:1800
  (115 shorter events, 26.0 us)
Async XLA Ops:
  7.2 5.6 copy-start
  7.2 2.9 copy-start.19
  7.2 3.7 copy-start.14
  7.2 4.5 copy-start.13
  7.2 93.8 %all-gather.5.cloned.1.call-start = ((), (), s32[]{:S(2)}) async-start(), calls=%async_computation.3 | async-start | bytes 2621440 | tf_op jit(solution)/shard_map/all_gather | solution.py:1880
  10.0 2.7 copy-start.20
  10.0 196.6 %all-gather.7.cloned.1.call-start = ((), (), s32[]{:S(2)}) async-start(), calls=%async_computation.4 | async-start | bytes 5242880 | tf_op jit(solution)/shard_map/all_gather | solution.py:1892
  14.1 86.8 %copy-start.8 = (bf16[256,2048]{1,0:T(8,128)(2,1)}, bf16[256,2048]{1,0:T(8,128)(2,1)S(1)}, u32[]{:S(2)}) copy-start(bf16[256,2048]{1,0:T(8,128)(2,1)S(1)} %gather_fusion) | copy-start | bytes 3145732
  101.0 196.4 %all-gather.9.cloned.1.call-start = ((), (), s32[]{:S(2)}) async-start(), calls=%async_computation.8 | async-start | bytes 7864320 | tf_op jit(solution)/shard_map/all_gather | solution.py:1898
  102.2 1.6 copy-start.3
  103.6 294.0 %reduce-scatter.4.cloned.1.call-start = ((), (), s32[]{:S(2)}) async-start(), calls=%async_computation.5 | async-start | bytes 5242880 | tf_op jit(solution)/shard_map/reduce_scatter | solution.py:1819
  105.2 7.1 %copy-start.5 = (bf16[256,2048]{1,0:T(8,128)(2,1)}, bf16[256,2048]{1,0:T(8,128)(2,1)S(1)}, u32[]{:S(2)}) copy-start(bf16[256,2048]{1,0:T(8,128)(2,1)S(1)} %gather_fusion.1) | copy-start | bytes 3145732
  113.6 89.5 %copy-start.6 = (bf16[256,2048]{1,0:T(8,128)(2,1)S(1)}, bf16[256,2048]{1,0:T(8,128)(2,1)}, u32[]{:S(2)}) copy-start(bf16[256,2048]{1,0:T(8,128)(2,1)} %copy-done.5) | copy-start | bytes 3145732
  205.2 190.4 %copy-start.2 = (f32[256,2048]{1,0:T(8,128)}, f32[256,2048]{1,0:T(8,128)S(1)}, u32[]{:S(2)}) copy-start(f32[256,2048]{1,0:T(8,128)S(1)} %get-tuple-element.146.refs_0_) | copy-start | bytes 6291460
  264.7 287.0 %reduce-scatter.6.cloned.1.call-start = ((), (), s32[]{:S(2)}) async-start(), calls=%async_computation.6 | async-start | bytes 10485760 | tf_op jit(solution)/shard_map/reduce_scatter | solution.py:1819
  341.5 235.6 %reduce-scatter.8.cloned.1.call-start = ((), (), s32[]{:S(2)}) async-start(), calls=%async_computation.7 | async-start | bytes 3276800 | tf_op jit(solution)/shard_map/reduce_scatter | solution.py:1819
  393.3 2.3 copy-start.7
  393.3 2.5 copy-start.9
  488.3 2.3 copy-start.10
  498.4 51.3 %copy-start.12 = (bf16[8,64,1024]{2,1,0:T(8,128)(2,1)S(1)}, bf16[8,64,1024]{2,1,0:T(8,128)(2,1)}, u32[]{:S(2)}) copy-start(bf16[8,64,1024]{2,1,0:T(8,128)(2,1)} %reduce-scatter.4.cloned.1.call-done) | copy-start | bytes 3145732
  549.7 2.0 copy-start.4
  554.0 39.0 %copy-start.17 = (f32[4224]{0:T(1024)S(1)}, f32[4224]{0:T(1024)}, u32[]{:S(2)}) copy-start(f32[4224]{0:T(1024)} %param.32) | copy-start | bytes 50692
  554.0 39.0 %copy-start.18 = (f32[4224]{0:T(1024)S(1)}, f32[4224]{0:T(1024)}, u32[]{:S(2)}) copy-start(f32[4224]{0:T(1024)} %param.37) | copy-start | bytes 50692
  595.0 17.7 %copy-start.1 = (bf16[256,2048]{1,0:T(8,128)(2,1)S(1)}, bf16[256,2048]{1,0:T(8,128)(2,1)}, u32[]{:S(2)}) copy-start(bf16[256,2048]{1,0:T(8,128)(2,1)} %param.20) | copy-start | bytes 3145732
  (3 other events, 4.2 us)
Sparse Core Ops, SparseCore 0:
  10.2 65.2 all-gather.4
  101.2 80.1 all-gather.6
  183.5 113.8 all-gather.8
  299.6 74.9 reduce-scatter.3
  377.0 144.9 reduce-scatter.5
  524.2 52.8 reduce-scatter.7

commit v5 on v4

--- a/solution.py
+++ b/solution.py
@@ -1080,22 +1080,45 @@
     )(*left_sides, *right_sides)
 
 
+def gather_kernel(x_ref, all_ref, own_sem, gather_send, gather_recv):
+    gather = Gather(x_ref, all_ref, gather_send, gather_recv)
+    rows = gather.rows
+    spot = pl.ds(pl.multiple_of(gather.me * rows, rows), rows)
+    keep = pltpu.make_async_copy(x_ref, all_ref.at[spot], own_sem)
+    greet((gather.sibling, gather.x_next, gather.y_next))
+    gather.begin()
+    keep.start()
+    for slot in (0, 2, 1, 3, 5, 6, 4, 7, 9, 8, 10, 11, 12):
+        gather.take(slot)
+    gather.finish()
+    keep.wait()
+
+
+def plane_gather(rows, number):
+    return pl.pallas_call(
+        gather_kernel,
+        out_shape=jax.ShapeDtypeStruct((PLANE * rows.shape[0], rows.shape[1]), rows.dtype),
+        in_specs=[ANY],
+        out_specs=ANY,
+        scratch_shapes=[pltpu.SemaphoreType.DMA] + gather_scratch(),
+        compiler_params=pltpu.CompilerParams(collective_id=number, has_side_effects=True),
+        cost_estimate=SHORT,
+        name=f"plane_gather_{number}",
+    )(rows)
+
+
 def start_kernel(
     nd,
     qkv_ref,
     out_rows_ref,
     wide_hbm,
-    df_ref,
     note_ref,
     own_qkv_ref,
     own_out_ref,
     half_a_ref,
     half_b_ref,
-    df_all_ref,
     notes_ref,
     own_sem,
-    gather_send,
-    gather_recv,
     block_send,
     block_recv,
     note_send,
@@ -1116,7 +1139,6 @@
     whole = hidden * PLANE
     fetch = pltpu.make_async_copy(wide_hbm, wide_full, wide_sem)
     fetch.start()
-    gather = Gather(df_ref, df_all_ref, gather_send, gather_recv)
     greet_line(nd, others)
 
     def line_spot(array, owner):
@@ -1204,7 +1226,6 @@
         ]
 
     own_block = own_qkv_ref.at[me, pl.ds(pl.multiple_of(line * count, count), count)]
-    rows = df_ref.shape[0]
 
     def local(index, source, target):
         return pltpu.make_async_copy(source, target, own_sem.at[index])
@@ -1213,10 +1234,9 @@
         local(0, qkv_ref.at[me], own_block),
         local(1, out_rows_ref, line_spot(1, line)),
         local(2, note_ref, notes_ref.at[me]),
-        local(3, df_ref, df_all_ref.at[pl.ds(pl.multiple_of(me * rows, rows), rows)]),
     ]
     keep_pieces = [
-        local(4 + index, source, target) for index, (source, target) in enumerate(pieces(me))
+        local(3 + index, source, target) for index, (source, target) in enumerate(pieces(me))
     ]
     order = (6, 7, 2, 4, 3, 5, 1)
     for number in order:
@@ -1224,7 +1244,6 @@
         put_note(number).start()
     keep[0].start()
     send_own(1, out_rows_ref)
-    gather.begin()
     for copy in keep[1:]:
         copy.start()
     for number in order:
@@ -1246,26 +1265,12 @@
                 target = pl.ds(pl.multiple_of(target, 128), part_width)
                 wide_ref[:, target] = wide_full[:, columns].astype(wide_ref.dtype)
 
-    for steps, slots in (
-        ((), (0, 2)),
-        (((1, 1),), (4, 1, 3)),
-        (((0, 1), (2, 1)), (5, 6)),
-        (((1, 2),), ()),
-        (((0, 2), (2, 2)), (7, 9, 8, 10)),
-        (((1, 3), (0, 3), (2, 3)), (11, 12)),
-    ):
-        for array, step in steps:
-            if step < nd:
-                line_step(array, step)
-        for slot in slots:
-            gather.take(slot)
-        if slots == (5, 6):
-            for number in order:
-                for copy in put_pieces(number):
-                    copy.start()
-            for copy in keep_pieces:
-                copy.start()
-    for step in range(4, nd):
+    for number in order:
+        for copy in put_pieces(number):
+            copy.start()
+    for copy in keep_pieces:
+        copy.start()
+    for step in range(1, nd):
         for array in (1, 0, 2):
             line_step(array, step)
     for number in order:
@@ -1273,7 +1278,6 @@
         put_note(number).wait()
         for copy in put_pieces(number):
             copy.wait()
-    gather.finish()
     for copy in keep[1:] + keep_pieces:
         copy.wait()
     for array in (1, 0, 2):
@@ -1298,7 +1302,7 @@
                 along(array, line + step, 1).wait_send()
 
 
-def start(qkv_blocks, out_rows, wide_rows, df_own, note, number):
+def start(qkv_blocks, out_rows, wide_rows, note, number):
     nd = lax.axis_size("dp")
     count, whole = wide_rows.shape
     half = whole // 4 // PLANE
@@ -1310,13 +1314,11 @@
             jax.ShapeDtypeStruct((nd * count, out_rows.shape[1]), low),
             jax.ShapeDtypeStruct((PLANE, count, 2 * half), low),
             jax.ShapeDtypeStruct((PLANE, count, 2 * half), low),
-            jax.ShapeDtypeStruct((PLANE * df_own.shape[0], df_own.shape[1]), low),
             jax.ShapeDtypeStruct((PLANE,) + note.shape, note.dtype),
         ],
-        in_specs=[ANY] * 5,
-        out_specs=[ANY] * 6,
-        scratch_shapes=[pltpu.SemaphoreType.DMA((8,))]
-        + gather_scratch()
+        in_specs=[ANY] * 4,
+        out_specs=[ANY] * 5,
+        scratch_shapes=[pltpu.SemaphoreType.DMA((7,))]
         + [pltpu.SemaphoreType.DMA((PLANE,))] * 4
         + [pltpu.SemaphoreType.DMA((4 * PLANE,))] * 2
         + [pltpu.SemaphoreType.DMA((3, 2, nd)), pltpu.SemaphoreType.DMA((3, nd))]
@@ -1330,7 +1332,7 @@
         ),
         cost_estimate=SHORT,
         name=f"start_{number}",
-    )(qkv_blocks, out_rows, wide_rows, df_own, note)
+    )(qkv_blocks, out_rows, wide_rows, note)
 
 
 def glu_block(
@@ -1878,11 +1880,10 @@
     down_low = w_down.astype(low)
     units = down_low.shape[0] // 2
     down_a = lax.all_gather(down_low[:units], "dp", axis=0, tiled=True)
-    own_qkv, own_out, half_a, half_b, down_back, notes = start(
+    own_qkv, own_out, half_a, half_b, notes = start(
         qkv_blocks,
         w_out.astype(low),
         w_gate_up,
-        (valid_col * back_rows).astype(low),
         jnp.pad(lengths, ((0, 8 - MB), (0, 128 - SEQS))),
         1,
     )
@@ -1901,6 +1902,9 @@
     attention_sums, attention_back = attention(
         normed_one.astype(low), own_qkv, own_out, lengths_all, query_gain, key_gain
     )
+    back_low = (valid_col * back_rows).astype(low)
+    back_low, attention_sums = lax.optimization_barrier((back_low, attention_sums))
+    down_back = plane_gather(back_low, 4)
     hidden = rows_in + valid_col * attention_sums
 
     normed_two, norm_two_pull = jax.vjp(rms_norm, hidden, ffn_gain)

time: 629 us -> 633 us (level)
  Pallas kernels: 518 us -> 558 us
  waiting for transfers between devices: 35.5 us -> 2.27 us
    pallas_call x0 -> x1, Pallas kernels: none -> 40.3 us  [plane_gather(): pl.pallas_call(gather_kernel, out_shape=jax.ShapeDtypeStruct((PLANE * row...]
    all_gather x1, waiting for transfers between devices: 32.7 us -> 0.02 us  [per_device_plane(): gathered_b = lax.all_gather(with_down, 'dp', axis=0)]
  transfers between devices with their start and end apart: 6 -> 6, of which waited for: 2 -> 1; matrix products, arithmetic and copies ran while one was open for 7% -> 6% of each run, Pallas kernels for 79% -> 84%
where the time goes in v5:
time: 633 us; the launch traced here: 624 us
  Pallas kernels  558 us (88%)
  other arithmetic  28.1 us (4%)
  local copies, waits for them, and re-layouts  19.9 us (3%)
  between operations  16.1 us (3%)
    pallas_call x1, Pallas kernels, attend_back(): pl.pallas_call(staged(attend_back_kernel, len(arrays), places), out_shape...  90.9 us
    pallas_call x1, Pallas kernels, attend(): pl.pallas_call(staged(attend_kernel, len(arrays), places), out_shape=[jax...  88.5 us
    pallas_call x1, Pallas kernels, start(): pl.pallas_call(functools.partial(start_kernel, nd), out_shape=[jax.ShapeD...  84.1 us
    pallas_call x1, Pallas kernels, gather_glu(): pl.pallas_call(gather_glu_kernel, out_shape=[jax.ShapeDtypeStruct((count,...  58.3 us
    pallas_call x1, Pallas kernels, last(): pl.pallas_call(staged(last_kernel, len(arrays) + 1, places), out_shape=[j...  51.2 us
    pallas_call x1, Pallas kernels, product_scatter(): pl.pallas_call(functools.partial(scatter_kernel, turned, len(left_sides))...  50.4 us
    pallas_call x1, Pallas kernels, glu(): pl.pallas_call(glu_kernel, grid=(count // step,), out_shape=[jax.ShapeDty...  44.7 us
    pallas_call x1, Pallas kernels, plane_gather(): pl.pallas_call(gather_kernel, out_shape=jax.ShapeDtypeStruct((PLANE * row...  40.3 us
  transfers between devices with their start and end apart: 6, of which 1 were waited for; matrix products, arithmetic and copies ran while one was open for 6% of the time, Pallas kernels for 84%

profile of v5, /device:TPU:0, one launch (start us, length us, event | category | flops | bytes accessed | tf_op | source)
XLA Modules:
  0.0 624.4 jit_solution(124180281365689477)
XLA Ops:
  7.3 1.9 convert_element_type.86
  12.7 84.1 %start_1.1 = (bf16[8,256,384]{2,1,0:T(8,128)(2,1)}, bf16[256,2048]{1,0:T(8,128)(2,1)}, bf16[8,64,1024]{2,1,0:T(8,128)(2,1)}, bf16[8,64,1024]{2,1,0:T(8,128)(2,1)}, s32[8,8,128]{2,1,0:T(8,128)}) custom-call(bf16[8,64,384]{2,1,0:T(8,128)(2,1)} %pad_maximum_fusion.1.qkv_ref, bf16[64,2048]{1,0:T(8,128)(2,1)} %convert_element_type.80.out_rows_ref, ...), custom_call_target="tpu_custom_call" | custom-call | bytes 1024 | tf_op jit(solution)/shard_map/start_1/pallas_call | solution.py:1310
  100.0 1.4 gather_fusion.1
  101.4 1.4 gather_fusion
  111.1 88.5 %attend_3.1 = (f32[256,2048]{1,0:T(8,128)}, bf16[2048,2048]{1,0:T(8,128)(2,1)}, f32[2048,384]{1,0:T(8,128)}, bf16[2048,256]{1,0:T(8,128)(2,1)}, bf16[2048,128]{1...) custom-call(bf16[256,2048]{1,0:T(8,128)(2,1)} %fusion.2.refs_0_, ...), custom_call_target="tpu_custom_call" | custom-call | bytes 1024 | tf_op jit(solution)/shard_map/attend_3/pallas_call | solution.py:988
  201.0 40.3 %plane_gather_4.1.df_hbm.df_ref = bf16[2048,2048]{1,0:T(8,128)(2,1)} custom-call(bf16[256,2048]{1,0:T(8,128)(2,1)} %fusion.4.x_ref), custom_call_target="tpu_custom_call" | custom-call | bytes 1024 | tf_op jit(solution)/shard_map/plane_gather_4/pallas_call | solution.py:1098
  241.3 2.1 multiply_reduce_fusion.3
  243.4 1.4 multiply_convert_fusion.1.x_ref
  244.8 58.3 %gather_glu_5.1 = (bf16[2048,2048]{1,0:T(8,128)(2,1)}, bf16[2048,512]{1,0:T(8,128)(2,1)}, bf16[2048,1024]{1,0:T(8,128)(2,1)}, bf16[512,2048]{1,0:T(8,128)(2,1)}, bf16[2048,1024]{1,0:T(8,128)(2,1)}) custom-call(bf16[256,2048]{1,0:T(8,128)(2,1)} %multiply_convert_fusion.1.x_ref, bf16[2048,1024]{1,0:T(8,128)(2,1)} %bitcast.47, ...), custom_call_target="tpu_custom_call" | custom-call | bytes 1024 | tf_op jit(solution)/shard_map/gather_glu_5/pallas_call | solution.py:1450
  303.2 44.7 %glu_6.1 = (bf16[2048,512]{1,0:T(8,128)(2,1)}, bf16[2048,1024]{1,0:T(8,128)(2,1)}, bf16[4,1024,1024]{2,1,0:T(8,128)(2,1)}, bf16[2048,1024]{1,0:T(8,128)(2,1)}, bf16[512,2048]{1,0:T(8,128)(2,1)}) custom-call(bf16[2048,2048]{1,0:T(8,128)(2,1)} %get-tuple-element.88.x_ref, bf16[2048,2048]{1,0:T(8,128)(2,1)} %plane_gather_4.1.df_hbm.df_ref, ...), custom_call_target="tpu_custom_call" | custom-call | bytes 1024 | tf_op jit(solution)/shard_map/glu_6/pallas_call | solution.py:1546
  348.0 50.4 %product_scatter_8.1 = f32[256,2048]{1,0:T(8,128)} custom-call(bf16[2048,1024]{1,0:T(8,128)(2,1)} %get-tuple-element.87.refs_0_, bf16[2048,1024]{1,0:T(8,128)(2,1)} %get-tuple-element.91.refs_1_, bf16[2048,1024]{1,0:T(8,128)(2,1)} %bitcast.48, bf16[2048,1024]{1,0:T(8,128)(2,1)} %get-tuple-element.92.refs_3_), custom_call_target="tpu_custom_call" | custom-call | bytes 1024 | tf_op jit(solution)/shard_map/product_scatter_8/pallas_call | solution.py:1064
  398.4 2.3 multiply_reduce_fusion
  400.8 1.7 multiply_convert_fusion.refs_0_
  402.5 90.9 %attend_back_9.1 = (f32[256,2048]{1,0:T(8,128)}, bf16[2048,640]{1,0:T(8,128)(2,1)}, f32[8,128]{1,0:T(8,128)}) custom-call(bf16[256,2048]{1,0:T(8,128)(2,1)} %multiply_convert_fusion.refs_0_, bf16[2048,384]{1,0:T(8,128)(2,1)} %bitcast.52, bf16[256,2048]{1,0:T(8,128)(2,1)} %get-tuple-element.79.refs_2_, f32[2048,128]{1,0:T(8,128)} %copy.56.refs_3_, ...), custom_call_target="tpu_custom_call" | custom-call | bytes 1024 | tf_op jit(solution)/shard_map/attend_back_9/pallas_call | solution.py:1034
  493.5 1.4 scatter_custom_fusion
  497.3 3.6 fusion.5
  501.0 2.7 gather_fusion.2
  503.7 51.2 %last_7.1 = (bf16[256,2048]{1,0:T(8,128)(2,1)}, bf16[64,8192]{1,0:T(8,128)(2,1)}) custom-call(f32[256,2048]{1,0:T(8,128)} %copy-done.2, f32[256,1]{1,0:T(8,128)} %copy.60.refs_1_, bf16[2048,512]{1,0:T(8,128)(2,1)} %get-tuple-element.105.refs_2_, bf16[2048,512]{1,0:T(8,128)(2,1)} %get-tuple-element.106.refs_3_, ...), custom_call_target="tpu_custom_call" | custom-call | bytes 1024 | tf_op jit(solution)/shard_map/last_7/pallas_call | solution.py:1660
  556.9 2.3 gather_fusion.3
  559.2 17.7 %exchange_half_11.1 = (bf16[64,8192]{1,0:T(8,128)(2,1)}, f32[1,1024]{1,0:T(1,128)}) custom-call(bf16[1024,1024]{1,0:T(8,128)(2,1)} %bitcast.49), custom_call_target="tpu_custom_call" | custom-call | bytes 1024 | tf_op jit(solution)/shard_map/exchange_half_11/pallas_call | solution.py:206
  579.6 2.1 reduce-scatter.8.cloned.1.call-done.blocks_ref
  582.4 14.0 %sum_everywhere_13.1 = (f32[40,128]{1,0:T(8,128)}, f32[8,128]{1,0:T(8,128)}, bf16[64,3072]{1,0:T(8,128)(2,1)}, bf16[64,2048]{1,0:T(8,128)(2,1)}) custom-call(f32[40,128]{1,0:T(8,128)} %pad_bitcast_fusion.x_ref, bf16[8,64,640]{2,1,0:T(8,128)(2,1)} %reduce-scatter.8.cloned.1.call-done.blocks_ref), custom_call_target="tpu_custom_call" | custom-call | bytes 1024 | tf_op jit(solution)/shard_map/sum_everywhere_13/pallas_call | solution.py:356
  597.6 2.0 multiply_subtract_fusion
  599.6 17.7 %adam_matrices.1 = (f32[64,3072]{1,0:T(8,128)}, f32[64,2048]{1,0:T(8,128)}, f32[64,16384]{1,0:T(8,128)}, f32[256,2048]{1,0:T(8,128)}, f32[64,3072]{1,0:T(8,128)}...) custom-call(f32[8,128]{1,0:T(8,128)} %get-tuple-element.120.norm_ref, ...), custom_call_target="tpu_custom_call" | custom-call | tf_op jit(solution)/shard_map/adam_matrices/pallas_call | solution.py:1802
  (116 shorter events, 24.3 us)
Async XLA Ops:
  7.2 92.8 %copy-start = (bf16[256,2048]{1,0:T(8,128)(2,1)S(1)}, bf16[256,2048]{1,0:T(8,128)(2,1)}, u32[]{:S(2)}) copy-start(bf16[256,2048]{1,0:T(8,128)(2,1)} %param.19) | copy-start | bytes 3145732
  7.2 2.9 copy-start.14
  7.2 3.6 copy-start.13
  7.2 89.6 %all-gather.5.cloned.1.call-start = ((), (), s32[]{:S(2)}) async-start(), calls=%async_computation.3 | async-start | bytes 2621440 | tf_op jit(solution)/shard_map/all_gather | solution.py:1882
  10.0 234.8 %all-gather.7.cloned.1.call-start = ((), (), s32[]{:S(2)}) async-start(), calls=%async_computation.4 | async-start | bytes 5242880 | tf_op jit(solution)/shard_map/all_gather | solution.py:1893
  96.9 206.4 %all-gather.9.cloned.1.call-start = ((), (), s32[]{:S(2)}) async-start(), calls=%async_computation.8 | async-start | bytes 7864320 | tf_op jit(solution)/shard_map/all_gather | solution.py:1899
  98.0 1.7 copy-start.16
  98.0 1.9 copy-start.20
  99.4 303.2 %reduce-scatter.4.cloned.1.call-start = ((), (), s32[]{:S(2)}) async-start(), calls=%async_computation.5 | async-start | bytes 5242880 | tf_op jit(solution)/shard_map/reduce_scatter | solution.py:1821
  101.3 8.5 %copy-start.5 = (bf16[256,2048]{1,0:T(8,128)(2,1)}, bf16[256,2048]{1,0:T(8,128)(2,1)S(1)}, u32[]{:S(2)}) copy-start(bf16[256,2048]{1,0:T(8,128)(2,1)S(1)} %gather_fusion.1) | copy-start | bytes 3145732
  102.7 97.0 %copy-start.8 = (bf16[256,2048]{1,0:T(8,128)(2,1)}, bf16[256,2048]{1,0:T(8,128)(2,1)S(1)}, u32[]{:S(2)}) copy-start(bf16[256,2048]{1,0:T(8,128)(2,1)S(1)} %gather_fusion) | copy-start | bytes 3145732
  201.0 40.3 %copy-start.6 = (bf16[256,2048]{1,0:T(8,128)(2,1)S(1)}, bf16[256,2048]{1,0:T(8,128)(2,1)}, u32[]{:S(2)}) copy-start(bf16[256,2048]{1,0:T(8,128)(2,1)} %copy-done.5) | copy-start | bytes 3145732
  243.3 157.3 %copy-start.2 = (f32[256,2048]{1,0:T(8,128)}, f32[256,2048]{1,0:T(8,128)S(1)}, u32[]{:S(2)}) copy-start(f32[256,2048]{1,0:T(8,128)S(1)} %get-tuple-element.148.refs_0_) | copy-start | bytes 6291460
  303.2 253.8 %reduce-scatter.6.cloned.1.call-start = ((), (), s32[]{:S(2)}) async-start(), calls=%async_computation.6 | async-start | bytes 10485760 | tf_op jit(solution)/shard_map/reduce_scatter | solution.py:1821
  347.9 233.7 %reduce-scatter.8.cloned.1.call-start = ((), (), s32[]{:S(2)}) async-start(), calls=%async_computation.7 | async-start | bytes 3276800 | tf_op jit(solution)/shard_map/reduce_scatter | solution.py:1821
  398.4 2.3 copy-start.7
  398.4 2.5 copy-start.9
  493.4 2.3 copy-start.10
  495.7 1.7 copy-start.11
  503.7 51.2 %copy-start.12 = (bf16[8,64,1024]{2,1,0:T(8,128)(2,1)S(1)}, bf16[8,64,1024]{2,1,0:T(8,128)(2,1)}, u32[]{:S(2)}) copy-start(bf16[8,64,1024]{2,1,0:T(8,128)(2,1)} %reduce-scatter.4.cloned.1.call-done) | copy-start | bytes 3145732
  554.9 2.0 copy-start.4
  559.2 38.4 %copy-start.17 = (f32[4224]{0:T(1024)S(1)}, f32[4224]{0:T(1024)}, u32[]{:S(2)}) copy-start(f32[4224]{0:T(1024)} %param.32) | copy-start | bytes 50692
  559.2 38.4 %copy-start.18 = (f32[4224]{0:T(1024)S(1)}, f32[4224]{0:T(1024)}, u32[]{:S(2)}) copy-start(f32[4224]{0:T(1024)} %param.37) | copy-start | bytes 50692
  599.6 17.7 %copy-start.1 = (bf16[256,2048]{1,0:T(8,128)(2,1)S(1)}, bf16[256,2048]{1,0:T(8,128)(2,1)}, u32[]{:S(2)}) copy-start(bf16[256,2048]{1,0:T(8,128)(2,1)} %param.19) | copy-start | bytes 3145732
  (3 other events, 3.8 us)
Sparse Core Ops, SparseCore 0:
  10.2 65.3 all-gather.4
  97.0 79.3 all-gather.6
  178.5 113.8 all-gather.8
  303.3 75.9 reduce-scatter.3
  381.6 144.9 reduce-scatter.5
  528.8 52.8 reduce-scatter.7
